TPU v7x, 128 devices: a whole 4x4x4 slice. The times are simulated.
128 devices in a mesh: psg: 32 (over z, y_hi, x), cen: 4 (over y_lo, core).
Axes of the slice: x: 4, y: 4 (y_hi: 2, y_lo: 2; y = y_hi * 2 + y_lo), z: 4, core: 2. Of those that a mesh axis runs over, the one named last changes fastest.
Arguments:
- passages: bfloat16 [1024, 4096], P('psg'), may hold values from -8 to 8
- centroids: bfloat16 [65536, 4096], P(('psg', 'cen')), may hold values from -4 to 4
- dual_init: float32 [65536], P(('psg', 'cen')), may hold values from -8 to 8
Outputs:
- new_centroids: bfloat16 [65536, 4096], P(('psg', 'cen'))
- passage_duals: float32 [1024], P('psg')
- centroid_duals: float32 [65536], P(('psg', 'cen'))
All inputs are finite; a program needn't handle non-finite values.
Results may differ from a plain program's by a relative error of at most 0.0047.
Values may be sent and summed in bfloat16 or wider, within the bound.
No kernel may reach another device: no remote copies, remote signals or barrier semaphores. Data moves between devices by JAX's collectives and lax.ppermute only.
A program may use at most 64 MiB of HBM per device.

v0:
```python
import math

import jax
import jax.numpy as jnp
from jax import lax
from jax.sharding import PartitionSpec as P

CENTROIDS = 65536
ITERS = 3


def tile_logits(rows_block, centroids, factor):
    product = lax.dot_general(
        rows_block, centroids, (((1,), (1,)), ((), ())), preferred_element_type=jnp.float32
    )
    return product * factor


def row_logsum(shifted):
    top = lax.pmax(jnp.max(shifted, axis=1), ("psg", "cen"))
    total = lax.psum(jnp.sum(jnp.exp(shifted - top[:, None]), axis=1), ("psg", "cen"))
    return top + jnp.log(total)


def body(passages, centroids, dual_init):
    factor = 4.0 / math.sqrt(passages.shape[1])
    local_rows = passages.shape[0]
    gathered = lax.all_gather(passages, "psg", axis=0, tiled=True)
    count_rows = local_rows * lax.axis_size("psg")

    def logits_now():
        return tile_logits(gathered, centroids, factor)

    centroid_duals = dual_init
    passage_duals = jnp.zeros((count_rows,), jnp.float32)
    for number in range(ITERS):
        logits = logits_now()
        passage_duals = -math.log(count_rows) - row_logsum(logits + centroid_duals[None, :])
        column_terms = logits + passage_duals[:, None]
        column_top = jnp.max(column_terms, axis=0)
        column_sum = jnp.sum(jnp.exp(column_terms - column_top[None, :]), axis=0)
        centroid_duals = -math.log(CENTROIDS) - (column_top + jnp.log(column_sum))
    logits = logits_now()
    weight = (
        CENTROIDS * jnp.exp(logits + passage_duals[:, None] + centroid_duals[None, :])
    ).astype(jnp.bfloat16)
    summed = lax.dot_general(
        weight, gathered, (((0,), (0,)), ((), ())), preferred_element_type=jnp.float32
    )
    new_centroids = summed.astype(jnp.bfloat16)
    own_duals = lax.dynamic_slice_in_dim(
        passage_duals, lax.axis_index("psg") * local_rows, local_rows
    )
    return (new_centroids, own_duals, centroid_duals)


def solution(mesh):
    in_specs = (P("psg", None), P(("psg", "cen"), None), P(("psg", "cen")))
    out_specs = (P(("psg", "cen"), None), P("psg"), P(("psg", "cen")))
    return jax.shard_map(body, mesh=mesh, in_specs=in_specs, out_specs=out_specs, check_vma=False)
```

profile of v0, /device:TPU:1, one launch (start us, length us, event | category | flops | bytes accessed | tf_op | source)
XLA Modules:
  0.0 528.3 jit_solution(2918943290544177959)
XLA Ops:
  7.2 0.0 all-gather.2.cloned.1.call-start
  7.2 0.7 all-gather.2.cloned.1.call-update
  7.9 110.2 %all-gather.2.cloned.1.call-done = bf16[1024,4096]{1,0:T(8,128)(2,1)} async-done(((bf16[32,4096]{1,0:T(8,128)(2,1)}), bf16[1024,4096]{1,0:T(8,128)(2,1)}) %all-gather.2.cloned.1.call-update) | async-done | bytes 8388624 | tf_op jit(solution)/shard_map/all_gather | solution.py:28
  118.1 8.4 %add_reduce_fusion.4 = (f32[1024]{0:T(1024)S(1)}, f32[1024,512]{1,0:T(8,128)S(1)}) fusion(f32[512]{0:T(512)} %param.5, bf16[1024,4096]{1,0:T(8,128)(2,1)} %all-gather.2.cloned.1.call-done, bf16[512,4096]{1,0:T(8,128)(2,1)} %param.4), kind=kOutput, calls=%fused_computation.12 | convolution fusion | flops 4296539136 | bytes 14686208 | tf_op jit(solution)/shard_map/dot_general | solution.py:13
  126.5 64.5 %pmax.21 = f32[1024]{0:T(1024)S(1)} all-reduce(f32[1024]{0:T(1024)S(1)} %get-tuple-element.3), channel_id=1, replica_groups=mesh['psg'=32,'cen'=4] {'psg','cen'}, use_global_device_ids=true, to_apply=%region_1.0 | all-reduce | flops 1024 | bytes 8192 | tf_op jit(solution)/shard_map/pmax | solution.py:20
  191.0 0.6 exponential_reduce_fusion.5
  191.6 62.6 %psum.21 = f32[1024]{0:T(1024)S(1)} all-reduce(f32[1024]{0:T(1024)S(1)} %exponential_reduce_fusion.5), channel_id=1, replica_groups=mesh['psg'=32,'cen'=4] {'psg','cen'}, use_global_device_ids=true, to_apply=%region_3.0 | all-reduce | flops 1024 | bytes 8192 | tf_op jit(solution)/shard_map/psum | solution.py:21
  254.1 0.2 add_reduce_fusion.3
  254.4 0.4 exponential_reduce_fusion.4
  254.8 0.2 add_reduce_fusion.2
  255.0 64.0 %pmax.22 = f32[1024]{0:T(1024)S(1)} all-reduce(f32[1024]{0:T(1024)S(1)} %add_reduce_fusion.2), channel_id=1, replica_groups=mesh['psg'=32,'cen'=4] {'psg','cen'}, use_global_device_ids=true, to_apply=%region_7.0 | all-reduce | flops 1024 | bytes 8192 | tf_op jit(solution)/shard_map/pmax | solution.py:20
  319.1 0.6 exponential_reduce_fusion.3
  319.6 62.5 %psum.22 = f32[1024]{0:T(1024)S(1)} all-reduce(f32[1024]{0:T(1024)S(1)} %exponential_reduce_fusion.3), channel_id=1, replica_groups=mesh['psg'=32,'cen'=4] {'psg','cen'}, use_global_device_ids=true, to_apply=%region_9.0 | all-reduce | flops 1024 | bytes 8192 | tf_op jit(solution)/shard_map/psum | solution.py:21
  382.2 0.2 add_reduce_fusion.1
  382.4 0.4 exponential_reduce_fusion.2
  382.9 0.2 add_reduce_fusion
  383.1 64.1 %pmax.23 = f32[1024]{0:T(1024)S(1)} all-reduce(f32[1024]{0:T(1024)S(1)} %add_reduce_fusion), channel_id=1, replica_groups=mesh['psg'=32,'cen'=4] {'psg','cen'}, use_global_device_ids=true, to_apply=%region_13.0 | all-reduce | flops 1024 | bytes 8192 | tf_op jit(solution)/shard_map/pmax | solution.py:20
  447.1 0.6 exponential_reduce_fusion.1
  447.7 62.7 %psum.23 = f32[1024]{0:T(1024)S(1)} all-reduce(f32[1024]{0:T(1024)S(1)} %exponential_reduce_fusion.1), channel_id=1, replica_groups=mesh['psg'=32,'cen'=4] {'psg','cen'}, use_global_device_ids=true, to_apply=%region_15.0 | all-reduce | flops 1024 | bytes 8192 | tf_op jit(solution)/shard_map/psum | solution.py:21
  510.4 0.2 add_reduce_fusion.5
  510.7 0.4 exponential_reduce_fusion
  511.1 0.0 copy-start.1
  511.1 0.6 dynamic_slice.3
  511.7 9.7 %convolution_convert_fusion = bf16[512,4096]{1,0:T(8,128)(2,1)} fusion(bf16[1024,4096]{1,0:T(8,128)(2,1)} %all-gather.2.cloned.1.call-done, f32[1024,512]{1,0:T(8,128)S(1)} %get-tuple-element.4, f32[512]{0:T(512)S(1)} %add_subtract_fusion.3, f32[1024]{0:T(1024)S(1)} %add_subtract_fusion), kind=kOutput, calls=%fused_computation | convolution fusion | flops 4299161600 | bytes 14686208 | tf_op jit(solution)/shard_map/dot_general | solution.py:47
  (9 shorter events, 0.0 us)
Async XLA Ops:
  7.2 111.0 %all-gather.2.cloned.1.call-start = ((), (), s32[]{:S(2)}) async-start(), calls=%async_computation | async-start | bytes 8650752 | tf_op jit(solution)/shard_map/all_gather | solution.py:28
  7.9 183.1 %copy-start = (f32[512]{0:T(512)S(1)}, f32[512]{0:T(512)}, u32[]{:S(2)}) copy-start(f32[512]{0:T(512)} %param.5) | copy-start | bytes 6148
  511.1 10.4 %copy-start.1 = (f32[512]{0:T(512)}, f32[512]{0:T(512)S(1)}, u32[]{:S(2)}) copy-start(f32[512]{0:T(512)S(1)} %add_subtract_fusion.3) | copy-start | bytes 6148
Sparse Core Ops, SparseCore 0:
  11.0 107.0 all-gather.1
where the time goes:
time: 529 us; the launch traced here: 528 us
  blocking collectives  380 us (72%)
  waiting for transfers between devices  111 us (21%)
  matrix products  18.1 us (3%)
  between operations  14.1 us (3%)
    pmax x3, blocking collectives, row_logsum(): top = lax.pmax(jnp.max(shifted, axis=1), ('psg', 'cen'))  193 us
    psum x3, blocking collectives, row_logsum(): lax.psum(jnp.sum(jnp.exp(shifted - top[:, None]), axis=1), ('psg', 'cen'))  188 us
    all_gather x1, waiting for transfers between devices, body(): gathered = lax.all_gather(passages, 'psg', axis=0, tiled=True)  110 us
  transfers between devices with their start and end apart: 1, of which 1 were waited for; matrix products, arithmetic and copies ran while one was open for 0% of the time, Pallas kernels for 0%

commit v1 on v0

v1 whole, which is shorter than its diff:
```python
import math

import jax
import jax.numpy as jnp
from jax import lax
from jax.sharding import PartitionSpec as P

CENTROIDS = 65536
PASSAGES = 1024
EVERY = ("psg", "cen")


def to_every(values):
    count = lax.axis_size(EVERY)
    return lax.all_to_all(jnp.broadcast_to(values[None], (count, *values.shape)), EVERY, 0, 0)


def total_over_devices(partial):
    return jnp.sum(to_every(partial.astype(jnp.bfloat16)).astype(jnp.float32), axis=0)


def body(passages, centroids, dual_init):
    factor = 4.0 / math.sqrt(passages.shape[1])
    local_rows = passages.shape[0]
    gathered = lax.all_gather(passages, "psg", axis=0, tiled=True)
    logits = factor * lax.dot_general(
        centroids, gathered, (((1,), (1,)), ((), ())), preferred_element_type=jnp.float32
    )

    shifted = logits + dual_init[:, None]
    top = jnp.max(shifted, axis=0)
    own = top + jnp.log(jnp.sum(jnp.exp(shifted - top[None, :]), axis=0))
    parts = to_every(own)
    top = jnp.max(parts, axis=0)
    passage_first = -math.log(PASSAGES) - (
        top + jnp.log(jnp.sum(jnp.exp(parts - top[None, :]), axis=0))
    )
    terms = logits + passage_first[None, :]
    top = jnp.max(terms, axis=1)
    total = jnp.sum(jnp.exp(terms - top[:, None]), axis=1)
    centroid_first = -math.log(CENTROIDS) - (top + jnp.log(total))

    kernel = jnp.exp(terms - top[:, None]) / total[:, None]
    ratio = CENTROIDS / PASSAGES
    row_scale = ratio / total_over_devices(jnp.sum(kernel, axis=0))
    col_scale = 1.0 / jnp.sum(kernel * row_scale[None, :], axis=1)
    row_scale = ratio / total_over_devices(jnp.sum(kernel * col_scale[:, None], axis=0))
    col_sum = jnp.sum(kernel * row_scale[None, :], axis=1)

    weight = (kernel * row_scale[None, :] / col_sum[:, None]).astype(jnp.bfloat16)
    new_centroids = lax.dot_general(
        weight, gathered, (((1,), (0,)), ((), ())), preferred_element_type=jnp.float32
    ).astype(jnp.bfloat16)
    passage_duals = passage_first + jnp.log(row_scale)
    own_duals = lax.dynamic_slice_in_dim(
        passage_duals, lax.axis_index("psg") * local_rows, local_rows
    )
    return (new_centroids, own_duals, centroid_first - jnp.log(col_sum))


def solution(mesh):
    in_specs = (P("psg", None), P(("psg", "cen"), None), P(("psg", "cen")))
    out_specs = (P(("psg", "cen"), None), P("psg"), P(("psg", "cen")))
    return jax.shard_map(body, mesh=mesh, in_specs=in_specs, out_specs=out_specs, check_vma=False)
```

time: 529 us -> 207 us (0.39)
  blocking collectives: 380 us -> 35.2 us
  waiting for transfers between devices: 111 us -> 122 us
  other arithmetic: 4.14 us -> 9.72 us
    pmax x3 -> x0, blocking collectives: 193 us -> none  [row_logsum(): top = lax.pmax(jnp.max(shifted, axis=1), ('psg', 'cen'))]
    psum x3 -> x0, blocking collectives: 188 us -> none  [row_logsum(): lax.psum(jnp.sum(jnp.exp(shifted - top[:, None]), axis=1), ('psg', 'cen'))]
    all_to_all x0 -> x2, blocking collectives: none -> 35.2 us  [to_every(): lax.all_to_all(jnp.broadcast_to(values[None], (count, *values.shape)), EV...]
    all_to_all x0 -> x1, waiting for transfers between devices: none -> 11.4 us  [to_every(): lax.all_to_all(jnp.broadcast_to(values[None], (count, *values.shape)), EV...]
  transfers between devices with their start and end apart: 1 -> 2, of which waited for: 1 -> 2; matrix products, arithmetic and copies ran while one was open for 0% -> 0% of each run, Pallas kernels for 0% -> 0%
where the time goes in v1:
time: 207 us
  waiting for transfers between devices  122 us (59%)
  blocking collectives  35.2 us (17%)
  matrix products  17.8 us (9%)
  between operations  14.2 us (7%)
  other arithmetic  9.72 us (5%)
  starting transfers between devices  3.96 us (2%)
  local copies, waits for them, and re-layouts  3.42 us (2%)
    all_gather x1, waiting for transfers between devices, body(): gathered = lax.all_gather(passages, 'psg', axis=0, tiled=True)  110 us
    all_to_all x2, blocking collectives, to_every(): lax.all_to_all(jnp.broadcast_to(values[None], (count, *values.shape)), EV...  35.2 us
    all_to_all x1, waiting for transfers between devices, to_every(): lax.all_to_all(jnp.broadcast_to(values[None], (count, *values.shape)), EV...  11.4 us
    dot_general x1, matrix products, body(): lax.dot_general(weight, gathered, (((1,), (0,)), ((), ())), preferred_ele...  9.57 us
    dot_general x1, matrix products, body(): lax.dot_general(centroids, gathered, (((1,), (1,)), ((), ())), preferred_...  8.25 us
    broadcast_in_dim x2, other arithmetic, to_every(): jnp.broadcast_to(values[None], (count, *values.shape))  4.53 us
  transfers between devices with their start and end apart: 2, of which 2 were waited for; matrix products, arithmetic and copies ran while one was open for 0% of the time, Pallas kernels for 0%

profile of v1, /device:TPU:1, one launch (start us, length us, event | category | flops | bytes accessed | tf_op | source)
XLA Modules:
  0.0 206.7 jit_solution(2055032910663638040)
XLA Ops:
  7.2 0.7 all-gather.2.cloned.1.call-update
  7.9 110.2 %all-gather.2.cloned.1.call-done = bf16[1024,4096]{1,0:T(8,128)(2,1)} async-done(((bf16[32,4096]{1,0:T(8,128)(2,1)}), bf16[1024,4096]{1,0:T(8,128)(2,1)}) %all-gather.2.cloned.1.call-update) | async-done | bytes 8388624 | tf_op jit(solution)/shard_map/all_gather | solution.py:25
  118.1 8.3 %add_reduce_fusion.1 = (f32[1024]{0:T(1024)S(1)}, f32[512,1024]{1,0:T(8,128)S(1)}) fusion(f32[512]{0:T(512)} %param.5, bf16[512,4096]{1,0:T(8,128)(2,1)} %param.4, bf16[1024,4096]{1,0:T(8,128)(2,1)} %all-gather.2.cloned.1.call-done), kind=kOutput, calls=%fused_computation.8 | convolution fusion | flops 4296539136 | bytes 14686208 | tf_op jit(solution)/shard_map/dot_general | solution.py:26
  126.4 0.4 exponential_reduce_fusion
  126.8 0.3 broadcast_in_dim.6
  127.1 20.2 %all_to_all.21 = f32[128,1,1024]{2,1,0:T(1,128)S(1)} all-to-all(f32[128,1,1024]{2,1,0:T(1,128)S(1)} %broadcast_in_dim.6), channel_id=1, replica_groups=mesh['psg'=32,'cen'=4] {'psg','cen'}, dimensions={0} | all-to-all | bytes 1048576 | tf_op jit(solution)/shard_map/all_to_all | solution.py:15
  147.4 0.4 reduce_max.28
  148.1 0.5 fusion.1
  148.6 2.1 %fusion.6 = (bf16[1024]{0:T(1024)(128)(2,1)S(1)}, f32[512,1024]{1,0:T(8,128)S(1)}) fusion(f32[512]{0:T(512)S(1)} %fusion.1, f32[512]{0:T(512)S(1)} %add_reduce_fusion, f32[512,1024]{1,0:T(8,128)} %copy-done, f32[1024]{0:T(1024)S(1)} %add_subtract_fusion), kind=kLoop, calls=%fused_computation.26 | loop fusion | flops 2096128 | bytes 4204544 | tf_op jit(solution)/shard_map/reduce_sum | solution.py:45
  150.7 0.3 broadcast_in_dim.7
  151.0 0.5 broadcast.44
  151.5 2.3 %reduce.3 = bf16[128,1024]{1,0:T(8,128)(2,1)S(1)} reduce(bf16[128,1,1024]{2,1,0:T(2,128)(2,1)S(1)} %broadcast_in_dim.7, bf16[]{:T(256)} %broadcast.44), dimensions={1}, to_apply=%broadcast_in_dim.7.reduce_sub_computation | reduce | bytes 524290 | tf_op jit(solution)/shard_map/broadcast_in_dim | solution.py:15
  153.9 15.0 %all_to_all.22 = bf16[128,2,512]{2,1,0:T(2,128)(2,1)S(1)} all-to-all(bf16[128,2,512]{2,1,0:T(2,128)(2,1)S(1)} %reshape.60), channel_id=1, replica_groups=mesh['psg'=32,'cen'=4] {'psg','cen'}, dimensions={0} | all-to-all | bytes 524288 | tf_op jit(solution)/shard_map/all_to_all | solution.py:15
  168.9 0.2 reshape.61
  169.5 0.2 multiply_reduce_fusion
  169.7 0.3 broadcast_in_dim.8
  170.0 2.3 %reduce.4 = bf16[128,1024]{1,0:T(8,128)(2,1)S(1)} reduce(bf16[128,1,1024]{2,1,0:T(2,128)(2,1)S(1)} %broadcast_in_dim.8, bf16[]{:T(256)} %broadcast.44), dimensions={1}, to_apply=%broadcast_in_dim.8.reduce_sub_computation | reduce | bytes 524290 | tf_op jit(solution)/shard_map/broadcast_in_dim | solution.py:15
  172.3 0.9 reshape.62
  173.2 3.9 %all-to-all-start.2 = ((bf16[128,2,512]{2,1,0:T(2,128)(2,1)}), bf16[128,2,512]{2,1,0:T(2,128)(2,1)S(1)}, u32[]{:S(2)}, u32[]{:S(2)}) async-start(bf16[128,2,512]{2,1,0:T(2,128)(2,1)} %reshape.62), calls=%async_computation.2 | async-start | bytes 524288 | tf_op jit(solution)/shard_map/all_to_all | solution.py:15
  177.1 11.4 %all-to-all-done.2 = bf16[128,2,512]{2,1,0:T(2,128)(2,1)S(1)} async-done(((bf16[128,2,512]{2,1,0:T(2,128)(2,1)}), bf16[128,2,512]{2,1,0:T(2,128)(2,1)S(1)}, u32[]{:S(2)}, u32[]{:S(2)}) %all-to-all-start.2) | async-done | bytes 262176 | tf_op jit(solution)/shard_map/all_to_all | solution.py:15
  188.5 0.2 reshape.63
  189.1 0.6 log_subtract_fusion
  189.7 0.6 dynamic_slice.3
  190.3 9.6 %convolution_convert_fusion = bf16[512,4096]{1,0:T(8,128)(2,1)} fusion(bf16[1024,4096]{1,0:T(8,128)(2,1)} %all-gather.2.cloned.1.call-done, f32[512,1024]{1,0:T(8,128)S(1)} %get-tuple-element.4, f32[512]{0:T(512)S(1)} %multiply_reduce_fusion.2, f32[1024]{0:T(1024)S(1)} %get-tuple-element.6), kind=kOutput, calls=%fused_computation | convolution fusion | flops 4298637312 | bytes 14686208 | tf_op jit(solution)/shard_map/dot_general | solution.py:51
  (17 shorter events, 1.2 us)
Async XLA Ops:
  7.2 111.0 %all-gather.2.cloned.1.call-start = ((), (), s32[]{:S(2)}) async-start(), calls=%async_computation.3 | async-start | bytes 8650752 | tf_op jit(solution)/shard_map/all_gather | solution.py:25
  7.9 118.5 %copy-start.1 = (f32[512]{0:T(512)S(1)}, f32[512]{0:T(512)}, u32[]{:S(2)}) copy-start(f32[512]{0:T(512)} %param.5) | copy-start | bytes 6148
  126.4 21.7 %copy-start = (f32[512,1024]{1,0:T(8,128)}, f32[512,1024]{1,0:T(8,128)S(1)}, u32[]{:S(2)}) copy-start(f32[512,1024]{1,0:T(8,128)S(1)} %get-tuple-element.8) | copy-start | bytes 6291460
  173.2 15.4 %all-to-all-start.2 = ((bf16[128,2,512]{2,1,0:T(2,128)(2,1)}), bf16[128,2,512]{2,1,0:T(2,128)(2,1)S(1)}, u32[]{:S(2)}, u32[]{:S(2)}) async-start(bf16[128,2,512]{2,1,0:T(2,128)(2,1)} %reshape.62), calls=%async_computation.2 | async-start | bytes 524288 | tf_op jit(solution)/shard_map/all_to_all | solution.py:15
Sparse Core Ops, SparseCore 0:
  11.0 107.0 all-gather.1

commit v2 on v1

v2 whole, which is shorter than its diff:
```python
import math

import jax
import jax.numpy as jnp
from jax import lax
from jax.sharding import PartitionSpec as P

CENTROIDS = 65536
PASSAGES = 1024
EVERY = ("psg", "cen")
X, Z, HALVES, CORES = 4, 4, 2, 2


def coords(device):
    return (
        device // (HALVES * X * 4),
        device // (X * 4) % HALVES,
        device // 4 % X,
        device // 2 % 2,
        device % 2,
    )


def move(value, target):
    pairs = []
    for device in range(Z * HALVES * X * 4):
        there = target(*coords(device))
        if there is not None:
            z, h, x, l, c = there
            pairs.append((device, (((z % Z) * HALVES + h) * X + x % X) * 4 + l * 2 + c))
    return lax.ppermute(value, EVERY, pairs)


def along_first(value, step):
    return move(
        value,
        lambda z, h, x, l, c: (z, h, x + step, l, c) if c == 0 else (z + step, h, x, l, c),
    )


def along_second(value, step):
    return move(
        value,
        lambda z, h, x, l, c: (z + step, h, x, l, c) if c == 0 else (z, h, x + step, l, c),
    )


def to_sibling(value):
    return move(value, lambda z, h, x, l, c: (z, h, x, l, 1 - c))


def to_every(values):
    count = lax.axis_size(EVERY)
    return lax.all_to_all(jnp.broadcast_to(values[None], (count, *values.shape)), EVERY, 0, 0)


def total_over_devices(partial):
    return jnp.sum(to_every(partial.astype(jnp.bfloat16)).astype(jnp.float32), axis=0)


def turned(rows, places):
    return lax.dynamic_slice_in_dim(jnp.concatenate([rows, rows], 0), 4 - places, 4, 0)


def body(passages, centroids, dual_init):
    depth = passages.shape[1]
    local_rows = passages.shape[0]
    factor = 4.0 / math.sqrt(depth)
    z, h, x, _, c = coords(lax.axis_index(EVERY))
    first = jnp.where(c == 0, x, z)
    second = jnp.where(c == 0, z, x)

    other = move(passages, lambda z, h, x, l, c: (z, 1 - h, x, l, c) if h == c else None)
    mine = jnp.where(h == c, passages, other)
    ring = [mine, along_first(mine, -1), along_first(mine, 2), along_first(mine, 1)]
    ring = turned(jnp.stack(ring), first).reshape(4 * local_rows, depth)
    left, right = ring[:, : depth // 2], ring[:, depth // 2 :]
    left_before = along_second(left, 1)
    right_after = along_second(right, -1)
    right_before = along_second(right, 1)
    left_after = along_second(left, -1)
    left_across = along_second(left_before, 1)
    right_across = along_second(right_after, -1)
    own = [
        (left, right),
        (left_after, right_after),
        (left_across, right_across),
        (left_before, right_before),
    ]
    sibling = [(to_sibling(a), to_sibling(b)) for a, b in own]
    chunks = own + sibling

    def chunk_logits(pair):
        parts = [
            lax.dot_general(
                weights, part, (((1,), (1,)), ((), ())), preferred_element_type=jnp.float32
            )
            for weights, part in zip(
                (centroids[:, : depth // 2], centroids[:, depth // 2 :]), pair
            )
        ]
        return factor * (parts[0] + parts[1])

    logits = jnp.concatenate([chunk_logits(pair) for pair in chunks], axis=1)
    span = logits.shape[1] // 2

    def common(values):
        a, b = values.reshape(2, 4, span // 4)
        a, b = turned(a, second), turned(b, first)
        return jnp.where(c == 0, jnp.stack([a, b]), jnp.stack([b, a])).reshape(8, span // 4)

    def local(values):
        a, b = values.reshape(2, 4, span // 4)
        a, b = jnp.where(c == 0, a, b), jnp.where(c == 0, b, a)
        return jnp.stack([turned(a, (4 - second) % 4), turned(b, (4 - first) % 4)]).reshape(2 * span)

    shifted = logits + dual_init[:, None]
    top = jnp.max(shifted, axis=0)
    parts = to_every(common(top + jnp.log(jnp.sum(jnp.exp(shifted - top[None, :]), axis=0))))
    top = jnp.max(parts, axis=0)
    passage_first = -math.log(PASSAGES) - (
        top + jnp.log(jnp.sum(jnp.exp(parts - top[None]), axis=0))
    )
    terms = logits + local(passage_first)[None, :]
    top = jnp.max(terms, axis=1)
    total = jnp.sum(jnp.exp(terms - top[:, None]), axis=1)
    centroid_first = -math.log(CENTROIDS) - (top + jnp.log(total))

    kernel = jnp.exp(terms - top[:, None]) / total[:, None]
    ratio = CENTROIDS / PASSAGES
    row_scale = ratio / total_over_devices(common(jnp.sum(kernel, axis=0)))
    col_scale = 1.0 / jnp.sum(kernel * local(row_scale)[None, :], axis=1)
    row_scale = ratio / total_over_devices(common(jnp.sum(kernel * col_scale[:, None], axis=0)))
    scaled = kernel * local(row_scale)[None, :]
    col_sum = jnp.sum(scaled, axis=1)

    weight = (scaled / col_sum[:, None]).astype(jnp.bfloat16)
    new_centroids = jnp.concatenate(
        [
            lax.dot_general(
                weight,
                jnp.concatenate([pair[side] for pair in chunks], axis=0),
                (((1,), (0,)), ((), ())),
                preferred_element_type=jnp.float32,
            ).astype(jnp.bfloat16)
            for side in (0, 1)
        ],
        axis=1,
    )
    passage_duals = passage_first + jnp.log(row_scale)
    start = jnp.where(h == 0, z * X + x, (Z + x) * X + z) * local_rows
    own_duals = lax.dynamic_slice_in_dim(passage_duals.reshape(2 * span), start, local_rows)
    return (new_centroids, own_duals, centroid_first - jnp.log(col_sum))


def solution(mesh):
    in_specs = (P("psg", None), P(("psg", "cen"), None), P(("psg", "cen")))
    out_specs = (P(("psg", "cen"), None), P("psg"), P(("psg", "cen")))
    return jax.shard_map(body, mesh=mesh, in_specs=in_specs, out_specs=out_specs, check_vma=False)
```

time: 207 us -> 140 us (0.68)
  waiting for transfers between devices: 122 us -> 53 us
  starting transfers between devices: 3.96 us -> 42.4 us
  blocking collectives: 35.2 us -> 0 us
  between operations: 14.2 us -> 1.45 us
  local copies, waits for them, and re-layouts: 3.42 us -> 13.9 us
  matrix products: 17.8 us -> 20.8 us
    all_gather x1 -> x0, waiting for transfers between devices: 110 us -> none  [body(): gathered = lax.all_gather(passages, 'psg', axis=0, tiled=True)]
    all_to_all x2 -> x0, blocking collectives: 35.2 us -> none  [to_every(): lax.all_to_all(jnp.broadcast_to(values[None], (count, *values.shape)), EV...]
    ppermute x0 -> x18, starting transfers between devices: none -> 28.9 us  [move(): return lax.ppermute(value, EVERY, pairs)]
    ppermute x0 -> x18, waiting for transfers between devices: none -> 25 us  [move(): return lax.ppermute(value, EVERY, pairs)]
    all_to_all x1 -> x3, waiting for transfers between devices: 11.4 us -> 27.9 us  [to_every(): lax.all_to_all(jnp.broadcast_to(values[None], (count, *values.shape)), EV...]
    all_to_all x1 -> x3, starting transfers between devices: 3.93 us -> 13.5 us  [to_every(): lax.all_to_all(jnp.broadcast_to(values[None], (count, *values.shape)), EV...]
    unnamed x8 -> x49, local copies, waits for them, and re-layouts: 1.51 us -> 9.05 us
    broadcast_in_dim x2 -> x0, other arithmetic: 4.53 us -> none  [to_every(): jnp.broadcast_to(values[None], (count, *values.shape))]
  transfers between devices with their start and end apart: 2 -> 21, of which waited for: 2 -> 8; matrix products, arithmetic and copies ran while one was open for 0% -> 16% of each run, Pallas kernels for 0% -> 0%
where the time goes in v2:
time: 140 us; the launch traced here: 139 us
  waiting for transfers between devices  53 us (38%)
  starting transfers between devices  42.4 us (30%)
  matrix products  20.8 us (15%)
  local copies, waits for them, and re-layouts  13.9 us (10%)
  other arithmetic  7.87 us (6%)
  between operations  1.45 us (1%)
    ppermute x18, starting transfers between devices, move(): return lax.ppermute(value, EVERY, pairs)  28.9 us
    all_to_all x3, waiting for transfers between devices, to_every(): lax.all_to_all(jnp.broadcast_to(values[None], (count, *values.shape)), EV...  27.9 us
    ppermute x18, waiting for transfers between devices, move(): return lax.ppermute(value, EVERY, pairs)  25 us
    all_to_all x3, starting transfers between devices, to_every(): lax.all_to_all(jnp.broadcast_to(values[None], (count, *values.shape)), EV...  13.5 us
    dot_general x16, matrix products, chunk_logits(): lax.dot_general(weights, part, (((1,), (1,)), ((), ())), preferred_elemen...  13.3 us
    unnamed x49, local copies, waits for them, and re-layouts  9.05 us
    dot_general x2, matrix products, body(): lax.dot_general(weight, jnp.concatenate([pair[side] for pair in chunks],...  7.47 us
  transfers between devices with their start and end apart: 21, of which 8 were waited for; matrix products, arithmetic and copies ran while one was open for 16% of the time, Pallas kernels for 0%

profile of v2, /device:TPU:1, one launch (start us, length us, event | category | flops | bytes accessed | tf_op | source)
XLA Modules:
  0.0 139.4 jit_solution(1302963441951268467)
XLA Ops:
  2.0 7.6 %collective-permute-done = bf16[32,4096]{1,0:T(8,128)(2,1)S(1)} collective-permute-done((bf16[32,4096]{1,0:T(8,128)(2,1)}, bf16[32,4096]{1,0:T(8,128)(2,1)S(1)}, u32[]{:S(2)}, u32[]{:S(2)}) %collective-permute-start) | collective-permute-done | bytes 262176 | tf_op jit(solution)/shard_map/ppermute | solution.py:31
  9.7 4.5 %collective-permute-start.1 = (bf16[32,4096]{1,0:T(8,128)(2,1)S(1)}, bf16[32,4096]{1,0:T(8,128)(2,1)S(1)}, u32[]{:S(2)}, u32[]{:S(2)}) collective-permute-start(bf16[32,4096]{1,0:T(8,128)(2,1)S(1)} %get-tuple-element.6), channel_id=1, source_target_pairs={{0,12},{1,97},{2,14},{3,99},{4,0},{5,101},{6,2},{7,103},{8,4},{9,1... | collective-permute-start | bytes 786440 | tf_op jit(solution)/shard_map/ppermute | solution.py:31
  15.0 5.3 %collective-permute-done.1 = bf16[32,4096]{1,0:T(8,128)(2,1)S(1)} collective-permute-done((bf16[32,4096]{1,0:T(8,128)(2,1)S(1)}, bf16[32,4096]{1,0:T(8,128)(2,1)S(1)}, u32[]{:S(2)}, u32[]{:S(2)}) %collective-permute-start.1) | collective-permute-done | bytes 262176 | tf_op jit(solution)/shard_map/ppermute | solution.py:31
  21.3 2.5 %collective-permute-done.3 = bf16[32,4096]{1,0:T(8,128)(2,1)S(1)} collective-permute-done((bf16[32,4096]{1,0:T(8,128)(2,1)S(1)}, bf16[32,4096]{1,0:T(8,128)(2,1)S(1)}, u32[]{:S(2)}, u32[]{:S(2)}) %collective-permute-start.3) | collective-permute-done | bytes 262176 | tf_op jit(solution)/shard_map/ppermute | solution.py:31
  24.3 2.3 %collective-permute-start.5 = (bf16[128,2048]{1,0:T(8,128)(2,1)S(1)}, bf16[128,2048]{1,0:T(8,128)(2,1)S(1)}, u32[]{:S(2)}, u32[]{:S(2)}) collective-permute-start(bf16[128,2048]{1,0:T(8,128)(2,1)S(1)} %get-tuple-element.9), channel_id=1, source_target_pairs={{0,96},{1,13},{2,98},{3,15},{4,100},{5,1},{6,102},{7,3},{8,104},{9... | collective-permute-start | bytes 1572872 | tf_op jit(solution)/shard_map/ppermute | solution.py:31
  26.5 4.0 %collective-permute-start.11 = (bf16[128,2048]{1,0:T(8,128)(2,1)S(1)}, bf16[128,2048]{1,0:T(8,128)(2,1)S(1)}, u32[]{:S(2)}, u32[]{:S(2)}) collective-permute-start(bf16[128,2048]{1,0:T(8,128)(2,1)S(1)} %get-tuple-element.9), channel_id=1, source_target_pairs={{0,1},{1,0},{2,3},{3,2},{4,5},{5,4},{6,7},{7,6},{8,9},{9,8},{10,11... | collective-permute-start | bytes 1572872 | tf_op jit(solution)/shard_map/ppermute | solution.py:31
  33.7 3.5 %collective-permute-start.10 = (bf16[128,2048]{1,0:T(8,128)(2,1)S(1)}, bf16[128,2048]{1,0:T(8,128)(2,1)S(1)}, u32[]{:S(2)}, u32[]{:S(2)}) collective-permute-start(bf16[128,2048]{1,0:T(8,128)(2,1)S(1)} %get-tuple-element.10), channel_id=1, source_target_pairs={{0,1},{1,0},{2,3},{3,2},{4,5},{5,4},{6,7},{7,6},{8,9},{9,8},{10,11... | collective-permute-start | bytes 1572872 | tf_op jit(solution)/shard_map/ppermute | solution.py:31
  39.4 3.4 %collective-permute-start.13 = (bf16[128,2048]{1,0:T(8,128)(2,1)S(1)}, bf16[128,2048]{1,0:T(8,128)(2,1)S(1)}, u32[]{:S(2)}, u32[]{:S(2)}) collective-permute-start(bf16[128,2048]{1,0:T(8,128)(2,1)S(1)} %collective-permute-done.5), channel_id=1, source_target_pairs={{0,1},{1,0},{2,3},{3,2},{4,5},{5,4},{6,7},{7,6},{8,9},{9,8},{10,11... | collective-permute-start | bytes 1572872 | tf_op jit(solution)/shard_map/ppermute | solution.py:31
  44.7 1.9 %collective-permute-start.12 = (bf16[128,2048]{1,0:T(8,128)(2,1)S(1)}, bf16[128,2048]{1,0:T(8,128)(2,1)S(1)}, u32[]{:S(2)}, u32[]{:S(2)}) collective-permute-start(bf16[128,2048]{1,0:T(8,128)(2,1)S(1)} %collective-permute-done.4), channel_id=1, source_target_pairs={{0,1},{1,0},{2,3},{3,2},{4,5},{5,4},{6,7},{7,6},{8,9},{9,8},{10,11... | collective-permute-start | bytes 1572872 | tf_op jit(solution)/shard_map/ppermute | solution.py:31
  47.5 8.6 %collective-permute-done.7 = bf16[128,2048]{1,0:T(8,128)(2,1)S(1)} collective-permute-done((bf16[128,2048]{1,0:T(8,128)(2,1)S(1)}, bf16[128,2048]{1,0:T(8,128)(2,1)S(1)}, u32[]{:S(2)}, u32[]{:S(2)}) %collective-permute-start.7) | collective-permute-done | bytes 524320 | tf_op jit(solution)/shard_map/ppermute | solution.py:31
  56.1 4.4 %collective-permute-start.16 = (bf16[128,2048]{1,0:T(8,128)(2,1)S(1)}, bf16[128,2048]{1,0:T(8,128)(2,1)S(1)}, u32[]{:S(2)}, u32[]{:S(2)}) collective-permute-start(bf16[128,2048]{1,0:T(8,128)(2,1)S(1)} %collective-permute-done.6), channel_id=1, source_target_pairs={{0,1},{1,0},{2,3},{3,2},{4,5},{5,4},{6,7},{7,6},{8,9},{9,8},{10,11... | collective-permute-start | bytes 1572872 | tf_op jit(solution)/shard_map/ppermute | solution.py:31
  72.0 5.8 %all-to-all-start = ((f32[128,8,128]{2,1,0:T(8,128)}), f32[128,8,128]{2,1,0:T(8,128)S(1)}, u32[]{:S(2)}, u32[]{:S(2)}) async-start(f32[128,8,128]{2,1,0:T(8,128)} %broadcast_in_dim.6), calls=%async_computation | async-start | bytes 1048576 | tf_op jit(solution)/shard_map/all_to_all | solution.py:54
  77.7 1.9 %constant_dynamic-update-slice_fusion.4 = bf16[1024,2048]{1,0:T(8,128)(2,1)} fusion(bf16[1024,2048]{1,0:T(8,128)(2,1)} %copy-done.10, bf16[128,2048]{1,0:T(8,128)(2,1)} %copy-done.5), kind=kLoop, calls=%fused_computation.85 | loop fusion | bytes 1048576
  79.7 1.9 %constant_dynamic-update-slice_fusion.3 = bf16[1024,2048]{1,0:T(8,128)(2,1)} fusion(bf16[1024,2048]{1,0:T(8,128)(2,1)} %constant_dynamic-update-slice_fusion.4, bf16[128,2048]{1,0:T(8,128)(2,1)} %copy-done.6), kind=kLoop, calls=%fused_computation.84 | loop fusion | bytes 1048576
  82.4 9.3 %all-to-all-done = f32[128,8,128]{2,1,0:T(8,128)S(1)} async-done(((f32[128,8,128]{2,1,0:T(8,128)}), f32[128,8,128]{2,1,0:T(8,128)S(1)}, u32[]{:S(2)}, u32[]{:S(2)}) %all-to-all-start) | async-done | bytes 524320 | tf_op jit(solution)/shard_map/all_to_all | solution.py:54
  92.8 1.8 %fusion.66 = (bf16[1024]{0:T(1024)(128)(2,1)S(1)}, f32[512,1024]{0,1:T(8,128)}) fusion(f32[512]{0:T(512)S(1)} %fusion.1, f32[512]{0:T(512)S(1)} %add_reduce_fusion, f32[512,1024]{0,1:T(8,128)S(1)} %fusion.4, f32[1024]{0:T(1024)S(1)} %bitcast.110), kind=kLoop, calls=%fused_computation.163 | loop fusion | flops 2096128 | bytes 4204544 | tf_op jit(solution)/shard_map/reduce_sum | solution.py:131
  95.5 3.8 %all-to-all-start.1 = ((bf16[128,8,128]{2,1,0:T(8,128)(2,1)}), bf16[128,8,128]{2,1,0:T(8,128)(2,1)S(1)}, u32[]{:S(2)}, u32[]{:S(2)}) async-start(bf16[128,8,128]{2,1,0:T(8,128)(2,1)} %broadcast_in_dim.7), calls=%async_computation.1 | async-start | bytes 524288 | tf_op jit(solution)/shard_map/all_to_all | solution.py:54
  99.3 1.9 %constant_dynamic-update-slice_fusion.9 = bf16[1024,2048]{1,0:T(8,128)(2,1)} fusion(bf16[1024,2048]{1,0:T(8,128)(2,1)} %copy-done.12, bf16[128,2048]{1,0:T(8,128)(2,1)} %copy-done.7), kind=kLoop, calls=%fused_computation.90 | loop fusion | bytes 1048576
  102.0 8.8 %all-to-all-done.1 = bf16[128,8,128]{2,1,0:T(8,128)(2,1)S(1)} async-done(((bf16[128,8,128]{2,1,0:T(8,128)(2,1)}), bf16[128,8,128]{2,1,0:T(8,128)(2,1)S(1)}, u32[]{:S(2)}, u32[]{:S(2)}) %all-to-all-start.1) | async-done | bytes 262176 | tf_op jit(solution)/shard_map/all_to_all | solution.py:54
  112.4 3.9 %all-to-all-start.2 = ((bf16[128,8,128]{2,1,0:T(8,128)(2,1)}), bf16[128,8,128]{2,1,0:T(8,128)(2,1)S(1)}, u32[]{:S(2)}, u32[]{:S(2)}) async-start(bf16[128,8,128]{2,1,0:T(8,128)(2,1)} %broadcast_in_dim.8), calls=%async_computation.2 | async-start | bytes 524288 | tf_op jit(solution)/shard_map/all_to_all | solution.py:54
  118.0 9.7 %all-to-all-done.2 = bf16[128,8,128]{2,1,0:T(8,128)(2,1)S(1)} async-done(((bf16[128,8,128]{2,1,0:T(8,128)(2,1)}), bf16[128,8,128]{2,1,0:T(8,128)(2,1)S(1)}, u32[]{:S(2)}, u32[]{:S(2)}) %all-to-all-start.2) | async-done | bytes 262176 | tf_op jit(solution)/shard_map/all_to_all | solution.py:54
  128.8 4.8 %convolution_convert_fusion = bf16[512,2048]{1,0:T(8,128)(2,1)S(1)} fusion(bf16[1024,2048]{1,0:T(8,128)(2,1)} %constant_dynamic-update-slice_fusion.8, f32[512,1024]{0,1:T(8,128)S(1)} %copy-done, f32[512]{0:T(512)S(1)} %multiply_reduce_fusion.2, f32[1024]{0:T(1024)S(1)} %bitcast.112), kind=kOutput, calls=%fused_computation.1 | convolution fusion | flops 2150105088 | bytes 8394752 | tf_op jit(solution)/shard_map/dot_general | solution.py:140
  133.7 2.6 %convolution_convert_fusion.1 = bf16[512,2048]{1,0:T(8,128)(2,1)S(1)} fusion(bf16[1024,2048]{1,0:T(8,128)(2,1)S(1)} %copy-done.11, f32[512,1024]{0,1:T(8,128)S(1)} %copy-done, f32[512]{0:T(512)S(1)} %multiply_reduce_fusion.2, f32[1024]{0:T(1024)S(1)} %bitcast.113), kind=kOutput, calls=%fused_computation.2 | convolution fusion | flops 2150105088 | bytes 8394752 | tf_op jit(solution)/shard_map/dot_general | solution.py:140
  136.3 2.5 %pad_maximum_fusion = bf16[512,4096]{1,0:T(8,128)(2,1)} fusion(bf16[512,2048]{1,0:T(8,128)(2,1)S(1)} %convolution_convert_fusion, bf16[512,2048]{1,0:T(8,128)(2,1)S(1)} %convolution_convert_fusion.1), kind=kLoop, calls=%fused_computation | loop fusion | flops 8388608 | bytes 8388608 | tf_op jit(solution)/shard_map/concatenate | solution.py:138
  (148 shorter events, 30.9 us)
Async XLA Ops:
  0.6 9.0 %collective-permute-start = (bf16[32,4096]{1,0:T(8,128)(2,1)}, bf16[32,4096]{1,0:T(8,128)(2,1)S(1)}, u32[]{:S(2)}, u32[]{:S(2)}) collective-permute-start(bf16[32,4096]{1,0:T(8,128)(2,1)} %param.3), channel_id=1, source_target_pairs={{0,16},{2,18},{4,20},{6,22},{8,24},{10,26},{12,28},{14,30},{17,1},... | collective-permute-start | bytes 786440 | tf_op jit(solution)/shard_map/ppermute | solution.py:31
  9.7 10.6 %collective-permute-start.1 = (bf16[32,4096]{1,0:T(8,128)(2,1)S(1)}, bf16[32,4096]{1,0:T(8,128)(2,1)S(1)}, u32[]{:S(2)}, u32[]{:S(2)}) collective-permute-start(bf16[32,4096]{1,0:T(8,128)(2,1)S(1)} %get-tuple-element.6), channel_id=1, source_target_pairs={{0,12},{1,97},{2,14},{3,99},{4,0},{5,101},{6,2},{7,103},{8,4},{9,1... | collective-permute-start | bytes 786440 | tf_op jit(solution)/shard_map/ppermute | solution.py:31
  14.2 7.1 %collective-permute-start.2 = (bf16[32,4096]{1,0:T(8,128)(2,1)S(1)}, bf16[32,4096]{1,0:T(8,128)(2,1)S(1)}, u32[]{:S(2)}, u32[]{:S(2)}) collective-permute-start(bf16[32,4096]{1,0:T(8,128)(2,1)S(1)} %get-tuple-element.6), channel_id=1, source_target_pairs={{0,8},{1,65},{2,10},{3,67},{4,12},{5,69},{6,14},{7,71},{8,0},{9,73... | collective-permute-start | bytes 786440 | tf_op jit(solution)/shard_map/ppermute | solution.py:31
  14.2 9.5 %collective-permute-start.3 = (bf16[32,4096]{1,0:T(8,128)(2,1)S(1)}, bf16[32,4096]{1,0:T(8,128)(2,1)S(1)}, u32[]{:S(2)}, u32[]{:S(2)}) collective-permute-start(bf16[32,4096]{1,0:T(8,128)(2,1)S(1)} %get-tuple-element.6), channel_id=1, source_target_pairs={{0,4},{1,33},{2,6},{3,35},{4,8},{5,37},{6,10},{7,39},{8,12},{9,41}... | collective-permute-start | bytes 786440 | tf_op jit(solution)/shard_map/ppermute | solution.py:31
  24.3 9.5 %collective-permute-start.5 = (bf16[128,2048]{1,0:T(8,128)(2,1)S(1)}, bf16[128,2048]{1,0:T(8,128)(2,1)S(1)}, u32[]{:S(2)}, u32[]{:S(2)}) collective-permute-start(bf16[128,2048]{1,0:T(8,128)(2,1)S(1)} %get-tuple-element.9), channel_id=1, source_target_pairs={{0,96},{1,13},{2,98},{3,15},{4,100},{5,1},{6,102},{7,3},{8,104},{9... | collective-permute-start | bytes 1572872 | tf_op jit(solution)/shard_map/ppermute | solution.py:31
  26.5 11.6 %collective-permute-start.9 = (bf16[128,2048]{1,0:T(8,128)(2,1)S(1)}, bf16[128,2048]{1,0:T(8,128)(2,1)S(1)}, u32[]{:S(2)}, u32[]{:S(2)}) collective-permute-start(bf16[128,2048]{1,0:T(8,128)(2,1)S(1)} %get-tuple-element.9), channel_id=1, source_target_pairs={{0,32},{1,5},{2,34},{3,7},{4,36},{5,9},{6,38},{7,11},{8,40},{9,13}... | collective-permute-start | bytes 1572872 | tf_op jit(solution)/shard_map/ppermute | solution.py:31
  26.5 12.9 %collective-permute-start.11 = (bf16[128,2048]{1,0:T(8,128)(2,1)S(1)}, bf16[128,2048]{1,0:T(8,128)(2,1)S(1)}, u32[]{:S(2)}, u32[]{:S(2)}) collective-permute-start(bf16[128,2048]{1,0:T(8,128)(2,1)S(1)} %get-tuple-element.9), channel_id=1, source_target_pairs={{0,1},{1,0},{2,3},{3,2},{4,5},{5,4},{6,7},{7,6},{8,9},{9,8},{10,11... | collective-permute-start | bytes 1572872 | tf_op jit(solution)/shard_map/ppermute | solution.py:31
  30.6 13.1 %collective-permute-start.4 = (bf16[128,2048]{1,0:T(8,128)(2,1)S(1)}, bf16[128,2048]{1,0:T(8,128)(2,1)S(1)}, u32[]{:S(2)}, u32[]{:S(2)}) collective-permute-start(bf16[128,2048]{1,0:T(8,128)(2,1)S(1)} %get-tuple-element.10), channel_id=1, source_target_pairs={{0,96},{1,13},{2,98},{3,15},{4,100},{5,1},{6,102},{7,3},{8,104},{9... | collective-permute-start | bytes 1572872 | tf_op jit(solution)/shard_map/ppermute | solution.py:31
  30.9 13.8 %collective-permute-start.6 = (bf16[128,2048]{1,0:T(8,128)(2,1)S(1)}, bf16[128,2048]{1,0:T(8,128)(2,1)S(1)}, u32[]{:S(2)}, u32[]{:S(2)}) collective-permute-start(bf16[128,2048]{1,0:T(8,128)(2,1)S(1)} %get-tuple-element.10), channel_id=1, source_target_pairs={{0,32},{1,5},{2,34},{3,7},{4,36},{5,9},{6,38},{7,11},{8,40},{9,13}... | collective-permute-start | bytes 1572872 | tf_op jit(solution)/shard_map/ppermute | solution.py:31
  33.7 28.5 %collective-permute-start.10 = (bf16[128,2048]{1,0:T(8,128)(2,1)S(1)}, bf16[128,2048]{1,0:T(8,128)(2,1)S(1)}, u32[]{:S(2)}, u32[]{:S(2)}) collective-permute-start(bf16[128,2048]{1,0:T(8,128)(2,1)S(1)} %get-tuple-element.10), channel_id=1, source_target_pairs={{0,1},{1,0},{2,3},{3,2},{4,5},{5,4},{6,7},{7,6},{8,9},{9,8},{10,11... | collective-permute-start | bytes 1572872 | tf_op jit(solution)/shard_map/ppermute | solution.py:31
  38.1 8.5 %collective-permute-start.8 = (bf16[128,2048]{1,0:T(8,128)(2,1)S(1)}, bf16[128,2048]{1,0:T(8,128)(2,1)S(1)}, u32[]{:S(2)}, u32[]{:S(2)}) collective-permute-start(bf16[128,2048]{1,0:T(8,128)(2,1)S(1)} %collective-permute-done.5), channel_id=1, source_target_pairs={{0,96},{1,13},{2,98},{3,15},{4,100},{5,1},{6,102},{7,3},{8,104},{9... | collective-permute-start | bytes 1572872 | tf_op jit(solution)/shard_map/ppermute | solution.py:31
  39.4 23.8 %collective-permute-start.13 = (bf16[128,2048]{1,0:T(8,128)(2,1)S(1)}, bf16[128,2048]{1,0:T(8,128)(2,1)S(1)}, u32[]{:S(2)}, u32[]{:S(2)}) collective-permute-start(bf16[128,2048]{1,0:T(8,128)(2,1)S(1)} %collective-permute-done.5), channel_id=1, source_target_pairs={{0,1},{1,0},{2,3},{3,2},{4,5},{5,4},{6,7},{7,6},{8,9},{9,8},{10,11... | collective-permute-start | bytes 1572872 | tf_op jit(solution)/shard_map/ppermute | solution.py:31
  43.7 22.1 %collective-permute-start.17 = (bf16[128,2048]{1,0:T(8,128)(2,1)S(1)}, bf16[128,2048]{1,0:T(8,128)(2,1)S(1)}, u32[]{:S(2)}, u32[]{:S(2)}) collective-permute-start(bf16[128,2048]{1,0:T(8,128)(2,1)S(1)} %collective-permute-done.9), channel_id=1, source_target_pairs={{0,1},{1,0},{2,3},{3,2},{4,5},{5,4},{6,7},{7,6},{8,9},{9,8},{10,11... | collective-permute-start | bytes 1572872 | tf_op jit(solution)/shard_map/ppermute | solution.py:31
  44.7 16.7 %copy-start.5 = (bf16[128,2048]{1,0:T(8,128)(2,1)}, bf16[128,2048]{1,0:T(8,128)(2,1)S(1)}, u32[]{:S(2)}) copy-start(bf16[128,2048]{1,0:T(8,128)(2,1)S(1)} %collective-permute-done.6) | copy-start | bytes 1572868
  44.7 20.2 %collective-permute-start.12 = (bf16[128,2048]{1,0:T(8,128)(2,1)S(1)}, bf16[128,2048]{1,0:T(8,128)(2,1)S(1)}, u32[]{:S(2)}, u32[]{:S(2)}) collective-permute-start(bf16[128,2048]{1,0:T(8,128)(2,1)S(1)} %collective-permute-done.4), channel_id=1, source_target_pairs={{0,1},{1,0},{2,3},{3,2},{4,5},{5,4},{6,7},{7,6},{8,9},{9,8},{10,11... | collective-permute-start | bytes 1572872 | tf_op jit(solution)/shard_map/ppermute | solution.py:31
  46.6 9.5 %collective-permute-start.7 = (bf16[128,2048]{1,0:T(8,128)(2,1)S(1)}, bf16[128,2048]{1,0:T(8,128)(2,1)S(1)}, u32[]{:S(2)}, u32[]{:S(2)}) collective-permute-start(bf16[128,2048]{1,0:T(8,128)(2,1)S(1)} %collective-permute-done.6), channel_id=1, source_target_pairs={{0,32},{1,5},{2,34},{3,7},{4,36},{5,9},{6,38},{7,11},{8,40},{9,13}... | collective-permute-start | bytes 1572872 | tf_op jit(solution)/shard_map/ppermute | solution.py:31
  56.1 13.2 %collective-permute-start.16 = (bf16[128,2048]{1,0:T(8,128)(2,1)S(1)}, bf16[128,2048]{1,0:T(8,128)(2,1)S(1)}, u32[]{:S(2)}, u32[]{:S(2)}) collective-permute-start(bf16[128,2048]{1,0:T(8,128)(2,1)S(1)} %collective-permute-done.6), channel_id=1, source_target_pairs={{0,1},{1,0},{2,3},{3,2},{4,5},{5,4},{6,7},{7,6},{8,9},{9,8},{10,11... | collective-permute-start | bytes 1572872 | tf_op jit(solution)/shard_map/ppermute | solution.py:31
  62.3 4.9 %collective-permute-start.15 = (bf16[128,2048]{1,0:T(8,128)(2,1)S(1)}, bf16[128,2048]{1,0:T(8,128)(2,1)S(1)}, u32[]{:S(2)}, u32[]{:S(2)}) collective-permute-start(bf16[128,2048]{1,0:T(8,128)(2,1)S(1)} %collective-permute-done.8), channel_id=1, source_target_pairs={{0,1},{1,0},{2,3},{3,2},{4,5},{5,4},{6,7},{7,6},{8,9},{9,8},{10,11... | collective-permute-start | bytes 1572872 | tf_op jit(solution)/shard_map/ppermute | solution.py:31
  63.2 4.8 %collective-permute-start.14 = (bf16[128,2048]{1,0:T(8,128)(2,1)S(1)}, bf16[128,2048]{1,0:T(8,128)(2,1)S(1)}, u32[]{:S(2)}, u32[]{:S(2)}) collective-permute-start(bf16[128,2048]{1,0:T(8,128)(2,1)S(1)} %collective-permute-done.7), channel_id=1, source_target_pairs={{0,1},{1,0},{2,3},{3,2},{4,5},{5,4},{6,7},{7,6},{8,9},{9,8},{10,11... | collective-permute-start | bytes 1572872 | tf_op jit(solution)/shard_map/ppermute | solution.py:31
  72.0 19.8 %all-to-all-start = ((f32[128,8,128]{2,1,0:T(8,128)}), f32[128,8,128]{2,1,0:T(8,128)S(1)}, u32[]{:S(2)}, u32[]{:S(2)}) async-start(f32[128,8,128]{2,1,0:T(8,128)} %broadcast_in_dim.6), calls=%async_computation | async-start | bytes 1048576 | tf_op jit(solution)/shard_map/all_to_all | solution.py:54
  92.8 8.4 %copy-start.2 = (bf16[128,2048]{1,0:T(8,128)(2,1)S(1)}, bf16[128,2048]{1,0:T(8,128)(2,1)}, u32[]{:S(2)}) copy-start(bf16[128,2048]{1,0:T(8,128)(2,1)} %copy-done.1) | copy-start | bytes 1572868
  94.6 16.4 %copy-start = (f32[512,1024]{0,1:T(8,128)S(1)}, f32[512,1024]{0,1:T(8,128)}, u32[]{:S(2)}) copy-start(f32[512,1024]{0,1:T(8,128)} %get-tuple-element.4) | copy-start | bytes 6291460
  95.5 15.3 %all-to-all-start.1 = ((bf16[128,8,128]{2,1,0:T(8,128)(2,1)}), bf16[128,8,128]{2,1,0:T(8,128)(2,1)S(1)}, u32[]{:S(2)}, u32[]{:S(2)}) async-start(bf16[128,8,128]{2,1,0:T(8,128)(2,1)} %broadcast_in_dim.7), calls=%async_computation.1 | async-start | bytes 524288 | tf_op jit(solution)/shard_map/all_to_all | solution.py:54
  112.4 15.4 %all-to-all-start.2 = ((bf16[128,8,128]{2,1,0:T(8,128)(2,1)}), bf16[128,8,128]{2,1,0:T(8,128)(2,1)S(1)}, u32[]{:S(2)}, u32[]{:S(2)}) async-start(bf16[128,8,128]{2,1,0:T(8,128)(2,1)} %broadcast_in_dim.8), calls=%async_computation.2 | async-start | bytes 524288 | tf_op jit(solution)/shard_map/all_to_all | solution.py:54
  (12 other events, 35.7 us)

commit v3 on v2

--- a/solution.py
+++ b/solution.py
@@ -29,13 +29,6 @@
             z, h, x, l, c = there
             pairs.append((device, (((z % Z) * HALVES + h) * X + x % X) * 4 + l * 2 + c))
     return lax.ppermute(value, EVERY, pairs)
-
-
-def along_first(value, step):
-    return move(
-        value,
-        lambda z, h, x, l, c: (z, h, x + step, l, c) if c == 0 else (z + step, h, x, l, c),
-    )
 
 
 def along_second(value, step):
@@ -70,38 +63,32 @@
     first = jnp.where(c == 0, x, z)
     second = jnp.where(c == 0, z, x)
 
-    other = move(passages, lambda z, h, x, l, c: (z, 1 - h, x, l, c) if h == c else None)
-    mine = jnp.where(h == c, passages, other)
-    ring = [mine, along_first(mine, -1), along_first(mine, 2), along_first(mine, 1)]
+    def fetch(step):
+        def target(z, h, x, l, c):
+            stays = h == c
+            if stays and step == 0:
+                return None
+            h, c = (h, c) if stays else (1 - h, 1 - c)
+            return (z, h, x - step, l, c) if c == 0 else (z - step, h, x, l, c)
+
+        return move(passages, target)
+
+    ring = [jnp.where(h == c, passages, fetch(0)), fetch(1), fetch(2), fetch(3)]
     ring = turned(jnp.stack(ring), first).reshape(4 * local_rows, depth)
-    left, right = ring[:, : depth // 2], ring[:, depth // 2 :]
-    left_before = along_second(left, 1)
-    right_after = along_second(right, -1)
-    right_before = along_second(right, 1)
-    left_after = along_second(left, -1)
-    left_across = along_second(left_before, 1)
-    right_across = along_second(right_after, -1)
     own = [
-        (left, right),
-        (left_after, right_after),
-        (left_across, right_across),
-        (left_before, right_before),
+        ring,
+        along_second(ring, -1),
+        along_second(ring, 2),
+        along_second(ring, 1),
     ]
-    sibling = [(to_sibling(a), to_sibling(b)) for a, b in own]
-    chunks = own + sibling
+    chunks = own + [to_sibling(chunk) for chunk in own]
 
-    def chunk_logits(pair):
-        parts = [
-            lax.dot_general(
-                weights, part, (((1,), (1,)), ((), ())), preferred_element_type=jnp.float32
-            )
-            for weights, part in zip(
-                (centroids[:, : depth // 2], centroids[:, depth // 2 :]), pair
-            )
-        ]
-        return factor * (parts[0] + parts[1])
+    def chunk_logits(chunk):
+        return factor * lax.dot_general(
+            centroids, chunk, (((1,), (1,)), ((), ())), preferred_element_type=jnp.float32
+        )
 
-    logits = jnp.concatenate([chunk_logits(pair) for pair in chunks], axis=1)
+    logits = jnp.concatenate([chunk_logits(chunk) for chunk in chunks], axis=1)
     span = logits.shape[1] // 2
 
     def common(values):
@@ -135,18 +122,12 @@
     col_sum = jnp.sum(scaled, axis=1)
 
     weight = (scaled / col_sum[:, None]).astype(jnp.bfloat16)
-    new_centroids = jnp.concatenate(
-        [
-            lax.dot_general(
-                weight,
-                jnp.concatenate([pair[side] for pair in chunks], axis=0),
-                (((1,), (0,)), ((), ())),
-                preferred_element_type=jnp.float32,
-            ).astype(jnp.bfloat16)
-            for side in (0, 1)
-        ],
-        axis=1,
-    )
+    new_centroids = lax.dot_general(
+        weight,
+        jnp.concatenate(chunks, axis=0),
+        (((1,), (0,)), ((), ())),
+        preferred_element_type=jnp.float32,
+    ).astype(jnp.bfloat16)
     passage_duals = passage_first + jnp.log(row_scale)
     start = jnp.where(h == 0, z * X + x, (Z + x) * X + z) * local_rows
     own_duals = lax.dynamic_slice_in_dim(passage_duals.reshape(2 * span), start, local_rows)

time: 140 us -> 144 us (1.029)
  matrix products: 20.8 us -> 26.6 us
  waiting for transfers between devices: 53 us -> 47.9 us
  starting transfers between devices: 42.4 us -> 46.2 us
  other arithmetic: 7.87 us -> 5.41 us
  local copies, waits for them, and re-layouts: 13.9 us -> 15.8 us
    ppermute x18 -> x11, waiting for transfers between devices: 25 us -> 16.4 us  [move(): return lax.ppermute(value, EVERY, pairs)]
    all_to_all x3, starting transfers between devices: 13.5 us -> 19.6 us  [to_every(): lax.all_to_all(jnp.broadcast_to(values[None], (count, *values.shape)), EV...]
    dot_general x18 -> x9, matrix products: 20.8 us -> 26.6 us  [the longest x8 16.9 us: chunk_logits(): lax.dot_general(centroids, chunk, (((1,), (1,)), ((), ())), preferred_ele...]
    all_to_all x3, waiting for transfers between devices: 27.9 us -> 31.5 us  [to_every(): lax.all_to_all(jnp.broadcast_to(values[None], (count, *values.shape)), EV...]
    concatenate x1 -> x0, other arithmetic: 2.51 us -> none  [body(): jnp.concatenate([lax.dot_general(weight, jnp.concatenate([pair[side] for...]
    unnamed x49 -> x34, local copies, waits for them, and re-layouts: 9.05 us -> 11.6 us
    ppermute x18 -> x11, starting transfers between devices: 28.9 us -> 26.6 us  [move(): return lax.ppermute(value, EVERY, pairs)]
  transfers between devices with their start and end apart: 21 -> 14, of which waited for: 8 -> 7; matrix products, arithmetic and copies ran while one was open for 16% -> 20% of each run, Pallas kernels for 0% -> 0%
where the time goes in v3:
time: 144 us; the launch traced here: 143 us
  waiting for transfers between devices  47.9 us (33%)
  starting transfers between devices  46.2 us (32%)
  matrix products  26.6 us (18%)
  local copies, waits for them, and re-layouts  15.8 us (11%)
  other arithmetic  5.41 us (4%)
    all_to_all x3, waiting for transfers between devices, to_every(): lax.all_to_all(jnp.broadcast_to(values[None], (count, *values.shape)), EV...  31.5 us
    ppermute x11, starting transfers between devices, move(): return lax.ppermute(value, EVERY, pairs)  26.6 us
    all_to_all x3, starting transfers between devices, to_every(): lax.all_to_all(jnp.broadcast_to(values[None], (count, *values.shape)), EV...  19.6 us
    dot_general x8, matrix products, chunk_logits(): lax.dot_general(centroids, chunk, (((1,), (1,)), ((), ())), preferred_ele...  16.9 us
    ppermute x11, waiting for transfers between devices, move(): return lax.ppermute(value, EVERY, pairs)  16.4 us
    unnamed x34, local copies, waits for them, and re-layouts  11.6 us
    dot_general x1, matrix products, body(): lax.dot_general(weight, jnp.concatenate(chunks, axis=0), (((1,), (0,)), (...  9.69 us
  transfers between devices with their start and end apart: 14, of which 7 were waited for; matrix products, arithmetic and copies ran while one was open for 20% of the time, Pallas kernels for 0%

profile of v3, /device:TPU:1, one launch (start us, length us, event | category | flops | bytes accessed | tf_op | source)
XLA Modules:
  0.0 143.1 jit_solution(1978598773363283822)
XLA Ops:
  0.6 6.3 %collective-permute-start = (bf16[32,4096]{1,0:T(8,128)(2,1)}, bf16[32,4096]{1,0:T(8,128)(2,1)S(1)}, u32[]{:S(2)}, u32[]{:S(2)}) collective-permute-start(bf16[32,4096]{1,0:T(8,128)(2,1)} %param.3), channel_id=1, source_target_pairs={{1,16},{3,18},{5,20},{7,22},{9,24},{11,26},{13,28},{15,30},{16,1},... | collective-permute-start | bytes 786440 | tf_op jit(solution)/shard_map/ppermute | solution.py:31
  7.0 2.3 %collective-permute-start.1 = (bf16[32,4096]{1,0:T(8,128)(2,1)}, bf16[32,4096]{1,0:T(8,128)(2,1)S(1)}, u32[]{:S(2)}, u32[]{:S(2)}) collective-permute-start(bf16[32,4096]{1,0:T(8,128)(2,1)} %param.3), channel_id=1, source_target_pairs={{0,12},{1,28},{2,14},{3,30},{4,0},{5,16},{6,2},{7,18},{8,4},{9,20}... | collective-permute-start | bytes 786440 | tf_op jit(solution)/shard_map/ppermute | solution.py:31
  9.3 7.0 %collective-permute-start.2 = (bf16[32,4096]{1,0:T(8,128)(2,1)}, bf16[32,4096]{1,0:T(8,128)(2,1)S(1)}, u32[]{:S(2)}, u32[]{:S(2)}) collective-permute-start(bf16[32,4096]{1,0:T(8,128)(2,1)} %param.3), channel_id=1, source_target_pairs={{0,8},{1,24},{2,10},{3,26},{4,12},{5,28},{6,14},{7,30},{8,0},{9,16... | collective-permute-start | bytes 786440 | tf_op jit(solution)/shard_map/ppermute | solution.py:31
  16.4 3.9 %collective-permute-done.2 = bf16[32,4096]{1,0:T(8,128)(2,1)S(1)} collective-permute-done((bf16[32,4096]{1,0:T(8,128)(2,1)}, bf16[32,4096]{1,0:T(8,128)(2,1)S(1)}, u32[]{:S(2)}, u32[]{:S(2)}) %collective-permute-start.2) | collective-permute-done | bytes 262176 | tf_op jit(solution)/shard_map/ppermute | solution.py:31
  20.3 5.6 %collective-permute-done.3 = bf16[32,4096]{1,0:T(8,128)(2,1)S(1)} collective-permute-done((bf16[32,4096]{1,0:T(8,128)(2,1)}, bf16[32,4096]{1,0:T(8,128)(2,1)S(1)}, u32[]{:S(2)}, u32[]{:S(2)}) %collective-permute-start.3) | collective-permute-done | bytes 262176 | tf_op jit(solution)/shard_map/ppermute | solution.py:31
  27.1 1.9 %collective-permute-start.5 = (bf16[128,4096]{1,0:T(8,128)(2,1)S(1)}, bf16[128,4096]{1,0:T(8,128)(2,1)}, u32[]{:S(2)}, u32[]{:S(2)}) collective-permute-start(bf16[128,4096]{1,0:T(8,128)(2,1)S(1)} %bitcast.107), channel_id=1, source_target_pairs={{0,64},{1,9},{2,66},{3,11},{4,68},{5,13},{6,70},{7,15},{8,72},{9,1... | collective-permute-start | bytes 3145736 | tf_op jit(solution)/shard_map/ppermute | solution.py:31
  30.0 3.7 %fusion.17 = f32[512,1024]{0,1:T(8,128)S(1)} fusion(bf16[128,4096]{1,0:T(8,128)(2,1)S(1)} %bitcast.111, bf16[512,4096]{1,0:T(8,128)(2,1)} %param.4), kind=kOutput, calls=%fused_computation.34 | convolution fusion | flops 536936448 | bytes 5505024 | tf_op jit(solution)/shard_map/dot_general | solution.py:87
  33.8 6.5 %collective-permute-done.4 = bf16[128,4096]{1,0:T(8,128)(2,1)} collective-permute-done((bf16[128,4096]{1,0:T(8,128)(2,1)S(1)}, bf16[128,4096]{1,0:T(8,128)(2,1)}, u32[]{:S(2)}, u32[]{:S(2)}) %collective-permute-start.4) | collective-permute-done | bytes 1048608 | tf_op jit(solution)/shard_map/ppermute | solution.py:31
  40.3 8.0 %collective-permute-start.8 = (bf16[128,4096]{1,0:T(8,128)(2,1)}, bf16[128,4096]{1,0:T(8,128)(2,1)S(1)}, u32[]{:S(2)}, u32[]{:S(2)}) collective-permute-start(bf16[128,4096]{1,0:T(8,128)(2,1)} %collective-permute-done.4), channel_id=1, source_target_pairs={{0,1},{1,0},{2,3},{3,2},{4,5},{5,4},{6,7},{7,6},{8,9},{9,8},{10,11... | collective-permute-start | bytes 3145736 | tf_op jit(solution)/shard_map/ppermute | solution.py:31
  48.3 2.5 %constant_dynamic-update-slice_fusion.6 = bf16[1024,4096]{1,0:T(8,128)(2,1)} fusion(bf16[1024,4096]{1,0:T(8,128)(2,1)} %constant_dynamic-update-slice_fusion.7, bf16[128,4096]{1,0:T(8,128)(2,1)} %collective-permute-done.4), kind=kLoop, calls=%fused_computation.55 | loop fusion | bytes 2097152
  50.8 2.3 %constant_dynamic-update-slice_fusion.5 = bf16[1024,4096]{1,0:T(8,128)(2,1)} fusion(bf16[1024,4096]{1,0:T(8,128)(2,1)} %constant_dynamic-update-slice_fusion.6, bf16[128,4096]{1,0:T(8,128)(2,1)} %collective-permute-done.5), kind=kLoop, calls=%fused_computation.54 | loop fusion | bytes 2097152
  54.7 2.8 %fusion.15 = f32[512,1024]{0,1:T(8,128)S(1)} fusion(f32[512,1024]{0,1:T(8,128)S(1)} %fusion.17, bf16[128,4096]{1,0:T(8,128)(2,1)} %collective-permute-done.4, bf16[512,4096]{1,0:T(8,128)(2,1)S(1)} %copy-done), kind=kOutput, calls=%fused_computation.31 | convolution fusion | flops 536936448 | bytes 5505024 | tf_op jit(solution)/shard_map/dot_general | solution.py:87
  57.4 2.8 %fusion.13 = f32[512,1024]{0,1:T(8,128)S(1)} fusion(f32[512,1024]{0,1:T(8,128)S(1)} %fusion.15, bf16[128,4096]{1,0:T(8,128)(2,1)} %collective-permute-done.5, bf16[512,4096]{1,0:T(8,128)(2,1)S(1)} %copy-done), kind=kOutput, calls=%fused_computation.28 | convolution fusion | flops 536936448 | bytes 5505024 | tf_op jit(solution)/shard_map/dot_general | solution.py:87
  60.2 1.5 %fusion.11 = f32[512,1024]{0,1:T(8,128)S(1)} fusion(f32[512,1024]{0,1:T(8,128)S(1)} %fusion.13, bf16[128,4096]{1,0:T(8,128)(2,1)S(1)} %collective-permute-done.6, bf16[512,4096]{1,0:T(8,128)(2,1)S(1)} %copy-done), kind=kOutput, calls=%fused_computation.25 | convolution fusion | flops 536936448 | bytes 5505024 | tf_op jit(solution)/shard_map/dot_general | solution.py:87
  66.5 1.5 %fusion.3 = f32[512,1024]{0,1:T(8,128)S(1)} fusion(f32[512,1024]{0,1:T(8,128)S(1)} %fusion.5, bf16[128,4096]{1,0:T(8,128)(2,1)S(1)} %collective-permute-done.10, bf16[512,4096]{1,0:T(8,128)(2,1)S(1)} %copy-done), kind=kOutput, calls=%fused_computation.13 | convolution fusion | flops 536936448 | bytes 5505024 | tf_op jit(solution)/shard_map/dot_general | solution.py:87
  69.7 11.8 %all-to-all-start = ((f32[128,8,128]{2,1,0:T(8,128)}), f32[128,8,128]{2,1,0:T(8,128)S(1)}, u32[]{:S(2)}, u32[]{:S(2)}) async-start(f32[128,8,128]{2,1,0:T(8,128)} %broadcast_in_dim.6), calls=%async_computation | async-start | bytes 1048576 | tf_op jit(solution)/shard_map/all_to_all | solution.py:47
  81.5 2.4 %constant_dynamic-update-slice_fusion.3 = bf16[1024,4096]{1,0:T(8,128)(2,1)} fusion(bf16[1024,4096]{1,0:T(8,128)(2,1)} %constant_dynamic-update-slice_fusion.4, bf16[128,4096]{1,0:T(8,128)(2,1)} %copy-done.6), kind=kLoop, calls=%fused_computation.52 | loop fusion | bytes 2097152
  85.0 10.6 %all-to-all-done = f32[128,8,128]{2,1,0:T(8,128)S(1)} async-done(((f32[128,8,128]{2,1,0:T(8,128)}), f32[128,8,128]{2,1,0:T(8,128)S(1)}, u32[]{:S(2)}, u32[]{:S(2)}) %all-to-all-start) | async-done | bytes 524320 | tf_op jit(solution)/shard_map/all_to_all | solution.py:47
  96.6 1.8 %fusion.34 = (bf16[1024]{0:T(1024)(128)(2,1)S(1)}, f32[512,1024]{0,1:T(8,128)}) fusion(f32[512]{0:T(512)S(1)} %fusion.1, f32[512]{0:T(512)S(1)} %add_reduce_fusion, f32[512,1024]{0,1:T(8,128)S(1)} %fusion.3, f32[1024]{0:T(1024)S(1)} %bitcast.114), kind=kLoop, calls=%fused_computation.121 | loop fusion | flops 2096128 | bytes 4204544 | tf_op jit(solution)/shard_map/reduce_sum | solution.py:118
  99.3 3.8 %all-to-all-start.1 = ((bf16[128,8,128]{2,1,0:T(8,128)(2,1)}), bf16[128,8,128]{2,1,0:T(8,128)(2,1)S(1)}, u32[]{:S(2)}, u32[]{:S(2)}) async-start(bf16[128,8,128]{2,1,0:T(8,128)(2,1)} %broadcast_in_dim.7), calls=%async_computation.1 | async-start | bytes 524288 | tf_op jit(solution)/shard_map/all_to_all | solution.py:47
  104.2 10.5 %all-to-all-done.1 = bf16[128,8,128]{2,1,0:T(8,128)(2,1)S(1)} async-done(((bf16[128,8,128]{2,1,0:T(8,128)(2,1)}), bf16[128,8,128]{2,1,0:T(8,128)(2,1)S(1)}, u32[]{:S(2)}, u32[]{:S(2)}) %all-to-all-start.1) | async-done | bytes 262176 | tf_op jit(solution)/shard_map/all_to_all | solution.py:47
  116.2 4.0 %all-to-all-start.2 = ((bf16[128,8,128]{2,1,0:T(8,128)(2,1)}), bf16[128,8,128]{2,1,0:T(8,128)(2,1)S(1)}, u32[]{:S(2)}, u32[]{:S(2)}) async-start(bf16[128,8,128]{2,1,0:T(8,128)(2,1)} %broadcast_in_dim.8), calls=%async_computation.2 | async-start | bytes 524288 | tf_op jit(solution)/shard_map/all_to_all | solution.py:47
  121.3 10.5 %all-to-all-done.2 = bf16[128,8,128]{2,1,0:T(8,128)(2,1)S(1)} async-done(((bf16[128,8,128]{2,1,0:T(8,128)(2,1)}), bf16[128,8,128]{2,1,0:T(8,128)(2,1)S(1)}, u32[]{:S(2)}, u32[]{:S(2)}) %all-to-all-start.2) | async-done | bytes 262176 | tf_op jit(solution)/shard_map/all_to_all | solution.py:47
  132.8 9.7 %convolution_convert_fusion = bf16[512,4096]{1,0:T(8,128)(2,1)} fusion(bf16[1024,4096]{1,0:T(8,128)(2,1)} %constant_dynamic-update-slice_fusion, f32[512,1024]{0,1:T(8,128)S(1)} %copy-done.1, f32[512]{0:T(512)S(1)} %multiply_reduce_fusion.2, f32[1024]{0:T(1024)S(1)} %bitcast.116), kind=kOutput, calls=%fused_computation | convolution fusion | flops 4298637312 | bytes 14686208 | tf_op jit(solution)/shard_map/dot_general | solution.py:125
  (109 shorter events, 18.2 us)
Async XLA Ops:
  0.6 25.3 %copy-start.9 = (bf16[32,4096]{1,0:T(8,128)(2,1)S(1)}, bf16[32,4096]{1,0:T(8,128)(2,1)}, u32[]{:S(2)}) copy-start(bf16[32,4096]{1,0:T(8,128)(2,1)} %param.3) | copy-start | bytes 786436
  0.6 15.6 %collective-permute-start = (bf16[32,4096]{1,0:T(8,128)(2,1)}, bf16[32,4096]{1,0:T(8,128)(2,1)S(1)}, u32[]{:S(2)}, u32[]{:S(2)}) collective-permute-start(bf16[32,4096]{1,0:T(8,128)(2,1)} %param.3), channel_id=1, source_target_pairs={{1,16},{3,18},{5,20},{7,22},{9,24},{11,26},{13,28},{15,30},{16,1},... | collective-permute-start | bytes 786440 | tf_op jit(solution)/shard_map/ppermute | solution.py:31
  7.0 9.3 %collective-permute-start.1 = (bf16[32,4096]{1,0:T(8,128)(2,1)}, bf16[32,4096]{1,0:T(8,128)(2,1)S(1)}, u32[]{:S(2)}, u32[]{:S(2)}) collective-permute-start(bf16[32,4096]{1,0:T(8,128)(2,1)} %param.3), channel_id=1, source_target_pairs={{0,12},{1,28},{2,14},{3,30},{4,0},{5,16},{6,2},{7,18},{8,4},{9,20}... | collective-permute-start | bytes 786440 | tf_op jit(solution)/shard_map/ppermute | solution.py:31
  9.3 11.0 %collective-permute-start.2 = (bf16[32,4096]{1,0:T(8,128)(2,1)}, bf16[32,4096]{1,0:T(8,128)(2,1)S(1)}, u32[]{:S(2)}, u32[]{:S(2)}) collective-permute-start(bf16[32,4096]{1,0:T(8,128)(2,1)} %param.3), channel_id=1, source_target_pairs={{0,8},{1,24},{2,10},{3,26},{4,12},{5,28},{6,14},{7,30},{8,0},{9,16... | collective-permute-start | bytes 786440 | tf_op jit(solution)/shard_map/ppermute | solution.py:31
  16.2 9.6 %collective-permute-start.3 = (bf16[32,4096]{1,0:T(8,128)(2,1)}, bf16[32,4096]{1,0:T(8,128)(2,1)S(1)}, u32[]{:S(2)}, u32[]{:S(2)}) collective-permute-start(bf16[32,4096]{1,0:T(8,128)(2,1)} %param.3), channel_id=1, source_target_pairs={{0,4},{1,20},{2,6},{3,22},{4,8},{5,24},{6,10},{7,26},{8,12},{9,28}... | collective-permute-start | bytes 786440 | tf_op jit(solution)/shard_map/ppermute | solution.py:31
  26.2 14.1 %collective-permute-start.4 = (bf16[128,4096]{1,0:T(8,128)(2,1)S(1)}, bf16[128,4096]{1,0:T(8,128)(2,1)}, u32[]{:S(2)}, u32[]{:S(2)}) collective-permute-start(bf16[128,4096]{1,0:T(8,128)(2,1)S(1)} %bitcast.106), channel_id=1, source_target_pairs={{0,96},{1,13},{2,98},{3,15},{4,100},{5,1},{6,102},{7,3},{8,104},{9... | collective-permute-start | bytes 3145736 | tf_op jit(solution)/shard_map/ppermute | solution.py:31
  27.1 21.2 %collective-permute-start.5 = (bf16[128,4096]{1,0:T(8,128)(2,1)S(1)}, bf16[128,4096]{1,0:T(8,128)(2,1)}, u32[]{:S(2)}, u32[]{:S(2)}) collective-permute-start(bf16[128,4096]{1,0:T(8,128)(2,1)S(1)} %bitcast.107), channel_id=1, source_target_pairs={{0,64},{1,9},{2,66},{3,11},{4,68},{5,13},{6,70},{7,15},{8,72},{9,1... | collective-permute-start | bytes 3145736 | tf_op jit(solution)/shard_map/ppermute | solution.py:31
  29.0 24.5 %collective-permute-start.6 = (bf16[128,4096]{1,0:T(8,128)(2,1)S(1)}, bf16[128,4096]{1,0:T(8,128)(2,1)S(1)}, u32[]{:S(2)}, u32[]{:S(2)}) collective-permute-start(bf16[128,4096]{1,0:T(8,128)(2,1)S(1)} %bitcast.108), channel_id=1, source_target_pairs={{0,32},{1,5},{2,34},{3,7},{4,36},{5,9},{6,38},{7,11},{8,40},{9,13}... | collective-permute-start | bytes 3145736 | tf_op jit(solution)/shard_map/ppermute | solution.py:31
  29.0 32.8 %collective-permute-start.7 = (bf16[128,4096]{1,0:T(8,128)(2,1)S(1)}, bf16[128,4096]{1,0:T(8,128)(2,1)S(1)}, u32[]{:S(2)}, u32[]{:S(2)}) collective-permute-start(bf16[128,4096]{1,0:T(8,128)(2,1)S(1)} %bitcast.109), channel_id=1, source_target_pairs={{0,1},{1,0},{2,3},{3,2},{4,5},{5,4},{6,7},{7,6},{8,9},{9,8},{10,11... | collective-permute-start | bytes 3145736 | tf_op jit(solution)/shard_map/ppermute | solution.py:31
  40.3 23.0 %collective-permute-start.8 = (bf16[128,4096]{1,0:T(8,128)(2,1)}, bf16[128,4096]{1,0:T(8,128)(2,1)S(1)}, u32[]{:S(2)}, u32[]{:S(2)}) collective-permute-start(bf16[128,4096]{1,0:T(8,128)(2,1)} %collective-permute-done.4), channel_id=1, source_target_pairs={{0,1},{1,0},{2,3},{3,2},{4,5},{5,4},{6,7},{7,6},{8,9},{9,8},{10,11... | collective-permute-start | bytes 3145736 | tf_op jit(solution)/shard_map/ppermute | solution.py:31
  48.3 16.6 %collective-permute-start.9 = (bf16[128,4096]{1,0:T(8,128)(2,1)}, bf16[128,4096]{1,0:T(8,128)(2,1)S(1)}, u32[]{:S(2)}, u32[]{:S(2)}) collective-permute-start(bf16[128,4096]{1,0:T(8,128)(2,1)} %collective-permute-done.5), channel_id=1, source_target_pairs={{0,1},{1,0},{2,3},{3,2},{4,5},{5,4},{6,7},{7,6},{8,9},{9,8},{10,11... | collective-permute-start | bytes 3145736 | tf_op jit(solution)/shard_map/ppermute | solution.py:31
  48.3 6.4 %copy-start = (bf16[512,4096]{1,0:T(8,128)(2,1)S(1)}, bf16[512,4096]{1,0:T(8,128)(2,1)}, u32[]{:S(2)}) copy-start(bf16[512,4096]{1,0:T(8,128)(2,1)} %param.4) | copy-start | bytes 12582916
  53.5 13.0 %collective-permute-start.10 = (bf16[128,4096]{1,0:T(8,128)(2,1)S(1)}, bf16[128,4096]{1,0:T(8,128)(2,1)S(1)}, u32[]{:S(2)}, u32[]{:S(2)}) collective-permute-start(bf16[128,4096]{1,0:T(8,128)(2,1)S(1)} %collective-permute-done.6), channel_id=1, source_target_pairs={{0,1},{1,0},{2,3},{3,2},{4,5},{5,4},{6,7},{7,6},{8,9},{9,8},{10,11... | collective-permute-start | bytes 3145736 | tf_op jit(solution)/shard_map/ppermute | solution.py:31
  61.8 4.7 %copy-start.6 = (bf16[128,4096]{1,0:T(8,128)(2,1)}, bf16[128,4096]{1,0:T(8,128)(2,1)S(1)}, u32[]{:S(2)}) copy-start(bf16[128,4096]{1,0:T(8,128)(2,1)S(1)} %collective-permute-done.7) | copy-start | bytes 3145732
  64.9 1.6 %copy-start.4 = (bf16[128,4096]{1,0:T(8,128)(2,1)}, bf16[128,4096]{1,0:T(8,128)(2,1)S(1)}, u32[]{:S(2)}) copy-start(bf16[128,4096]{1,0:T(8,128)(2,1)S(1)} %collective-permute-done.9) | copy-start | bytes 3145732
  66.5 1.6 %copy-start.10 = (f32[512]{0:T(512)S(1)}, f32[512]{0:T(512)}, u32[]{:S(2)}) copy-start(f32[512]{0:T(512)} %param.5) | copy-start | bytes 6148
  66.5 1.6 %copy-start.2 = (bf16[128,4096]{1,0:T(8,128)(2,1)}, bf16[128,4096]{1,0:T(8,128)(2,1)S(1)}, u32[]{:S(2)}) copy-start(bf16[128,4096]{1,0:T(8,128)(2,1)S(1)} %collective-permute-done.10) | copy-start | bytes 3145732
  69.7 25.8 %all-to-all-start = ((f32[128,8,128]{2,1,0:T(8,128)}), f32[128,8,128]{2,1,0:T(8,128)S(1)}, u32[]{:S(2)}, u32[]{:S(2)}) async-start(f32[128,8,128]{2,1,0:T(8,128)} %broadcast_in_dim.6), calls=%async_computation | async-start | bytes 1048576 | tf_op jit(solution)/shard_map/all_to_all | solution.py:47
  81.5 2.4 %copy-start.8 = (bf16[128,4096]{1,0:T(8,128)(2,1)S(1)}, bf16[128,4096]{1,0:T(8,128)(2,1)}, u32[]{:S(2)}) copy-start(bf16[128,4096]{1,0:T(8,128)(2,1)} %copy-done.7) | copy-start | bytes 3145732
  96.6 6.5 %copy-start.5 = (bf16[128,4096]{1,0:T(8,128)(2,1)S(1)}, bf16[128,4096]{1,0:T(8,128)(2,1)}, u32[]{:S(2)}) copy-start(bf16[128,4096]{1,0:T(8,128)(2,1)} %copy-done.4) | copy-start | bytes 3145732
  98.4 16.4 %copy-start.1 = (f32[512,1024]{0,1:T(8,128)S(1)}, f32[512,1024]{0,1:T(8,128)}, u32[]{:S(2)}) copy-start(f32[512,1024]{0,1:T(8,128)} %get-tuple-element.4) | copy-start | bytes 6291460
  99.3 15.3 %all-to-all-start.1 = ((bf16[128,8,128]{2,1,0:T(8,128)(2,1)}), bf16[128,8,128]{2,1,0:T(8,128)(2,1)S(1)}, u32[]{:S(2)}, u32[]{:S(2)}) async-start(bf16[128,8,128]{2,1,0:T(8,128)(2,1)} %broadcast_in_dim.7), calls=%async_computation.1 | async-start | bytes 524288 | tf_op jit(solution)/shard_map/all_to_all | solution.py:47
  114.9 5.3 %copy-start.3 = (bf16[128,4096]{1,0:T(8,128)(2,1)S(1)}, bf16[128,4096]{1,0:T(8,128)(2,1)}, u32[]{:S(2)}) copy-start(bf16[128,4096]{1,0:T(8,128)(2,1)} %copy-done.2) | copy-start | bytes 3145732
  116.2 15.6 %all-to-all-start.2 = ((bf16[128,8,128]{2,1,0:T(8,128)(2,1)}), bf16[128,8,128]{2,1,0:T(8,128)(2,1)S(1)}, u32[]{:S(2)}, u32[]{:S(2)}) async-start(bf16[128,8,128]{2,1,0:T(8,128)(2,1)} %broadcast_in_dim.8), calls=%async_computation.2 | async-start | bytes 524288 | tf_op jit(solution)/shard_map/all_to_all | solution.py:47
  (1 other events, 1.5 us)

commit v4 on v3

v4 whole, which is shorter than its diff:
```python
import functools
import math

import jax
import jax.numpy as jnp
from jax import lax
from jax.experimental import pallas as pl
from jax.experimental.pallas import tpu as pltpu
from jax.sharding import PartitionSpec as P

CENTROIDS = 65536
PASSAGES = 1024
EVERY = ("psg", "cen")
X, Z, HALVES = 4, 4, 2
CHUNKS = 8
SLOTS = (0, 4, 2, 1, 3, 7, 6, 5)
LANES = 128
WIDTH = 1024


def coords(device):
    return (
        device // (HALVES * X * 4),
        device // (X * 4) % HALVES,
        device // 4 % X,
        device // 2 % 2,
        device % 2,
    )


def move(value, target):
    pairs = []
    for device in range(Z * HALVES * X * 4):
        there = target(*coords(device))
        if there is not None:
            z, h, x, l, c = there
            pairs.append((device, (((z % Z) * HALVES + h) * X + x % X) * 4 + l * 2 + c))
    return lax.ppermute(value, EVERY, pairs)


def along_second(value, step):
    return move(
        value,
        lambda z, h, x, l, c: (z + step, h, x, l, c) if c == 0 else (z, h, x + step, l, c),
    )


def to_sibling(value):
    return move(value, lambda z, h, x, l, c: (z, h, x, l, 1 - c))


def to_every(copies):
    return lax.all_to_all(copies, EVERY, 0, 0)


def turned(rows, places):
    return lax.dynamic_slice_in_dim(jnp.concatenate([rows, rows], 0), 4 - places, 4, 0)


def pair_kernel(factor, order_ref, duals_ref, centroids_ref, left_ref, right_ref, *refs):
    earlier, refs = refs[:-5], refs[-5:]
    logits_ref, out_ref, kept_ref, rows_ref, sem = refs
    span = left_ref.shape[0]
    total = lax.dot_general(
        centroids_ref[...],
        jnp.concatenate([left_ref[...], right_ref[...]], axis=0),
        (((1,), (1,)), ((), ())),
        preferred_element_type=jnp.float32,
    )
    for side in range(2):
        kept_ref[side] = factor * total[:, side * span : (side + 1) * span]
    copy_out = pltpu.make_async_copy(kept_ref, logits_ref, sem)
    copy_out.start()
    first = 2 * len(earlier)
    for side in range(2):
        shifted = kept_ref[side] + duals_ref[...]
        top = jnp.max(shifted, axis=0, keepdims=True)
        logsum = top + jnp.log(jnp.sum(jnp.exp(shifted - top), axis=0, keepdims=True))
        if earlier:
            rows_ref[pl.ds(order_ref[first + side], 1), :] = logsum
        else:
            out_ref[side : side + 1, :] = logsum
    if earlier:
        for pair, ref in enumerate(earlier):
            for side in range(2):
                rows_ref[pl.ds(order_ref[2 * pair + side], 1), :] = ref[side : side + 1, :]
        send_sums(rows_ref, out_ref)
    copy_out.wait()


def pair_logits(factor, order, duals, centroids, left, right, earlier=()):
    count, depth = centroids.shape
    span = left.shape[0]
    devices = lax.axis_size(EVERY)
    f32 = jnp.float32
    if earlier:
        out_spec = pl.BlockSpec((devices, CHUNKS, span), lambda: (0, 0, 0))
        out = jax.ShapeDtypeStruct((devices, CHUNKS, span), f32)
    else:
        out_spec, out = VMEM, jax.ShapeDtypeStruct((2, span), f32)
    return pl.pallas_call(
        functools.partial(pair_kernel, factor),
        in_specs=[SMEM] + [VMEM] * (4 + len(earlier)),
        out_specs=[ANY, out_spec],
        out_shape=[jax.ShapeDtypeStruct((2, count, span), f32), out],
        scratch_shapes=[
            pltpu.VMEM((2, count, span), f32),
            pltpu.VMEM((CHUNKS, span), f32),
            pltpu.SemaphoreType.DMA,
        ],
        cost_estimate=pl.CostEstimate(flops=1, bytes_accessed=1, transcendentals=0),
        compiler_params=LIMIT,
    )(order, duals, centroids, left, right, *earlier)


def send_sums(sums_ref, out_ref):
    out_ref[...] = jnp.broadcast_to(sums_ref[...].astype(out_ref.dtype)[None], out_ref.shape)


def first_kernel(order_ref, parts_ref, *refs):
    pairs = CHUNKS // 2
    kernel_ref, passage_ref, centroid_ref, out_ref, sums_ref, sems = refs[pairs:]
    copies = [
        pltpu.make_async_copy(ref, kernel_ref.at[pl.ds(2 * pair, 2)], sems.at[pair])
        for pair, ref in enumerate(refs[:pairs])
    ]
    for copy in copies:
        copy.start()
    parts = parts_ref[...]
    top = jnp.max(parts, axis=0)
    passage_ref[...] = -math.log(PASSAGES) - (
        top + jnp.log(jnp.sum(jnp.exp(parts - top[None]), axis=0))
    )
    peak = None
    for k in range(CHUNKS):
        if k % 2 == 0:
            copies[k // 2].wait()
        terms = kernel_ref[k] + passage_ref[pl.ds(order_ref[k], 1), :]
        kernel_ref[k] = terms
        peak = terms if peak is None else jnp.maximum(peak, terms)
    peak = jnp.max(peak, axis=1, keepdims=True)
    total = None
    for k in range(CHUNKS):
        terms = jnp.exp(kernel_ref[k] - peak)
        kernel_ref[k] = terms
        total = terms if total is None else total + terms
    total = jnp.sum(total, axis=1, keepdims=True)
    centroid_ref[...] = -math.log(CENTROIDS) - (peak + jnp.log(total))
    inverse = 1.0 / total
    for k in range(CHUNKS):
        terms = kernel_ref[k] * inverse
        kernel_ref[k] = terms
        sums_ref[pl.ds(order_ref[k], 1), :] = jnp.sum(terms, axis=0, keepdims=True)
    send_sums(sums_ref, out_ref)


def row_scale_of(parts_ref):
    parts = parts_ref[...].astype(jnp.float32)
    return (CENTROIDS / PASSAGES) / jnp.sum(parts, axis=0)


def column_sums(order_ref, kernel_ref, scale_ref):
    total = None
    for k in range(CHUNKS):
        terms = kernel_ref[k] * scale_ref[pl.ds(order_ref[k], 1), :]
        total = terms if total is None else total + terms
    return jnp.sum(total, axis=1, keepdims=True)


def middle_kernel(order_ref, parts_ref, kernel_ref, out_ref, sums_ref):
    sums_ref[...] = row_scale_of(parts_ref)
    scale = 1.0 / column_sums(order_ref, kernel_ref, sums_ref)
    for k in range(CHUNKS):
        sums_ref[pl.ds(order_ref[k], 1), :] = jnp.sum(
            kernel_ref[k] * scale, axis=0, keepdims=True
        )
    send_sums(sums_ref, out_ref)


def last_kernel(order_ref, parts_ref, kernel_ref, passage_ref, centroid_ref, *refs):
    chunk_refs = refs[:CHUNKS]
    new_ref, own_ref, duals_ref, weight_ref, held_ref, tile_ref, scale_ref, sems, out_sems = refs[CHUNKS:]
    span = chunk_refs[0].shape[0]
    tiles = held_ref.shape[0]
    for tile in range(tiles):
        for k in range(CHUNKS):
            pltpu.make_async_copy(
                chunk_refs[k].at[:, pl.ds(tile * WIDTH, WIDTH)],
                held_ref.at[tile, pl.ds(k * span, span), :],
                sems.at[tile],
            ).start()

    scale_ref[...] = row_scale_of(parts_ref)
    total = column_sums(order_ref, kernel_ref, scale_ref)
    inverse = 1.0 / total
    for k in range(CHUNKS):
        weight_ref[:, k * span : (k + 1) * span] = (
            kernel_ref[k] * scale_ref[pl.ds(order_ref[k], 1), :] * inverse
        ).astype(weight_ref.dtype)

    duals = centroid_ref[...] - jnp.log(total)
    square = (LANES, LANES)
    diagonal = lax.broadcasted_iota(jnp.int32, square, 0) == lax.broadcasted_iota(
        jnp.int32, square, 1
    )
    for k in range(duals.shape[0] // LANES):
        column = jnp.broadcast_to(duals[k * LANES : (k + 1) * LANES], square)
        duals_ref[pl.ds(k, 1), :] = jnp.sum(
            jnp.where(diagonal, column, 0.0), axis=0, keepdims=True
        )
    scale_ref[...] = passage_ref[...] + jnp.log(scale_ref[...])
    own_ref[...] = pltpu.roll(
        scale_ref[pl.ds(order_ref[CHUNKS], 1), :], LANES - order_ref[CHUNKS + 1], 1
    )

    def copy_out(tile):
        return pltpu.make_async_copy(
            tile_ref.at[tile % 2], new_ref.at[:, pl.ds(tile * WIDTH, WIDTH)], out_sems.at[tile % 2]
        )

    for tile in range(tiles):
        pltpu.make_async_copy(held_ref.at[tile], held_ref.at[tile], sems.at[tile]).wait()
        block = jnp.dot(
            weight_ref[...], held_ref[tile], preferred_element_type=jnp.float32
        ).astype(new_ref.dtype)
        if tile >= 2:
            copy_out(tile - 2).wait()
        tile_ref[tile % 2] = block
        copy_out(tile).start()
    for tile in range(tiles - 2, tiles):
        copy_out(tile).wait()


SMEM = pl.BlockSpec(memory_space=pltpu.SMEM)
VMEM = pl.BlockSpec(memory_space=pltpu.VMEM)
ANY = pl.BlockSpec(memory_space=pl.ANY)
LIMIT = pltpu.CompilerParams(vmem_limit_bytes=16 * 2**20)


def body(passages, centroids, dual_init):
    depth = passages.shape[1]
    local_rows = passages.shape[0]
    count = centroids.shape[0]
    factor = 4.0 / math.sqrt(depth)
    devices = lax.axis_size(EVERY)
    z, h, x, _, c = coords(lax.axis_index(EVERY))
    first = jnp.where(c == 0, x, z)
    second = jnp.where(c == 0, z, x)

    def fetch(step):
        def target(z, h, x, l, c):
            stays = h == c
            if stays and step == 0:
                return None
            h, c = (h, c) if stays else (1 - h, 1 - c)
            return (z, h, x - step, l, c) if c == 0 else (z - step, h, x, l, c)

        return move(passages, target)

    ring = [jnp.where(h == c, passages, fetch(0)), fetch(1), fetch(2), fetch(3)]
    ring = turned(jnp.stack(ring), first).reshape(4 * local_rows, depth)
    own = [ring, along_second(ring, -1), along_second(ring, 2), along_second(ring, 1)]
    order = [c * 4 + (second + k) % 4 for k in range(4)]
    order += [(1 - c) * 4 + (first + k) % 4 for k in range(4)]
    order = [order[k] for k in SLOTS]
    row, lane = jnp.where(h == 0, z, 4 + x), jnp.where(h == 0, x, z) * local_rows
    order = jnp.stack(order + [row, lane]).astype(jnp.int32)

    logits_of = functools.partial(
        pair_logits, factor, order, dual_init.reshape(count, 1), centroids
    )
    sibling = [None] * 4
    sibling[0] = to_sibling(own[0])
    pairs = [logits_of(own[0], sibling[0])]
    own[1], own[2], own[3], _ = lax.optimization_barrier((own[1], own[2], own[3], pairs[0]))
    sibling[3] = to_sibling(own[3])
    sibling[2] = to_sibling(own[2])
    sibling[1] = to_sibling(own[1])
    pairs.append(logits_of(own[2], own[1]))
    sibling[3], sibling[2], _ = lax.optimization_barrier((sibling[3], sibling[2], pairs[1]))
    pairs.append(logits_of(own[3], sibling[3]))
    sibling[1], sibling[2], _ = lax.optimization_barrier((sibling[1], sibling[2], pairs[2]))
    pairs.append(logits_of(sibling[2], sibling[1], [logsum for _, logsum in pairs]))
    chunks = own + sibling
    chunks = [chunks[k] for k in SLOTS]
    logits = [pair[0] for pair in pairs]
    span = chunks[0].shape[0]
    f32 = jnp.float32
    parts = to_every(pairs[-1][1])

    sent = jax.ShapeDtypeStruct((devices, CHUNKS, span), jnp.bfloat16)
    block = pl.BlockSpec((devices, CHUNKS, span), lambda: (0, 0, 0))
    sums = pltpu.VMEM((CHUNKS, span), f32)
    kernel, passage_first, centroid_first, partial = pl.pallas_call(
        first_kernel,
        in_specs=[SMEM, VMEM] + [ANY] * len(logits),
        out_specs=[VMEM] * 3 + [block],
        out_shape=[
            jax.ShapeDtypeStruct((CHUNKS, count, span), f32),
            jax.ShapeDtypeStruct((CHUNKS, span), f32),
            jax.ShapeDtypeStruct((count, 1), f32),
            sent,
        ],
        scratch_shapes=[sums, pltpu.SemaphoreType.DMA((len(logits),))],
        compiler_params=LIMIT,
    )(order, parts, *logits)
    partial = pl.pallas_call(
        middle_kernel,
        in_specs=[SMEM, VMEM, VMEM],
        out_specs=block,
        out_shape=sent,
        scratch_shapes=[sums],
        compiler_params=LIMIT,
    )(order, to_every(partial), kernel)
    new_centroids, own_duals, centroid_duals = pl.pallas_call(
        last_kernel,
        in_specs=[SMEM] + [VMEM] * 4 + [ANY] * CHUNKS,
        out_specs=[ANY, VMEM, VMEM],
        out_shape=[
            jax.ShapeDtypeStruct((count, depth), jnp.bfloat16),
            jax.ShapeDtypeStruct((1, span), f32),
            jax.ShapeDtypeStruct((count // LANES, LANES), f32),
        ],
        scratch_shapes=[
            pltpu.VMEM((count, CHUNKS * span), jnp.bfloat16),
            pltpu.VMEM((depth // WIDTH, CHUNKS * span, WIDTH), jnp.bfloat16),
            pltpu.VMEM((2, count, WIDTH), jnp.bfloat16),
            sums,
            pltpu.SemaphoreType.DMA((depth // WIDTH,)),
            pltpu.SemaphoreType.DMA((2,)),
        ],
        compiler_params=pltpu.CompilerParams(vmem_limit_bytes=24 * 2**20),
    )(order, to_every(partial), kernel, passage_first, centroid_first, *chunks)
    own_duals = own_duals[0, :local_rows]
    return (new_centroids, own_duals, centroid_duals.reshape(count))


def solution(mesh):
    in_specs = (P("psg", None), P(("psg", "cen"), None), P(("psg", "cen")))
    out_specs = (P(("psg", "cen"), None), P("psg"), P(("psg", "cen")))
    return jax.shard_map(body, mesh=mesh, in_specs=in_specs, out_specs=out_specs, check_vma=False)
```

time: 144 us -> 126 us (0.88)
  blocking collectives: 0 us -> 51.1 us
  matrix products: 26.6 us -> 0 us
  starting transfers between devices: 46.2 us -> 22.3 us
  waiting for transfers between devices: 47.9 us -> 26.4 us
  Pallas kernels: 0 us -> 21.4 us
  local copies, waits for them, and re-layouts: 15.8 us -> 3.16 us
  other arithmetic: 5.41 us -> 0.13 us
    all_to_all x0 -> x3, blocking collectives: none -> 51.1 us  [to_every(): return lax.all_to_all(copies, EVERY, 0, 0)]
    all_to_all x3 -> x0, waiting for transfers between devices: 31.5 us -> none  [to_every(): lax.all_to_all(jnp.broadcast_to(values[None], (count, *values.shape)), EV...]
    dot_general x9 -> x0, matrix products: 26.6 us -> none  [the longest x8 16.9 us: chunk_logits(): lax.dot_general(centroids, chunk, (((1,), (1,)), ((), ())), preferred_ele...]
    pallas_call x0 -> x7, Pallas kernels: none -> 21.4 us  [the longest x4 9.91 us: pair_logits(): pl.pallas_call(functools.partial(pair_kernel, factor), in_specs=[SMEM] +...]
    all_to_all x3 -> x0, starting transfers between devices: 19.6 us -> none  [to_every(): lax.all_to_all(jnp.broadcast_to(values[None], (count, *values.shape)), EV...]
    ppermute x11, waiting for transfers between devices: 16.4 us -> 26.4 us  [move(): return lax.ppermute(value, EVERY, pairs)]
    unnamed x34 -> x11, local copies, waits for them, and re-layouts: 11.6 us -> 2.29 us
    ppermute x11, starting transfers between devices: 26.6 us -> 22.3 us  [move(): return lax.ppermute(value, EVERY, pairs)]
  transfers between devices with their start and end apart: 14 -> 11, of which waited for: 7 -> 5; matrix products, arithmetic and copies ran while one was open for 20% -> 0% of each run, Pallas kernels for 0% -> 6%
where the time goes in v4:
time: 126 us; the launch traced here: 125 us
  blocking collectives  51.1 us (41%)
  waiting for transfers between devices  26.4 us (21%)
  starting transfers between devices  22.3 us (18%)
  Pallas kernels  21.4 us (17%)
  local copies, waits for them, and re-layouts  3.16 us (3%)
    all_to_all x3, blocking collectives, to_every(): return lax.all_to_all(copies, EVERY, 0, 0)  51.1 us
    ppermute x11, waiting for transfers between devices, move(): return lax.ppermute(value, EVERY, pairs)  26.4 us
    ppermute x11, starting transfers between devices, move(): return lax.ppermute(value, EVERY, pairs)  22.3 us
    pallas_call x4, Pallas kernels, pair_logits(): pl.pallas_call(functools.partial(pair_kernel, factor), in_specs=[SMEM] +...  9.91 us
    pallas_call x1, Pallas kernels, body(): pl.pallas_call(last_kernel, in_specs=[SMEM] + [VMEM] * 4 + [ANY] * CHUNKS...  8.63 us
  transfers between devices with their start and end apart: 11, of which 5 were waited for; matrix products, arithmetic and copies ran while one was open for 0% of the time, Pallas kernels for 6%

profile of v4, /device:TPU:1, one launch (start us, length us, event | category | flops | bytes accessed | tf_op | source)
XLA Modules:
  0.0 125.5 jit_solution(11643008146942137869)
XLA Ops:
  0.6 6.3 %collective-permute-start = (bf16[32,4096]{1,0:T(8,128)(2,1)}, bf16[32,4096]{1,0:T(8,128)(2,1)S(1)}, u32[]{:S(2)}, u32[]{:S(2)}) collective-permute-start(bf16[32,4096]{1,0:T(8,128)(2,1)} %param.3), channel_id=1, source_target_pairs={{1,16},{3,18},{5,20},{7,22},{9,24},{11,26},{13,28},{15,30},{16,1},... | collective-permute-start | bytes 786440 | tf_op jit(solution)/shard_map/ppermute | solution.py:38
  7.0 2.3 %collective-permute-start.1 = (bf16[32,4096]{1,0:T(8,128)(2,1)}, bf16[32,4096]{1,0:T(8,128)(2,1)S(1)}, u32[]{:S(2)}, u32[]{:S(2)}) collective-permute-start(bf16[32,4096]{1,0:T(8,128)(2,1)} %param.3), channel_id=1, source_target_pairs={{0,12},{1,28},{2,14},{3,30},{4,0},{5,16},{6,2},{7,18},{8,4},{9,20}... | collective-permute-start | bytes 786440 | tf_op jit(solution)/shard_map/ppermute | solution.py:38
  9.3 5.4 %collective-permute-start.3 = (bf16[32,4096]{1,0:T(8,128)(2,1)}, bf16[32,4096]{1,0:T(8,128)(2,1)S(1)}, u32[]{:S(2)}, u32[]{:S(2)}) collective-permute-start(bf16[32,4096]{1,0:T(8,128)(2,1)} %param.3), channel_id=1, source_target_pairs={{0,4},{1,20},{2,6},{3,22},{4,8},{5,24},{6,10},{7,26},{8,12},{9,28}... | collective-permute-start | bytes 786440 | tf_op jit(solution)/shard_map/ppermute | solution.py:38
  14.7 1.5 %collective-permute-start.2 = (bf16[32,4096]{1,0:T(8,128)(2,1)}, bf16[32,4096]{1,0:T(8,128)(2,1)S(1)}, u32[]{:S(2)}, u32[]{:S(2)}) collective-permute-start(bf16[32,4096]{1,0:T(8,128)(2,1)} %param.3), channel_id=1, source_target_pairs={{0,8},{1,24},{2,10},{3,26},{4,12},{5,28},{6,14},{7,30},{8,0},{9,16... | collective-permute-start | bytes 786440 | tf_op jit(solution)/shard_map/ppermute | solution.py:38
  16.4 8.3 %collective-permute-done.2 = bf16[32,4096]{1,0:T(8,128)(2,1)S(1)} collective-permute-done((bf16[32,4096]{1,0:T(8,128)(2,1)}, bf16[32,4096]{1,0:T(8,128)(2,1)S(1)}, u32[]{:S(2)}, u32[]{:S(2)}) %collective-permute-start.2) | collective-permute-done | bytes 262176 | tf_op jit(solution)/shard_map/ppermute | solution.py:38
  25.1 1.3 %collective-permute-start.6 = (bf16[128,4096]{1,0:T(8,128)(2,1)S(1)}, bf16[128,4096]{1,0:T(8,128)(2,1)S(1)}, u32[]{:S(2)}, u32[]{:S(2)}) collective-permute-start(bf16[128,4096]{1,0:T(8,128)(2,1)S(1)} %bitcast.28), channel_id=1, source_target_pairs={{0,32},{1,5},{2,34},{3,7},{4,36},{5,9},{6,38},{7,11},{8,40},{9,13}... | collective-permute-start | bytes 3145736 | tf_op jit(solution)/shard_map/ppermute | solution.py:38
  26.3 1.4 %collective-permute-start.5 = (bf16[128,4096]{1,0:T(8,128)(2,1)S(1)}, bf16[128,4096]{1,0:T(8,128)(2,1)}, u32[]{:S(2)}, u32[]{:S(2)}) collective-permute-start(bf16[128,4096]{1,0:T(8,128)(2,1)S(1)} %bitcast.29), channel_id=1, source_target_pairs={{0,64},{1,9},{2,66},{3,11},{4,68},{5,13},{6,70},{7,15},{8,72},{9,1... | collective-permute-start | bytes 3145736 | tf_op jit(solution)/shard_map/ppermute | solution.py:38
  27.8 1.9 %collective-permute-start.4 = (bf16[128,4096]{1,0:T(8,128)(2,1)S(1)}, bf16[128,4096]{1,0:T(8,128)(2,1)}, u32[]{:S(2)}, u32[]{:S(2)}) collective-permute-start(bf16[128,4096]{1,0:T(8,128)(2,1)S(1)} %bitcast.30), channel_id=1, source_target_pairs={{0,96},{1,13},{2,98},{3,15},{4,100},{5,1},{6,102},{7,3},{8,104},{9... | collective-permute-start | bytes 3145736 | tf_op jit(solution)/shard_map/ppermute | solution.py:38
  29.9 2.2 %copy-done = bf16[512,4096]{1,0:T(8,128)(2,1)S(1)} copy-done((bf16[512,4096]{1,0:T(8,128)(2,1)S(1)}, bf16[512,4096]{1,0:T(8,128)(2,1)}, u32[]{:S(2)}) %copy-start) | copy-done | bytes 4194328
  32.1 2.2 %shard_map.58 = (f32[2,512,128]{2,1,0:T(8,128)S(1)}, f32[2,128]{1,0:T(2,128)S(1)}) custom-call(s32[10]{0:T(128)S(1)} %stack.56.order_ref, f32[512,1]{1,0:T(8,128)S(1)} %copy.9.duals_ref, bf16[512,4096]{1,0:T(8,128)(2,1)S(1)} %copy-done, bf16[128,4096]{1,0:T(8,128)(2,1)S(1)} %bitcast.31, bf16[128,4096]{1,0:T(8,128)(2,1)S(1)} %collective-permute-done.7.right_ref.refs_1_), custom_call_target="tpu_custom_call" | custom-call | flops 1 | bytes 1 | tf_op jit(solution)/shard_map/pallas_call | solution.py:101
  34.3 6.1 %collective-permute-done.6.left_ref.refs_4_ = bf16[128,4096]{1,0:T(8,128)(2,1)S(1)} collective-permute-done((bf16[128,4096]{1,0:T(8,128)(2,1)S(1)}, bf16[128,4096]{1,0:T(8,128)(2,1)S(1)}, u32[]{:S(2)}, u32[]{:S(2)}) %collective-permute-start.6) | collective-permute-done | bytes 1048608 | tf_op jit(solution)/shard_map/ppermute | solution.py:38
  40.4 10.9 %collective-permute-done.5.left_ref.refs_2_ = bf16[128,4096]{1,0:T(8,128)(2,1)} collective-permute-done((bf16[128,4096]{1,0:T(8,128)(2,1)S(1)}, bf16[128,4096]{1,0:T(8,128)(2,1)}, u32[]{:S(2)}, u32[]{:S(2)}) %collective-permute-start.5) | collective-permute-done | bytes 1048608 | tf_op jit(solution)/shard_map/ppermute | solution.py:38
  51.3 0.9 collective-permute-done.4.right_ref.refs_3_
  52.2 1.6 %collective-permute-start.9 = (bf16[128,4096]{1,0:T(8,128)(2,1)S(1)}, bf16[128,4096]{1,0:T(8,128)(2,1)S(1)}, u32[]{:S(2)}, u32[]{:S(2)}) collective-permute-start(bf16[128,4096]{1,0:T(8,128)(2,1)S(1)} %collective-permute-done.6.left_ref.refs_4_), channel_id=1, source_target_pairs={{0,1},{1,0},{2,3},{3,2},{4,5},{5,4},{6,7},{7,6},{8,9},{9,8},{10,11... | collective-permute-start | bytes 3145736 | tf_op jit(solution)/shard_map/ppermute | solution.py:38
  54.3 3.2 %shard_map.59 = (f32[2,512,128]{2,1,0:T(8,128)S(1)}, f32[2,128]{1,0:T(2,128)S(1)}) custom-call(s32[10]{0:T(128)S(1)} %stack.56.order_ref, f32[512,1]{1,0:T(8,128)S(1)} %copy.9.duals_ref, bf16[512,4096]{1,0:T(8,128)(2,1)S(1)} %copy-done, bf16[128,4096]{1,0:T(8,128)(2,1)} %collective-permute-done.5.left_ref.refs_2_, ...), custom_call_target="tpu_custom_call" | custom-call | flops 1 | bytes 1 | tf_op jit(solution)/shard_map/pallas_call | solution.py:101
  57.8 2.2 %shard_map.60 = (f32[2,512,128]{2,1,0:T(8,128)S(1)}, f32[2,128]{1,0:T(2,128)S(1)}) custom-call(s32[10]{0:T(128)S(1)} %stack.56.order_ref, f32[512,1]{1,0:T(8,128)S(1)} %copy.9.duals_ref, bf16[512,4096]{1,0:T(8,128)(2,1)S(1)} %copy-done, bf16[128,4096]{1,0:T(8,128)(2,1)S(1)} %collective-permute-done.6.left_ref.refs_4_, ...), custom_call_target="tpu_custom_call" | custom-call | flops 1 | bytes 1 | tf_op jit(solution)/shard_map/pallas_call | solution.py:101
  60.0 2.2 %shard_map.61 = (f32[2,512,128]{2,1,0:T(8,128)S(1)}, f32[128,8,128]{2,1,0:T(8,128)S(1)}) custom-call(s32[10]{0:T(128)S(1)} %stack.56.order_ref, f32[512,1]{1,0:T(8,128)S(1)} %copy.9.duals_ref, bf16[512,4096]{1,0:T(8,128)(2,1)S(1)} %copy-done, bf16[128,4096]{1,0:T(8,128)(2,1)S(1)} %collective-permute-done.10.left_ref.refs_6_, ...), custom_call_target="tpu_custom_call" | custom-call | flops 1 | bytes 1 | tf_op jit(solution)/shard_map/pallas_call | solution.py:101
  62.3 21.0 %all_to_all.15.parts_ref = f32[128,8,128]{2,1,0:T(8,128)S(1)} all-to-all(f32[128,8,128]{2,1,0:T(8,128)S(1)} %get-tuple-element.38), channel_id=1, replica_groups=mesh['psg'=32,'cen'=4] {'psg','cen'}, dimensions={0} | all-to-all | bytes 1048576 | tf_op jit(solution)/shard_map/all_to_all | solution.py:53
  83.3 1.9 %shard_map.62 = (f32[8,512,128]{2,1,0:T(8,128)S(1)}, f32[8,128]{1,0:T(8,128)S(1)}, f32[512,1]{1,0:T(8,128)S(1)}, bf16[128,8,128]{2,1,0:T(8,128)(2,1)S(1)}) custom-call(s32[10]{0:T(128)S(1)} %stack.56.order_ref, f32[128,8,128]{2,1,0:T(8,128)S(1)} %all_to_all.15.parts_ref, f32[2,512,128]{2,1,0:T(8,128)S(1)} %get-tuple-element.25.refs_0_, ...), custom_call_target="tpu_custom_call" | custom-call | tf_op jit(solution)/shard_map/pallas_call | solution.py:294
  85.2 15.0 %all_to_all.16.parts_ref = bf16[128,8,128]{2,1,0:T(8,128)(2,1)S(1)} all-to-all(bf16[128,8,128]{2,1,0:T(8,128)(2,1)S(1)} %get-tuple-element.40), channel_id=1, replica_groups=mesh['psg'=32,'cen'=4] {'psg','cen'}, dimensions={0} | all-to-all | bytes 524288 | tf_op jit(solution)/shard_map/all_to_all | solution.py:53
  100.2 1.0 shard_map.63
  101.2 15.2 %all_to_all.17.parts_ref = bf16[128,8,128]{2,1,0:T(8,128)(2,1)S(1)} all-to-all(bf16[128,8,128]{2,1,0:T(8,128)(2,1)S(1)} %shard_map.63), channel_id=1, replica_groups=mesh['psg'=32,'cen'=4] {'psg','cen'}, dimensions={0} | all-to-all | bytes 524288 | tf_op jit(solution)/shard_map/all_to_all | solution.py:53
  116.3 8.6 %shard_map.64 = (bf16[512,4096]{1,0:T(8,128)(2,1)}, f32[1,128]{1,0:T(1,128)S(1)}, f32[4,128]{1,0:T(4,128)}) custom-call(s32[10]{0:T(128)S(1)} %stack.56.order_ref, bf16[128,8,128]{2,1,0:T(8,128)(2,1)S(1)} %all_to_all.17.parts_ref, f32[8,512,128]{2,1,0:T(8,128)S(1)} %get-tuple-element.41.kernel_ref, f32[8,128]{1,0:T(8,128)S(1)} %get-tuple-element.42.passage_ref, ...), custom_call_target="tpu_custom_call" | custom-call | tf_op jit(solution)/shard_map/pallas_call | solution.py:315
  125.0 0.5 slice_bitcast_fusion
  (26 shorter events, 1.4 us)
Async XLA Ops:
  0.6 24.1 %copy-start.1 = (bf16[32,4096]{1,0:T(8,128)(2,1)S(1)}, bf16[32,4096]{1,0:T(8,128)(2,1)}, u32[]{:S(2)}) copy-start(bf16[32,4096]{1,0:T(8,128)(2,1)} %param.3) | copy-start | bytes 786436
  0.6 15.6 %collective-permute-start = (bf16[32,4096]{1,0:T(8,128)(2,1)}, bf16[32,4096]{1,0:T(8,128)(2,1)S(1)}, u32[]{:S(2)}, u32[]{:S(2)}) collective-permute-start(bf16[32,4096]{1,0:T(8,128)(2,1)} %param.3), channel_id=1, source_target_pairs={{1,16},{3,18},{5,20},{7,22},{9,24},{11,26},{13,28},{15,30},{16,1},... | collective-permute-start | bytes 786440 | tf_op jit(solution)/shard_map/ppermute | solution.py:38
  7.0 9.3 %collective-permute-start.1 = (bf16[32,4096]{1,0:T(8,128)(2,1)}, bf16[32,4096]{1,0:T(8,128)(2,1)S(1)}, u32[]{:S(2)}, u32[]{:S(2)}) collective-permute-start(bf16[32,4096]{1,0:T(8,128)(2,1)} %param.3), channel_id=1, source_target_pairs={{0,12},{1,28},{2,14},{3,30},{4,0},{5,16},{6,2},{7,18},{8,4},{9,20}... | collective-permute-start | bytes 786440 | tf_op jit(solution)/shard_map/ppermute | solution.py:38
  9.3 15.4 %collective-permute-start.3 = (bf16[32,4096]{1,0:T(8,128)(2,1)}, bf16[32,4096]{1,0:T(8,128)(2,1)S(1)}, u32[]{:S(2)}, u32[]{:S(2)}) collective-permute-start(bf16[32,4096]{1,0:T(8,128)(2,1)} %param.3), channel_id=1, source_target_pairs={{0,4},{1,20},{2,6},{3,22},{4,8},{5,24},{6,10},{7,26},{8,12},{9,28}... | collective-permute-start | bytes 786440 | tf_op jit(solution)/shard_map/ppermute | solution.py:38
  14.7 9.9 %collective-permute-start.2 = (bf16[32,4096]{1,0:T(8,128)(2,1)}, bf16[32,4096]{1,0:T(8,128)(2,1)S(1)}, u32[]{:S(2)}, u32[]{:S(2)}) collective-permute-start(bf16[32,4096]{1,0:T(8,128)(2,1)} %param.3), channel_id=1, source_target_pairs={{0,8},{1,24},{2,10},{3,26},{4,12},{5,28},{6,14},{7,30},{8,0},{9,16... | collective-permute-start | bytes 786440 | tf_op jit(solution)/shard_map/ppermute | solution.py:38
  24.8 4.9 %copy-start.2 = (f32[512]{0:T(512)S(1)}, f32[512]{0:T(512)}, u32[]{:S(2)}) copy-start(f32[512]{0:T(512)} %param.5) | copy-start | bytes 6148
  25.0 4.9 %collective-permute-start.7 = (bf16[128,4096]{1,0:T(8,128)(2,1)S(1)}, bf16[128,4096]{1,0:T(8,128)(2,1)S(1)}, u32[]{:S(2)}, u32[]{:S(2)}) collective-permute-start(bf16[128,4096]{1,0:T(8,128)(2,1)S(1)} %bitcast.27), channel_id=1, source_target_pairs={{0,1},{1,0},{2,3},{3,2},{4,5},{5,4},{6,7},{7,6},{8,9},{9,8},{10,11... | collective-permute-start | bytes 3145736 | tf_op jit(solution)/shard_map/ppermute | solution.py:38
  25.1 15.3 %collective-permute-start.6 = (bf16[128,4096]{1,0:T(8,128)(2,1)S(1)}, bf16[128,4096]{1,0:T(8,128)(2,1)S(1)}, u32[]{:S(2)}, u32[]{:S(2)}) collective-permute-start(bf16[128,4096]{1,0:T(8,128)(2,1)S(1)} %bitcast.28), channel_id=1, source_target_pairs={{0,32},{1,5},{2,34},{3,7},{4,36},{5,9},{6,38},{7,11},{8,40},{9,13}... | collective-permute-start | bytes 3145736 | tf_op jit(solution)/shard_map/ppermute | solution.py:38
  26.3 25.0 %collective-permute-start.5 = (bf16[128,4096]{1,0:T(8,128)(2,1)S(1)}, bf16[128,4096]{1,0:T(8,128)(2,1)}, u32[]{:S(2)}, u32[]{:S(2)}) collective-permute-start(bf16[128,4096]{1,0:T(8,128)(2,1)S(1)} %bitcast.29), channel_id=1, source_target_pairs={{0,64},{1,9},{2,66},{3,11},{4,68},{5,13},{6,70},{7,15},{8,72},{9,1... | collective-permute-start | bytes 3145736 | tf_op jit(solution)/shard_map/ppermute | solution.py:38
  27.8 24.5 %collective-permute-start.4 = (bf16[128,4096]{1,0:T(8,128)(2,1)S(1)}, bf16[128,4096]{1,0:T(8,128)(2,1)}, u32[]{:S(2)}, u32[]{:S(2)}) collective-permute-start(bf16[128,4096]{1,0:T(8,128)(2,1)S(1)} %bitcast.30), channel_id=1, source_target_pairs={{0,96},{1,13},{2,98},{3,15},{4,100},{5,1},{6,102},{7,3},{8,104},{9... | collective-permute-start | bytes 3145736 | tf_op jit(solution)/shard_map/ppermute | solution.py:38
  29.9 2.2 %copy-start = (bf16[512,4096]{1,0:T(8,128)(2,1)S(1)}, bf16[512,4096]{1,0:T(8,128)(2,1)}, u32[]{:S(2)}) copy-start(bf16[512,4096]{1,0:T(8,128)(2,1)} %centroids_ref.7) | copy-start | bytes 12582916
  52.2 5.3 %collective-permute-start.9 = (bf16[128,4096]{1,0:T(8,128)(2,1)S(1)}, bf16[128,4096]{1,0:T(8,128)(2,1)S(1)}, u32[]{:S(2)}, u32[]{:S(2)}) collective-permute-start(bf16[128,4096]{1,0:T(8,128)(2,1)S(1)} %collective-permute-done.6.left_ref.refs_4_), channel_id=1, source_target_pairs={{0,1},{1,0},{2,3},{3,2},{4,5},{5,4},{6,7},{7,6},{8,9},{9,8},{10,11... | collective-permute-start | bytes 3145736 | tf_op jit(solution)/shard_map/ppermute | solution.py:38
  53.8 4.0 %collective-permute-start.10 = (bf16[128,4096]{1,0:T(8,128)(2,1)}, bf16[128,4096]{1,0:T(8,128)(2,1)S(1)}, u32[]{:S(2)}, u32[]{:S(2)}) collective-permute-start(bf16[128,4096]{1,0:T(8,128)(2,1)} %collective-permute-done.5.left_ref.refs_2_), channel_id=1, source_target_pairs={{0,1},{1,0},{2,3},{3,2},{4,5},{5,4},{6,7},{7,6},{8,9},{9,8},{10,11... | collective-permute-start | bytes 3145736 | tf_op jit(solution)/shard_map/ppermute | solution.py:38
  53.8 6.2 %collective-permute-start.8 = (bf16[128,4096]{1,0:T(8,128)(2,1)}, bf16[128,4096]{1,0:T(8,128)(2,1)S(1)}, u32[]{:S(2)}, u32[]{:S(2)}) collective-permute-start(bf16[128,4096]{1,0:T(8,128)(2,1)} %collective-permute-done.4.right_ref.refs_3_), channel_id=1, source_target_pairs={{0,1},{1,0},{2,3},{3,2},{4,5},{5,4},{6,7},{7,6},{8,9},{9,8},{10,11... | collective-permute-start | bytes 3145736 | tf_op jit(solution)/shard_map/ppermute | solution.py:38

commit v5 on v4

--- a/solution.py
+++ b/solution.py
@@ -13,7 +13,7 @@
 EVERY = ("psg", "cen")
 X, Z, HALVES = 4, 4, 2
 CHUNKS = 8
-SLOTS = (0, 4, 2, 1, 3, 7, 6, 5)
+OWN = (0, 3, 2, 1)
 LANES = 128
 WIDTH = 1024
 
@@ -57,60 +57,58 @@
     return lax.dynamic_slice_in_dim(jnp.concatenate([rows, rows], 0), 4 - places, 4, 0)
 
 
-def pair_kernel(factor, order_ref, duals_ref, centroids_ref, left_ref, right_ref, *refs):
-    earlier, refs = refs[:-5], refs[-5:]
-    logits_ref, out_ref, kept_ref, rows_ref, sem = refs
-    span = left_ref.shape[0]
-    total = lax.dot_general(
-        centroids_ref[...],
-        jnp.concatenate([left_ref[...], right_ref[...]], axis=0),
-        (((1,), (1,)), ((), ())),
-        preferred_element_type=jnp.float32,
-    )
-    for side in range(2):
-        kept_ref[side] = factor * total[:, side * span : (side + 1) * span]
-    copy_out = pltpu.make_async_copy(kept_ref, logits_ref, sem)
-    copy_out.start()
-    first = 2 * len(earlier)
-    for side in range(2):
-        shifted = kept_ref[side] + duals_ref[...]
+def logits_kernel(factor, count, order_ref, *refs):
+    duals_refs, centroids_refs = refs[:2], refs[2:4]
+    chunk_refs, earlier = refs[4 : 4 + count], refs[4 + count : -4]
+    logits_refs, out_ref, rows_ref = refs[-4:-2], refs[-2], refs[-1]
+    chunks = jnp.concatenate([ref[...] for ref in chunk_refs], axis=0)
+    tops, totals = [], []
+    for duals_ref, centroids_ref, logits_ref in zip(duals_refs, centroids_refs, logits_refs):
+        product = factor * lax.dot_general(
+            centroids_ref[...], chunks, (((1,), (1,)), ((), ())), preferred_element_type=jnp.float32
+        )
+        for k in range(count):
+            logits_ref[k] = product[:, k * LANES : (k + 1) * LANES]
+        shifted = product + duals_ref[...]
         top = jnp.max(shifted, axis=0, keepdims=True)
-        logsum = top + jnp.log(jnp.sum(jnp.exp(shifted - top), axis=0, keepdims=True))
-        if earlier:
-            rows_ref[pl.ds(order_ref[first + side], 1), :] = logsum
-        else:
-            out_ref[side : side + 1, :] = logsum
-    if earlier:
-        for pair, ref in enumerate(earlier):
-            for side in range(2):
-                rows_ref[pl.ds(order_ref[2 * pair + side], 1), :] = ref[side : side + 1, :]
-        send_sums(rows_ref, out_ref)
-    copy_out.wait()
-
-
-def pair_logits(factor, order, duals, centroids, left, right, earlier=()):
-    count, depth = centroids.shape
-    span = left.shape[0]
+        tops.append(top)
+        totals.append(jnp.sum(jnp.exp(shifted - top), axis=0, keepdims=True))
+    top = jnp.maximum(*tops)
+    logsum = top + jnp.log(sum(total * jnp.exp(own - top) for own, total in zip(tops, totals)))
+    logsums = [logsum[:, k * LANES : (k + 1) * LANES] for k in range(count)]
+    if not earlier:
+        for k in range(count):
+            out_ref[k : k + 1, :] = logsums[k]
+        return
+    logsums = [earlier[0][k : k + 1, :] for k in range(4 - count)] + logsums
+    for slot in range(4):
+        rows_ref[pl.ds(lax.rem(order_ref[slot], 4), 1), :] = logsums[slot]
+    send_sums(rows_ref, out_ref)
+
+
+def held(array):
+    return pltpu.with_memory_space_constraint(array, pltpu.VMEM)
+
+
+def chunk_logits(factor, order, duals, centroids, chunks, earlier=()):
+    rows = centroids[0].shape[0]
     devices = lax.axis_size(EVERY)
     f32 = jnp.float32
     if earlier:
-        out_spec = pl.BlockSpec((devices, CHUNKS, span), lambda: (0, 0, 0))
-        out = jax.ShapeDtypeStruct((devices, CHUNKS, span), f32)
+        out_spec = pl.BlockSpec((devices, 4, LANES), lambda: (0, 0, 0))
+        out = jax.ShapeDtypeStruct((devices, 4, LANES), f32)
     else:
-        out_spec, out = VMEM, jax.ShapeDtypeStruct((2, span), f32)
+        out_spec, out = VMEM, jax.ShapeDtypeStruct((len(chunks), LANES), f32)
+    logits = jax.ShapeDtypeStruct((len(chunks), rows, LANES), f32)
+    block = pl.BlockSpec(logits.shape, lambda: (0, 0, 0))
     return pl.pallas_call(
-        functools.partial(pair_kernel, factor),
-        in_specs=[SMEM] + [VMEM] * (4 + len(earlier)),
-        out_specs=[ANY, out_spec],
-        out_shape=[jax.ShapeDtypeStruct((2, count, span), f32), out],
-        scratch_shapes=[
-            pltpu.VMEM((2, count, span), f32),
-            pltpu.VMEM((CHUNKS, span), f32),
-            pltpu.SemaphoreType.DMA,
-        ],
-        cost_estimate=pl.CostEstimate(flops=1, bytes_accessed=1, transcendentals=0),
+        functools.partial(logits_kernel, factor, len(chunks)),
+        in_specs=[SMEM] + [VMEM] * (4 + len(chunks) + len(earlier)),
+        out_specs=[block, block, out_spec],
+        out_shape=[logits, logits, out],
+        scratch_shapes=[pltpu.VMEM((4, LANES), f32)],
         compiler_params=LIMIT,
-    )(order, duals, centroids, left, right, *earlier)
+    )(order, *duals, *[held(array) for array in (*centroids, *chunks)], *earlier)
 
 
 def send_sums(sums_ref, out_ref):
@@ -118,23 +116,26 @@
 
 
 def first_kernel(order_ref, parts_ref, *refs):
-    pairs = CHUNKS // 2
-    kernel_ref, passage_ref, centroid_ref, out_ref, sums_ref, sems = refs[pairs:]
+    logits_refs = refs[:4]
+    kernel_ref, passage_ref, centroid_ref, out_ref, sums_ref, sems = refs[4:]
+    starts = (0, 1, 4, 5)
     copies = [
-        pltpu.make_async_copy(ref, kernel_ref.at[pl.ds(2 * pair, 2)], sems.at[pair])
-        for pair, ref in enumerate(refs[:pairs])
+        pltpu.make_async_copy(ref, kernel_ref.at[pl.ds(start, ref.shape[0])], sems.at[number])
+        for number, (ref, start) in enumerate(zip(logits_refs, starts))
     ]
     for copy in copies:
         copy.start()
-    parts = parts_ref[...]
-    top = jnp.max(parts, axis=0)
-    passage_ref[...] = -math.log(PASSAGES) - (
-        top + jnp.log(jnp.sum(jnp.exp(parts - top[None]), axis=0))
-    )
+    parts = parts_ref[...].reshape(parts_ref.shape[0] // 2, 2, 4, LANES)
+    for core in range(2):
+        part = parts[:, core]
+        top = jnp.max(part, axis=0)
+        passage_ref[core * 4 : core * 4 + 4, :] = -math.log(PASSAGES) - (
+            top + jnp.log(jnp.sum(jnp.exp(part - top[None]), axis=0))
+        )
     peak = None
     for k in range(CHUNKS):
-        if k % 2 == 0:
-            copies[k // 2].wait()
+        if k in starts:
+            copies[starts.index(k)].wait()
         terms = kernel_ref[k] + passage_ref[pl.ds(order_ref[k], 1), :]
         kernel_ref[k] = terms
         peak = terms if peak is None else jnp.maximum(peak, terms)
@@ -198,21 +199,6 @@
             kernel_ref[k] * scale_ref[pl.ds(order_ref[k], 1), :] * inverse
         ).astype(weight_ref.dtype)
 
-    duals = centroid_ref[...] - jnp.log(total)
-    square = (LANES, LANES)
-    diagonal = lax.broadcasted_iota(jnp.int32, square, 0) == lax.broadcasted_iota(
-        jnp.int32, square, 1
-    )
-    for k in range(duals.shape[0] // LANES):
-        column = jnp.broadcast_to(duals[k * LANES : (k + 1) * LANES], square)
-        duals_ref[pl.ds(k, 1), :] = jnp.sum(
-            jnp.where(diagonal, column, 0.0), axis=0, keepdims=True
-        )
-    scale_ref[...] = passage_ref[...] + jnp.log(scale_ref[...])
-    own_ref[...] = pltpu.roll(
-        scale_ref[pl.ds(order_ref[CHUNKS], 1), :], LANES - order_ref[CHUNKS + 1], 1
-    )
-
     def copy_out(tile):
         return pltpu.make_async_copy(
             tile_ref.at[tile % 2], new_ref.at[:, pl.ds(tile * WIDTH, WIDTH)], out_sems.at[tile % 2]
@@ -223,6 +209,20 @@
         block = jnp.dot(
             weight_ref[...], held_ref[tile], preferred_element_type=jnp.float32
         ).astype(new_ref.dtype)
+        if tile == 0:
+            duals = centroid_ref[...] - jnp.log(total)
+            square = (LANES, LANES)
+            diagonal = lax.broadcasted_iota(jnp.int32, square, 0) == lax.broadcasted_iota(
+                jnp.int32, square, 1
+            )
+            for k in range(duals.shape[0] // LANES):
+                column = jnp.broadcast_to(duals[k * LANES : (k + 1) * LANES], square)
+                duals_ref[pl.ds(k, 1), :] = jnp.sum(
+                    jnp.where(diagonal, column, 0.0), axis=0, keepdims=True
+                )
+            scale_ref[...] = passage_ref[...] + jnp.log(scale_ref[...])
+            own = pltpu.roll(scale_ref[pl.ds(order_ref[CHUNKS], 1), :], LANES - order_ref[CHUNKS + 1], 1)
+            own_ref[...] = own[:, : own_ref.shape[1]]
         if tile >= 2:
             copy_out(tile - 2).wait()
         tile_ref[tile % 2] = block
@@ -252,7 +252,7 @@
             stays = h == c
             if stays and step == 0:
                 return None
-            h, c = (h, c) if stays else (1 - h, 1 - c)
+            h, l, c = (h, l, c) if stays else (1 - h, 1 - l, 1 - c)
             return (z, h, x - step, l, c) if c == 0 else (z - step, h, x, l, c)
 
         return move(passages, target)
@@ -260,33 +260,28 @@
     ring = [jnp.where(h == c, passages, fetch(0)), fetch(1), fetch(2), fetch(3)]
     ring = turned(jnp.stack(ring), first).reshape(4 * local_rows, depth)
     own = [ring, along_second(ring, -1), along_second(ring, 2), along_second(ring, 1)]
-    order = [c * 4 + (second + k) % 4 for k in range(4)]
-    order += [(1 - c) * 4 + (first + k) % 4 for k in range(4)]
-    order = [order[k] for k in SLOTS]
+    order = [c * 4 + (second + k) % 4 for k in OWN]
+    order += [(1 - c) * 4 + (first + k) % 4 for k in OWN]
     row, lane = jnp.where(h == 0, z, 4 + x), jnp.where(h == 0, x, z) * local_rows
     order = jnp.stack(order + [row, lane]).astype(jnp.int32)
 
+    column = lambda duals: duals.reshape(count, 1)
     logits_of = functools.partial(
-        pair_logits, factor, order, dual_init.reshape(count, 1), centroids
+        chunk_logits,
+        factor,
+        order,
+        (column(dual_init), column(to_sibling(dual_init))),
+        (centroids, to_sibling(centroids)),
     )
-    sibling = [None] * 4
-    sibling[0] = to_sibling(own[0])
-    pairs = [logits_of(own[0], sibling[0])]
-    own[1], own[2], own[3], _ = lax.optimization_barrier((own[1], own[2], own[3], pairs[0]))
-    sibling[3] = to_sibling(own[3])
-    sibling[2] = to_sibling(own[2])
-    sibling[1] = to_sibling(own[1])
-    pairs.append(logits_of(own[2], own[1]))
-    sibling[3], sibling[2], _ = lax.optimization_barrier((sibling[3], sibling[2], pairs[1]))
-    pairs.append(logits_of(own[3], sibling[3]))
-    sibling[1], sibling[2], _ = lax.optimization_barrier((sibling[1], sibling[2], pairs[2]))
-    pairs.append(logits_of(sibling[2], sibling[1], [logsum for _, logsum in pairs]))
-    chunks = own + sibling
-    chunks = [chunks[k] for k in SLOTS]
-    logits = [pair[0] for pair in pairs]
-    span = chunks[0].shape[0]
+    groups = [logits_of((own[0],))]
+    own[1], own[2], own[3], _ = lax.optimization_barrier((*own[1:], groups[0]))
+    groups.append(logits_of([own[k] for k in OWN[1:]], earlier=[groups[0][2]]))
+    own = [own[k] for k in OWN]
+    logits = [group[0] for group in groups] + [to_sibling(group[1]) for group in groups]
+    span = LANES
     f32 = jnp.float32
-    parts = to_every(pairs[-1][1])
+    parts = to_every(groups[-1][2])
+    pieces = own + [to_sibling(chunk) for chunk in own]
 
     sent = jax.ShapeDtypeStruct((devices, CHUNKS, span), jnp.bfloat16)
     block = pl.BlockSpec((devices, CHUNKS, span), lambda: (0, 0, 0))
@@ -304,6 +299,7 @@
         scratch_shapes=[sums, pltpu.SemaphoreType.DMA((len(logits),))],
         compiler_params=LIMIT,
     )(order, parts, *logits)
+    partial, *pieces = lax.optimization_barrier((partial, *pieces))
     partial = pl.pallas_call(
         middle_kernel,
         in_specs=[SMEM, VMEM, VMEM],
@@ -318,7 +314,7 @@
         out_specs=[ANY, VMEM, VMEM],
         out_shape=[
             jax.ShapeDtypeStruct((count, depth), jnp.bfloat16),
-            jax.ShapeDtypeStruct((1, span), f32),
+            jax.ShapeDtypeStruct((1, local_rows), f32),
             jax.ShapeDtypeStruct((count // LANES, LANES), f32),
         ],
         scratch_shapes=[
@@ -330,8 +326,8 @@
             pltpu.SemaphoreType.DMA((2,)),
         ],
         compiler_params=pltpu.CompilerParams(vmem_limit_bytes=24 * 2**20),
-    )(order, to_every(partial), kernel, passage_first, centroid_first, *chunks)
-    own_duals = own_duals[0, :local_rows]
+    )(order, to_every(partial), kernel, passage_first, centroid_first, *pieces)
+    own_duals = own_duals.reshape(local_rows)
     return (new_centroids, own_duals, centroid_duals.reshape(count))
 
 

time: 126 us -> 121 us (0.960)
  waiting for transfers between devices: 26.4 us -> 20.9 us
  Pallas kernels: 21.4 us -> 23.1 us
  blocking collectives: 51.1 us -> 49.6 us
  local copies, waits for them, and re-layouts: 3.16 us -> 4.46 us
    ppermute x11 -> x15, waiting for transfers between devices: 26.4 us -> 20.9 us  [move(): return lax.ppermute(value, EVERY, pairs)]
    pallas_call x4 -> x2, Pallas kernels: 9.91 us -> 11.9 us  [chunk_logits(): pl.pallas_call(functools.partial(logits_kernel, factor, len(chunks)), in_...]
    all_to_all x3, blocking collectives: 51.1 us -> 49.6 us  [to_every(): return lax.all_to_all(copies, EVERY, 0, 0)]
    unnamed x11 -> x13, local copies, waits for them, and re-layouts: 2.29 us -> 3.24 us
    ppermute x11 -> x15, starting transfers between devices: 22.3 us -> 21.5 us  [move(): return lax.ppermute(value, EVERY, pairs)]
  transfers between devices with their start and end apart: 11 -> 15, of which waited for: 5 -> 5; matrix products, arithmetic and copies ran while one was open for 0% -> 1% of each run, Pallas kernels for 6% -> 11%
where the time goes in v5:
time: 121 us
  blocking collectives  49.6 us (41%)
  Pallas kernels  23.1 us (19%)
  starting transfers between devices  21.5 us (18%)
  waiting for transfers between devices  20.9 us (17%)
  local copies, waits for them, and re-layouts  4.46 us (4%)
    all_to_all x3, blocking collectives, to_every(): return lax.all_to_all(copies, EVERY, 0, 0)  49.6 us
    ppermute x15, starting transfers between devices, move(): return lax.ppermute(value, EVERY, pairs)  21.5 us
    ppermute x15, waiting for transfers between devices, move(): return lax.ppermute(value, EVERY, pairs)  20.9 us
    pallas_call x2, Pallas kernels, chunk_logits(): pl.pallas_call(functools.partial(logits_kernel, factor, len(chunks)), in_...  11.9 us
    pallas_call x1, Pallas kernels, body(): pl.pallas_call(last_kernel, in_specs=[SMEM] + [VMEM] * 4 + [ANY] * CHUNKS...  8.41 us
    unnamed x13, local copies, waits for them, and re-layouts  3.24 us
  transfers between devices with their start and end apart: 15, of which 5 were waited for; matrix products, arithmetic and copies ran while one was open for 1% of the time, Pallas kernels for 11%

profile of v5, /device:TPU:1, one launch (start us, length us, event | category | flops | bytes accessed | tf_op | source)
XLA Modules:
  0.0 120.5 jit_solution(14133012003884512950)
XLA Ops:
  0.6 6.2 %collective-permute-start.2 = (bf16[32,4096]{1,0:T(8,128)(2,1)}, bf16[32,4096]{1,0:T(8,128)(2,1)S(1)}, u32[]{:S(2)}, u32[]{:S(2)}) collective-permute-start(bf16[32,4096]{1,0:T(8,128)(2,1)} %param.3), channel_id=1, source_target_pairs={{1,18},{3,16},{5,22},{7,20},{9,26},{11,24},{13,30},{15,28},{16,3},... | collective-permute-start | bytes 786440 | tf_op jit(solution)/shard_map/ppermute | solution.py:38
  6.8 2.3 %collective-permute-start.3 = (bf16[32,4096]{1,0:T(8,128)(2,1)}, bf16[32,4096]{1,0:T(8,128)(2,1)S(1)}, u32[]{:S(2)}, u32[]{:S(2)}) collective-permute-start(bf16[32,4096]{1,0:T(8,128)(2,1)} %param.3), channel_id=1, source_target_pairs={{0,12},{1,30},{2,14},{3,28},{4,0},{5,18},{6,2},{7,16},{8,4},{9,22}... | collective-permute-start | bytes 786440 | tf_op jit(solution)/shard_map/ppermute | solution.py:38
  9.1 5.2 %collective-permute-start.5 = (bf16[32,4096]{1,0:T(8,128)(2,1)}, bf16[32,4096]{1,0:T(8,128)(2,1)S(1)}, u32[]{:S(2)}, u32[]{:S(2)}) collective-permute-start(bf16[32,4096]{1,0:T(8,128)(2,1)} %param.3), channel_id=1, source_target_pairs={{0,4},{1,22},{2,6},{3,20},{4,8},{5,26},{6,10},{7,24},{8,12},{9,30}... | collective-permute-start | bytes 786440 | tf_op jit(solution)/shard_map/ppermute | solution.py:38
  14.2 1.5 %collective-permute-start.4 = (bf16[32,4096]{1,0:T(8,128)(2,1)}, bf16[32,4096]{1,0:T(8,128)(2,1)S(1)}, u32[]{:S(2)}, u32[]{:S(2)}) collective-permute-start(bf16[32,4096]{1,0:T(8,128)(2,1)} %param.3), channel_id=1, source_target_pairs={{0,8},{1,26},{2,10},{3,24},{4,12},{5,30},{6,14},{7,28},{8,0},{9,18... | collective-permute-start | bytes 786440 | tf_op jit(solution)/shard_map/ppermute | solution.py:38
  15.9 8.1 %collective-permute-done.4 = bf16[32,4096]{1,0:T(8,128)(2,1)S(1)} collective-permute-done((bf16[32,4096]{1,0:T(8,128)(2,1)}, bf16[32,4096]{1,0:T(8,128)(2,1)S(1)}, u32[]{:S(2)}, u32[]{:S(2)}) %collective-permute-start.4) | collective-permute-done | bytes 262176 | tf_op jit(solution)/shard_map/ppermute | solution.py:38
  24.3 1.3 %collective-permute-start.8 = (bf16[128,4096]{1,0:T(8,128)(2,1)S(1)}, bf16[128,4096]{1,0:T(8,128)(2,1)S(1)}, u32[]{:S(2)}, u32[]{:S(2)}) collective-permute-start(bf16[128,4096]{1,0:T(8,128)(2,1)S(1)} %bitcast.27), channel_id=1, source_target_pairs={{0,32},{1,5},{2,34},{3,7},{4,36},{5,9},{6,38},{7,11},{8,40},{9,13}... | collective-permute-start | bytes 3145736 | tf_op jit(solution)/shard_map/ppermute | solution.py:38
  25.6 1.6 %collective-permute-start.7 = (bf16[128,4096]{1,0:T(8,128)(2,1)S(1)}, bf16[128,4096]{1,0:T(8,128)(2,1)S(1)}, u32[]{:S(2)}, u32[]{:S(2)}) collective-permute-start(bf16[128,4096]{1,0:T(8,128)(2,1)S(1)} %bitcast.28), channel_id=1, source_target_pairs={{0,64},{1,9},{2,66},{3,11},{4,68},{5,13},{6,70},{7,15},{8,72},{9,1... | collective-permute-start | bytes 3145736 | tf_op jit(solution)/shard_map/ppermute | solution.py:38
  27.2 1.8 %collective-permute-start.6 = (bf16[128,4096]{1,0:T(8,128)(2,1)S(1)}, bf16[128,4096]{1,0:T(8,128)(2,1)}, u32[]{:S(2)}, u32[]{:S(2)}) collective-permute-start(bf16[128,4096]{1,0:T(8,128)(2,1)S(1)} %bitcast.29), channel_id=1, source_target_pairs={{0,96},{1,13},{2,98},{3,15},{4,100},{5,1},{6,102},{7,3},{8,104},{9... | collective-permute-start | bytes 3145736 | tf_op jit(solution)/shard_map/ppermute | solution.py:38
  29.2 0.9 collective-permute-done
  30.1 0.9 copy.9.refs_1_
  31.1 2.2 %copy-done = bf16[512,4096]{1,0:T(8,128)(2,1)S(1)} copy-done((bf16[512,4096]{1,0:T(8,128)(2,1)S(1)}, bf16[512,4096]{1,0:T(8,128)(2,1)}, u32[]{:S(2)}) %copy-start) | copy-done | bytes 4194328
  33.3 0.9 copy-done.1
  34.3 4.6 %shard_map.58 = (f32[1,512,128]{2,1,0:T(8,128)S(1)}, f32[1,512,128]{2,1,0:T(8,128)S(1)}, f32[1,128]{1,0:T(1,128)S(1)}) custom-call(s32[10]{0:T(128)S(1)} %stack.56.order_ref, f32[512,1]{1,0:T(8,128)S(1)} %copy.8.refs_0_, f32[512,1]{1,0:T(8,128)S(1)} %copy-done.1, bf16[512,4096]{1,0:T(8,128)(2,1)S(1)} %copy-done, ...), custom_call_target="tpu_custom_call" | custom-call | tf_op jit(solution)/shard_map/pallas_call | solution.py:104
  39.5 11.1 %collective-permute-done.7.refs_5_.refs_2_ = bf16[128,4096]{1,0:T(8,128)(2,1)S(1)} collective-permute-done((bf16[128,4096]{1,0:T(8,128)(2,1)S(1)}, bf16[128,4096]{1,0:T(8,128)(2,1)S(1)}, u32[]{:S(2)}, u32[]{:S(2)}) %collective-permute-start.7) | collective-permute-done | bytes 1048608 | tf_op jit(solution)/shard_map/ppermute | solution.py:38
  50.6 0.6 collective-permute-done.6.refs_6_.refs_3_
  51.2 0.5 collective-permute-start.13
  51.7 7.3 %shard_map.59 = (f32[3,512,128]{2,1,0:T(8,128)S(1)}, f32[3,512,128]{2,1,0:T(8,128)S(1)}, f32[128,4,128]{2,1,0:T(4,128)S(1)}) custom-call(s32[10]{0:T(128)S(1)} %stack.56.order_ref, f32[512,1]{1,0:T(8,128)S(1)} %copy.8.refs_0_, f32[512,1]{1,0:T(8,128)S(1)} %copy-done.1, bf16[512,4096]{1,0:T(8,128)(2,1)S(1)} %copy-done, ...), custom_call_target="tpu_custom_call" | custom-call | tf_op jit(solution)/shard_map/pallas_call | solution.py:104
  59.0 0.6 collective-permute-start.10
  59.6 19.2 %all_to_all.15.parts_ref = f32[128,4,128]{2,1,0:T(4,128)S(1)} all-to-all(f32[128,4,128]{2,1,0:T(4,128)S(1)} %get-tuple-element.34), channel_id=1, replica_groups=mesh['psg'=32,'cen'=4] {'psg','cen'}, dimensions={0} | all-to-all | bytes 524288 | tf_op jit(solution)/shard_map/all_to_all | solution.py:53
  78.9 1.7 %shard_map.60 = (f32[8,512,128]{2,1,0:T(8,128)S(1)}, f32[8,128]{1,0:T(8,128)S(1)}, f32[512,1]{1,0:T(8,128)S(1)}, bf16[128,8,128]{2,1,0:T(8,128)(2,1)S(1)}) custom-call(s32[10]{0:T(128)S(1)} %stack.56.order_ref, f32[128,4,128]{2,1,0:T(4,128)S(1)} %all_to_all.15.parts_ref, f32[1,512,128]{2,1,0:T(8,128)S(1)} %get-tuple-element.28.refs_0_, ...), custom_call_target="tpu_custom_call" | custom-call | tf_op jit(solution)/shard_map/pallas_call | solution.py:289
  80.6 15.2 %all_to_all.16.parts_ref = bf16[128,8,128]{2,1,0:T(8,128)(2,1)S(1)} all-to-all(bf16[128,8,128]{2,1,0:T(8,128)(2,1)S(1)} %get-tuple-element.38), channel_id=1, replica_groups=mesh['psg'=32,'cen'=4] {'psg','cen'}, dimensions={0} | all-to-all | bytes 524288 | tf_op jit(solution)/shard_map/all_to_all | solution.py:53
  95.8 1.0 shard_map.61
  96.8 15.2 %all_to_all.17.parts_ref = bf16[128,8,128]{2,1,0:T(8,128)(2,1)S(1)} all-to-all(bf16[128,8,128]{2,1,0:T(8,128)(2,1)S(1)} %shard_map.61), channel_id=1, replica_groups=mesh['psg'=32,'cen'=4] {'psg','cen'}, dimensions={0} | all-to-all | bytes 524288 | tf_op jit(solution)/shard_map/all_to_all | solution.py:53
  112.0 8.4 %shard_map.62 = (bf16[512,4096]{1,0:T(8,128)(2,1)}, f32[1,32]{1,0:T(1,128)}, f32[4,128]{1,0:T(4,128)}) custom-call(s32[10]{0:T(128)S(1)} %stack.56.order_ref, bf16[128,8,128]{2,1,0:T(8,128)(2,1)S(1)} %all_to_all.17.parts_ref, f32[8,512,128]{2,1,0:T(8,128)S(1)} %get-tuple-element.39.kernel_ref, f32[8,128]{1,0:T(8,128)S(1)} %get-tuple-element.40.passage_ref, ...), custom_call_target="tpu_custom_call" | custom-call | tf_op jit(solution)/shard_map/pallas_call | solution.py:311
  (34 shorter events, 1.4 us)
Async XLA Ops:
  0.6 23.4 %copy-start.2 = (bf16[32,4096]{1,0:T(8,128)(2,1)S(1)}, bf16[32,4096]{1,0:T(8,128)(2,1)}, u32[]{:S(2)}) copy-start(bf16[32,4096]{1,0:T(8,128)(2,1)} %param.3) | copy-start | bytes 786436
  0.6 15.1 %collective-permute-start.2 = (bf16[32,4096]{1,0:T(8,128)(2,1)}, bf16[32,4096]{1,0:T(8,128)(2,1)S(1)}, u32[]{:S(2)}, u32[]{:S(2)}) collective-permute-start(bf16[32,4096]{1,0:T(8,128)(2,1)} %param.3), channel_id=1, source_target_pairs={{1,18},{3,16},{5,22},{7,20},{9,26},{11,24},{13,30},{15,28},{16,3},... | collective-permute-start | bytes 786440 | tf_op jit(solution)/shard_map/ppermute | solution.py:38
  6.8 9.0 %collective-permute-start.3 = (bf16[32,4096]{1,0:T(8,128)(2,1)}, bf16[32,4096]{1,0:T(8,128)(2,1)S(1)}, u32[]{:S(2)}, u32[]{:S(2)}) collective-permute-start(bf16[32,4096]{1,0:T(8,128)(2,1)} %param.3), channel_id=1, source_target_pairs={{0,12},{1,30},{2,14},{3,28},{4,0},{5,18},{6,2},{7,16},{8,4},{9,22}... | collective-permute-start | bytes 786440 | tf_op jit(solution)/shard_map/ppermute | solution.py:38
  9.1 14.9 %collective-permute-start.5 = (bf16[32,4096]{1,0:T(8,128)(2,1)}, bf16[32,4096]{1,0:T(8,128)(2,1)S(1)}, u32[]{:S(2)}, u32[]{:S(2)}) collective-permute-start(bf16[32,4096]{1,0:T(8,128)(2,1)} %param.3), channel_id=1, source_target_pairs={{0,4},{1,22},{2,6},{3,20},{4,8},{5,26},{6,10},{7,24},{8,12},{9,30}... | collective-permute-start | bytes 786440 | tf_op jit(solution)/shard_map/ppermute | solution.py:38
  14.2 9.7 %collective-permute-start.4 = (bf16[32,4096]{1,0:T(8,128)(2,1)}, bf16[32,4096]{1,0:T(8,128)(2,1)S(1)}, u32[]{:S(2)}, u32[]{:S(2)}) collective-permute-start(bf16[32,4096]{1,0:T(8,128)(2,1)} %param.3), channel_id=1, source_target_pairs={{0,8},{1,26},{2,10},{3,24},{4,12},{5,30},{6,14},{7,28},{8,0},{9,18... | collective-permute-start | bytes 786440 | tf_op jit(solution)/shard_map/ppermute | solution.py:38
  15.8 15.4 %collective-permute-start.1 = (bf16[512,4096]{1,0:T(8,128)(2,1)}, bf16[512,4096]{1,0:T(8,128)(2,1)}, u32[]{:S(2)}, u32[]{:S(2)}) collective-permute-start(bf16[512,4096]{1,0:T(8,128)(2,1)} %refs_2_.3), channel_id=1, source_target_pairs={{0,1},{1,0},{2,3},{3,2},{4,5},{5,4},{6,7},{7,6},{8,9},{9,8},{10,11... | collective-permute-start | bytes 12582920 | tf_op jit(solution)/shard_map/ppermute | solution.py:38
  24.0 4.9 %copy-start.3 = (f32[512]{0:T(512)S(1)}, f32[512]{0:T(512)}, u32[]{:S(2)}) copy-start(f32[512]{0:T(512)} %param.5) | copy-start | bytes 6148
  24.3 15.2 %collective-permute-start.8 = (bf16[128,4096]{1,0:T(8,128)(2,1)S(1)}, bf16[128,4096]{1,0:T(8,128)(2,1)S(1)}, u32[]{:S(2)}, u32[]{:S(2)}) collective-permute-start(bf16[128,4096]{1,0:T(8,128)(2,1)S(1)} %bitcast.27), channel_id=1, source_target_pairs={{0,32},{1,5},{2,34},{3,7},{4,36},{5,9},{6,38},{7,11},{8,40},{9,13}... | collective-permute-start | bytes 3145736 | tf_op jit(solution)/shard_map/ppermute | solution.py:38
  25.6 25.0 %collective-permute-start.7 = (bf16[128,4096]{1,0:T(8,128)(2,1)S(1)}, bf16[128,4096]{1,0:T(8,128)(2,1)S(1)}, u32[]{:S(2)}, u32[]{:S(2)}) collective-permute-start(bf16[128,4096]{1,0:T(8,128)(2,1)S(1)} %bitcast.28), channel_id=1, source_target_pairs={{0,64},{1,9},{2,66},{3,11},{4,68},{5,13},{6,70},{7,15},{8,72},{9,1... | collective-permute-start | bytes 3145736 | tf_op jit(solution)/shard_map/ppermute | solution.py:38
  27.2 24.0 %collective-permute-start.6 = (bf16[128,4096]{1,0:T(8,128)(2,1)S(1)}, bf16[128,4096]{1,0:T(8,128)(2,1)}, u32[]{:S(2)}, u32[]{:S(2)}) collective-permute-start(bf16[128,4096]{1,0:T(8,128)(2,1)S(1)} %bitcast.29), channel_id=1, source_target_pairs={{0,96},{1,13},{2,98},{3,15},{4,100},{5,1},{6,102},{7,3},{8,104},{9... | collective-permute-start | bytes 3145736 | tf_op jit(solution)/shard_map/ppermute | solution.py:38
  28.9 1.2 collective-permute-start
  31.0 49.6 %collective-permute-start.11 = (bf16[128,4096]{1,0:T(8,128)(2,1)S(1)}, bf16[128,4096]{1,0:T(8,128)(2,1)S(1)}, u32[]{:S(2)}, u32[]{:S(2)}) collective-permute-start(bf16[128,4096]{1,0:T(8,128)(2,1)S(1)} %bitcast.30), channel_id=1, source_target_pairs={{0,1},{1,0},{2,3},{3,2},{4,5},{5,4},{6,7},{7,6},{8,9},{9,8},{10,11... | collective-permute-start | bytes 3145736 | tf_op jit(solution)/shard_map/ppermute | solution.py:38
  31.1 2.2 %copy-start = (bf16[512,4096]{1,0:T(8,128)(2,1)S(1)}, bf16[512,4096]{1,0:T(8,128)(2,1)}, u32[]{:S(2)}) copy-start(bf16[512,4096]{1,0:T(8,128)(2,1)} %refs_2_.3) | copy-start | bytes 12582916
  33.3 0.9 copy-start.1
  38.9 20.1 %collective-permute-start.9 = (f32[1,512,128]{2,1,0:T(8,128)S(1)}, f32[1,512,128]{2,1,0:T(8,128)S(1)}, u32[]{:S(2)}, u32[]{:S(2)}) collective-permute-start(f32[1,512,128]{2,1,0:T(8,128)S(1)} %get-tuple-element.29), channel_id=1, source_target_pairs={{0,1},{1,0},{2,3},{3,2},{4,5},{5,4},{6,7},{7,6},{8,9},{9,8},{10,11... | collective-permute-start | bytes 786440 | tf_op jit(solution)/shard_map/ppermute | solution.py:38
  51.2 29.4 %collective-permute-start.12 = (bf16[128,4096]{1,0:T(8,128)(2,1)S(1)}, bf16[128,4096]{1,0:T(8,128)(2,1)S(1)}, u32[]{:S(2)}, u32[]{:S(2)}) collective-permute-start(bf16[128,4096]{1,0:T(8,128)(2,1)S(1)} %collective-permute-done.8.refs_4_.refs_1_), channel_id=1, source_target_pairs={{0,1},{1,0},{2,3},{3,2},{4,5},{5,4},{6,7},{7,6},{8,9},{9,8},{10,11... | collective-permute-start | bytes 3145736 | tf_op jit(solution)/shard_map/ppermute | solution.py:38
  51.2 29.4 %collective-permute-start.13 = (bf16[128,4096]{1,0:T(8,128)(2,1)S(1)}, bf16[128,4096]{1,0:T(8,128)(2,1)S(1)}, u32[]{:S(2)}, u32[]{:S(2)}) collective-permute-start(bf16[128,4096]{1,0:T(8,128)(2,1)S(1)} %collective-permute-done.7.refs_5_.refs_2_), channel_id=1, source_target_pairs={{0,1},{1,0},{2,3},{3,2},{4,5},{5,4},{6,7},{7,6},{8,9},{9,8},{10,11... | collective-permute-start | bytes 3145736 | tf_op jit(solution)/shard_map/ppermute | solution.py:38
  51.7 28.9 %collective-permute-start.14 = (bf16[128,4096]{1,0:T(8,128)(2,1)}, bf16[128,4096]{1,0:T(8,128)(2,1)S(1)}, u32[]{:S(2)}, u32[]{:S(2)}) collective-permute-start(bf16[128,4096]{1,0:T(8,128)(2,1)} %collective-permute-done.6.refs_6_.refs_3_), channel_id=1, source_target_pairs={{0,1},{1,0},{2,3},{3,2},{4,5},{5,4},{6,7},{7,6},{8,9},{9,8},{10,11... | collective-permute-start | bytes 3145736 | tf_op jit(solution)/shard_map/ppermute | solution.py:38
  59.0 19.8 %collective-permute-start.10 = (f32[3,512,128]{2,1,0:T(8,128)S(1)}, f32[3,512,128]{2,1,0:T(8,128)S(1)}, u32[]{:S(2)}, u32[]{:S(2)}) collective-permute-start(f32[3,512,128]{2,1,0:T(8,128)S(1)} %get-tuple-element.36), channel_id=1, source_target_pairs={{0,1},{1,0},{2,3},{3,2},{4,5},{5,4},{6,7},{7,6},{8,9},{9,8},{10,11... | collective-permute-start | bytes 2359304 | tf_op jit(solution)/shard_map/ppermute | solution.py:38

commit v6 on v5

--- a/solution.py
+++ b/solution.py
@@ -15,7 +15,8 @@
 CHUNKS = 8
 OWN = (0, 3, 2, 1)
 LANES = 128
-WIDTH = 1024
+WIDTH = 2048
+PARTS = 16
 
 
 def coords(device):
@@ -59,11 +60,21 @@
 
 def logits_kernel(factor, count, order_ref, *refs):
     duals_refs, centroids_refs = refs[:2], refs[2:4]
-    chunk_refs, earlier = refs[4 : 4 + count], refs[4 + count : -4]
-    logits_refs, out_ref, rows_ref = refs[-4:-2], refs[-2], refs[-1]
+    chunk_refs, refs = refs[4 : 4 + count], refs[4 + count :]
+    if count == 1:
+        earlier, (*logits_refs, out_ref, near_ref, sem) = None, refs
+        size = near_ref.shape[0] // PARTS
+        for part in range(PARTS):
+            rows = pl.ds(part * size, size)
+            pltpu.make_async_copy(centroids_refs[1].at[rows], near_ref.at[rows], sem).start()
+        centroids_refs = centroids_refs[0], near_ref
+    else:
+        earlier, *logits_refs, out_ref, rows_ref = refs
     chunks = jnp.concatenate([ref[...] for ref in chunk_refs], axis=0)
     tops, totals = [], []
     for duals_ref, centroids_ref, logits_ref in zip(duals_refs, centroids_refs, logits_refs):
+        if count == 1 and centroids_ref is near_ref:
+            pltpu.make_async_copy(near_ref, near_ref, sem).wait()
         product = factor * lax.dot_general(
             centroids_ref[...], chunks, (((1,), (1,)), ((), ())), preferred_element_type=jnp.float32
         )
@@ -75,12 +86,10 @@
         totals.append(jnp.sum(jnp.exp(shifted - top), axis=0, keepdims=True))
     top = jnp.maximum(*tops)
     logsum = top + jnp.log(sum(total * jnp.exp(own - top) for own, total in zip(tops, totals)))
-    logsums = [logsum[:, k * LANES : (k + 1) * LANES] for k in range(count)]
-    if not earlier:
-        for k in range(count):
-            out_ref[k : k + 1, :] = logsums[k]
+    if earlier is None:
+        out_ref[...] = logsum
         return
-    logsums = [earlier[0][k : k + 1, :] for k in range(4 - count)] + logsums
+    logsums = [earlier[...]] + [logsum[:, k * LANES : (k + 1) * LANES] for k in range(count)]
     for slot in range(4):
         rows_ref[pl.ds(lax.rem(order_ref[slot], 4), 1), :] = logsums[slot]
     send_sums(rows_ref, out_ref)
@@ -94,21 +103,27 @@
     rows = centroids[0].shape[0]
     devices = lax.axis_size(EVERY)
     f32 = jnp.float32
-    if earlier:
-        out_spec = pl.BlockSpec((devices, 4, LANES), lambda: (0, 0, 0))
-        out = jax.ShapeDtypeStruct((devices, 4, LANES), f32)
-    else:
-        out_spec, out = VMEM, jax.ShapeDtypeStruct((len(chunks), LANES), f32)
     logits = jax.ShapeDtypeStruct((len(chunks), rows, LANES), f32)
     block = pl.BlockSpec(logits.shape, lambda: (0, 0, 0))
+    if earlier:
+        second = VMEM
+        out_specs = [pl.BlockSpec((devices, 4, LANES), lambda: (0, 0, 0))]
+        outs = [jax.ShapeDtypeStruct((devices, 4, LANES), f32)]
+        scratch = [pltpu.VMEM((4, LANES), f32)]
+    else:
+        second, out_specs = ANY, [VMEM, VMEM]
+        outs = [jax.ShapeDtypeStruct((1, LANES), f32)]
+        outs += [jax.ShapeDtypeStruct(centroids[1].shape, centroids[1].dtype)]
+        scratch = [pltpu.SemaphoreType.DMA]
+    near = [held(array) for array in chunks]
     return pl.pallas_call(
         functools.partial(logits_kernel, factor, len(chunks)),
-        in_specs=[SMEM] + [VMEM] * (4 + len(chunks) + len(earlier)),
-        out_specs=[block, block, out_spec],
-        out_shape=[logits, logits, out],
-        scratch_shapes=[pltpu.VMEM((4, LANES), f32)],
+        in_specs=[SMEM] + [VMEM] * 3 + [second] + [VMEM] * (len(chunks) + len(earlier)),
+        out_specs=[block, block] + out_specs,
+        out_shape=[logits, logits] + outs,
+        scratch_shapes=scratch,
         compiler_params=LIMIT,
-    )(order, *duals, *[held(array) for array in (*centroids, *chunks)], *earlier)
+    )(order, *duals, held(centroids[0]), centroids[1], *near, *earlier)
 
 
 def send_sums(sums_ref, out_ref):
@@ -267,15 +282,13 @@
 
     column = lambda duals: duals.reshape(count, 1)
     logits_of = functools.partial(
-        chunk_logits,
-        factor,
-        order,
-        (column(dual_init), column(to_sibling(dual_init))),
-        (centroids, to_sibling(centroids)),
+        chunk_logits, factor, order, (column(dual_init), column(to_sibling(dual_init)))
     )
-    groups = [logits_of((own[0],))]
+    groups = [logits_of((centroids, to_sibling(centroids)), (own[0],))]
     own[1], own[2], own[3], _ = lax.optimization_barrier((*own[1:], groups[0]))
-    groups.append(logits_of([own[k] for k in OWN[1:]], earlier=[groups[0][2]]))
+    groups.append(
+        logits_of((centroids, groups[0][3]), [own[k] for k in OWN[1:]], earlier=[groups[0][2]])
+    )
     own = [own[k] for k in OWN]
     logits = [group[0] for group in groups] + [to_sibling(group[1]) for group in groups]
     span = LANES

time: 121 us -> 120 us (level)
  waiting for transfers between devices: 20.9 us -> 18.5 us
    ppermute x15, waiting for transfers between devices: 20.9 us -> 18.5 us  [move(): return lax.ppermute(value, EVERY, pairs)]
  transfers between devices with their start and end apart: 15 -> 15, of which waited for: 5 -> 4; matrix products, arithmetic and copies ran while one was open for 1% -> 1% of each run, Pallas kernels for 11% -> 12%
where the time goes in v6:
time: 120 us; the launch traced here: 119 us
  blocking collectives  49.6 us (41%)
  Pallas kernels  24.1 us (20%)
  starting transfers between devices  21.5 us (18%)
  waiting for transfers between devices  18.5 us (15%)
  local copies, waits for them, and re-layouts  4.46 us (4%)
    all_to_all x3, blocking collectives, to_every(): return lax.all_to_all(copies, EVERY, 0, 0)  49.6 us
    ppermute x15, starting transfers between devices, move(): return lax.ppermute(value, EVERY, pairs)  21.5 us
    ppermute x15, waiting for transfers between devices, move(): return lax.ppermute(value, EVERY, pairs)  18.5 us
    pallas_call x2, Pallas kernels, chunk_logits(): pl.pallas_call(functools.partial(logits_kernel, factor, len(chunks)), in_...  13 us
    pallas_call x1, Pallas kernels, body(): pl.pallas_call(last_kernel, in_specs=[SMEM] + [VMEM] * 4 + [ANY] * CHUNKS...  8.3 us
    unnamed x13, local copies, waits for them, and re-layouts  3.24 us
  transfers between devices with their start and end apart: 15, of which 4 were waited for; matrix products, arithmetic and copies ran while one was open for 1% of the time, Pallas kernels for 12%

profile of v6, /device:TPU:1, one launch (start us, length us, event | category | flops | bytes accessed | tf_op | source)
XLA Modules:
  0.0 119.2 jit_solution(10918920005476270999)
XLA Ops:
  0.6 6.2 %collective-permute-start.2 = (bf16[32,4096]{1,0:T(8,128)(2,1)}, bf16[32,4096]{1,0:T(8,128)(2,1)S(1)}, u32[]{:S(2)}, u32[]{:S(2)}) collective-permute-start(bf16[32,4096]{1,0:T(8,128)(2,1)} %param.3), channel_id=1, source_target_pairs={{1,18},{3,16},{5,22},{7,20},{9,26},{11,24},{13,30},{15,28},{16,3},... | collective-permute-start | bytes 786440 | tf_op jit(solution)/shard_map/ppermute | solution.py:39
  6.8 2.3 %collective-permute-start.3 = (bf16[32,4096]{1,0:T(8,128)(2,1)}, bf16[32,4096]{1,0:T(8,128)(2,1)S(1)}, u32[]{:S(2)}, u32[]{:S(2)}) collective-permute-start(bf16[32,4096]{1,0:T(8,128)(2,1)} %param.3), channel_id=1, source_target_pairs={{0,12},{1,30},{2,14},{3,28},{4,0},{5,18},{6,2},{7,16},{8,4},{9,22}... | collective-permute-start | bytes 786440 | tf_op jit(solution)/shard_map/ppermute | solution.py:39
  9.1 5.2 %collective-permute-start.5 = (bf16[32,4096]{1,0:T(8,128)(2,1)}, bf16[32,4096]{1,0:T(8,128)(2,1)S(1)}, u32[]{:S(2)}, u32[]{:S(2)}) collective-permute-start(bf16[32,4096]{1,0:T(8,128)(2,1)} %param.3), channel_id=1, source_target_pairs={{0,4},{1,22},{2,6},{3,20},{4,8},{5,26},{6,10},{7,24},{8,12},{9,30}... | collective-permute-start | bytes 786440 | tf_op jit(solution)/shard_map/ppermute | solution.py:39
  14.2 1.5 %collective-permute-start.4 = (bf16[32,4096]{1,0:T(8,128)(2,1)}, bf16[32,4096]{1,0:T(8,128)(2,1)S(1)}, u32[]{:S(2)}, u32[]{:S(2)}) collective-permute-start(bf16[32,4096]{1,0:T(8,128)(2,1)} %param.3), channel_id=1, source_target_pairs={{0,8},{1,26},{2,10},{3,24},{4,12},{5,30},{6,14},{7,28},{8,0},{9,18... | collective-permute-start | bytes 786440 | tf_op jit(solution)/shard_map/ppermute | solution.py:39
  15.9 8.1 %collective-permute-done.4 = bf16[32,4096]{1,0:T(8,128)(2,1)S(1)} collective-permute-done((bf16[32,4096]{1,0:T(8,128)(2,1)}, bf16[32,4096]{1,0:T(8,128)(2,1)S(1)}, u32[]{:S(2)}, u32[]{:S(2)}) %collective-permute-start.4) | collective-permute-done | bytes 262176 | tf_op jit(solution)/shard_map/ppermute | solution.py:39
  24.3 1.3 %collective-permute-start.8 = (bf16[128,4096]{1,0:T(8,128)(2,1)S(1)}, bf16[128,4096]{1,0:T(8,128)(2,1)S(1)}, u32[]{:S(2)}, u32[]{:S(2)}) collective-permute-start(bf16[128,4096]{1,0:T(8,128)(2,1)S(1)} %bitcast.27), channel_id=1, source_target_pairs={{0,32},{1,5},{2,34},{3,7},{4,36},{5,9},{6,38},{7,11},{8,40},{9,13}... | collective-permute-start | bytes 3145736 | tf_op jit(solution)/shard_map/ppermute | solution.py:39
  25.6 1.6 %collective-permute-start.7 = (bf16[128,4096]{1,0:T(8,128)(2,1)S(1)}, bf16[128,4096]{1,0:T(8,128)(2,1)S(1)}, u32[]{:S(2)}, u32[]{:S(2)}) collective-permute-start(bf16[128,4096]{1,0:T(8,128)(2,1)S(1)} %bitcast.28), channel_id=1, source_target_pairs={{0,64},{1,9},{2,66},{3,11},{4,68},{5,13},{6,70},{7,15},{8,72},{9,1... | collective-permute-start | bytes 3145736 | tf_op jit(solution)/shard_map/ppermute | solution.py:39
  27.2 1.8 %collective-permute-start.6 = (bf16[128,4096]{1,0:T(8,128)(2,1)S(1)}, bf16[128,4096]{1,0:T(8,128)(2,1)}, u32[]{:S(2)}, u32[]{:S(2)}) collective-permute-start(bf16[128,4096]{1,0:T(8,128)(2,1)S(1)} %bitcast.29), channel_id=1, source_target_pairs={{0,96},{1,13},{2,98},{3,15},{4,100},{5,1},{6,102},{7,3},{8,104},{9... | collective-permute-start | bytes 3145736 | tf_op jit(solution)/shard_map/ppermute | solution.py:39
  29.2 0.9 collective-permute-done
  30.1 0.9 copy.9.refs_1_
  31.1 2.2 %copy-done = bf16[512,4096]{1,0:T(8,128)(2,1)S(1)} copy-done((bf16[512,4096]{1,0:T(8,128)(2,1)S(1)}, bf16[512,4096]{1,0:T(8,128)(2,1)}, u32[]{:S(2)}) %copy-start) | copy-done | bytes 4194328
  33.3 0.9 copy-done.1
  34.3 7.0 %shard_map.58 = (f32[1,512,128]{2,1,0:T(8,128)S(1)}, f32[1,512,128]{2,1,0:T(8,128)S(1)}, f32[1,128]{1,0:T(1,128)S(1)}, bf16[512,4096]{1,0:T(8,128)(2,1)S(1)}) custom-call(s32[10]{0:T(128)S(1)} %stack.56.order_ref, f32[512,1]{1,0:T(8,128)S(1)} %copy.8.refs_0_, f32[512,1]{1,0:T(8,128)S(1)} %copy-done.1, bf16[512,4096]{1,0:T(8,128)(2,1)S(1)} %copy-done, ...), custom_call_target="tpu_custom_call" | custom-call | tf_op jit(solution)/shard_map/pallas_call | solution.py:119
  41.7 8.9 %collective-permute-done.7.refs_5_.refs_2_ = bf16[128,4096]{1,0:T(8,128)(2,1)S(1)} collective-permute-done((bf16[128,4096]{1,0:T(8,128)(2,1)S(1)}, bf16[128,4096]{1,0:T(8,128)(2,1)S(1)}, u32[]{:S(2)}, u32[]{:S(2)}) %collective-permute-start.7) | collective-permute-done | bytes 1048608 | tf_op jit(solution)/shard_map/ppermute | solution.py:39
  50.6 0.6 collective-permute-done.6.refs_6_.refs_3_
  51.2 0.5 collective-permute-start.13
  51.7 6.0 %shard_map.59 = (f32[3,512,128]{2,1,0:T(8,128)S(1)}, f32[3,512,128]{2,1,0:T(8,128)S(1)}, f32[128,4,128]{2,1,0:T(4,128)S(1)}) custom-call(s32[10]{0:T(128)S(1)} %stack.56.order_ref, f32[512,1]{1,0:T(8,128)S(1)} %copy.8.refs_0_, f32[512,1]{1,0:T(8,128)S(1)} %copy-done.1, bf16[512,4096]{1,0:T(8,128)(2,1)S(1)} %copy-done, ...), custom_call_target="tpu_custom_call" | custom-call | tf_op jit(solution)/shard_map/pallas_call | solution.py:119
  57.8 0.6 collective-permute-start.10
  58.4 19.2 %all_to_all.15.parts_ref = f32[128,4,128]{2,1,0:T(4,128)S(1)} all-to-all(f32[128,4,128]{2,1,0:T(4,128)S(1)} %get-tuple-element.36), channel_id=1, replica_groups=mesh['psg'=32,'cen'=4] {'psg','cen'}, dimensions={0} | all-to-all | bytes 524288 | tf_op jit(solution)/shard_map/all_to_all | solution.py:54
  77.6 1.7 %shard_map.60 = (f32[8,512,128]{2,1,0:T(8,128)S(1)}, f32[8,128]{1,0:T(8,128)S(1)}, f32[512,1]{1,0:T(8,128)S(1)}, bf16[128,8,128]{2,1,0:T(8,128)(2,1)S(1)}) custom-call(s32[10]{0:T(128)S(1)} %stack.56.order_ref, f32[128,4,128]{2,1,0:T(4,128)S(1)} %all_to_all.15.parts_ref, f32[1,512,128]{2,1,0:T(8,128)S(1)} %get-tuple-element.30.refs_0_, ...), custom_call_target="tpu_custom_call" | custom-call | tf_op jit(solution)/shard_map/pallas_call | solution.py:302
  79.4 15.2 %all_to_all.16.parts_ref = bf16[128,8,128]{2,1,0:T(8,128)(2,1)S(1)} all-to-all(bf16[128,8,128]{2,1,0:T(8,128)(2,1)S(1)} %get-tuple-element.40), channel_id=1, replica_groups=mesh['psg'=32,'cen'=4] {'psg','cen'}, dimensions={0} | all-to-all | bytes 524288 | tf_op jit(solution)/shard_map/all_to_all | solution.py:54
  94.5 1.0 shard_map.61
  95.5 15.2 %all_to_all.17.parts_ref = bf16[128,8,128]{2,1,0:T(8,128)(2,1)S(1)} all-to-all(bf16[128,8,128]{2,1,0:T(8,128)(2,1)S(1)} %shard_map.61), channel_id=1, replica_groups=mesh['psg'=32,'cen'=4] {'psg','cen'}, dimensions={0} | all-to-all | bytes 524288 | tf_op jit(solution)/shard_map/all_to_all | solution.py:54
  110.7 8.3 %shard_map.62 = (bf16[512,4096]{1,0:T(8,128)(2,1)}, f32[1,32]{1,0:T(1,128)}, f32[4,128]{1,0:T(4,128)}) custom-call(s32[10]{0:T(128)S(1)} %stack.56.order_ref, bf16[128,8,128]{2,1,0:T(8,128)(2,1)S(1)} %all_to_all.17.parts_ref, f32[8,512,128]{2,1,0:T(8,128)S(1)} %get-tuple-element.41.kernel_ref, f32[8,128]{1,0:T(8,128)S(1)} %get-tuple-element.42.passage_ref, ...), custom_call_target="tpu_custom_call" | custom-call | tf_op jit(solution)/shard_map/pallas_call | solution.py:324
  (34 shorter events, 1.2 us)
Async XLA Ops:
  0.6 23.4 %copy-start.2 = (bf16[32,4096]{1,0:T(8,128)(2,1)S(1)}, bf16[32,4096]{1,0:T(8,128)(2,1)}, u32[]{:S(2)}) copy-start(bf16[32,4096]{1,0:T(8,128)(2,1)} %param.3) | copy-start | bytes 786436
  0.6 15.1 %collective-permute-start.2 = (bf16[32,4096]{1,0:T(8,128)(2,1)}, bf16[32,4096]{1,0:T(8,128)(2,1)S(1)}, u32[]{:S(2)}, u32[]{:S(2)}) collective-permute-start(bf16[32,4096]{1,0:T(8,128)(2,1)} %param.3), channel_id=1, source_target_pairs={{1,18},{3,16},{5,22},{7,20},{9,26},{11,24},{13,30},{15,28},{16,3},... | collective-permute-start | bytes 786440 | tf_op jit(solution)/shard_map/ppermute | solution.py:39
  6.8 9.0 %collective-permute-start.3 = (bf16[32,4096]{1,0:T(8,128)(2,1)}, bf16[32,4096]{1,0:T(8,128)(2,1)S(1)}, u32[]{:S(2)}, u32[]{:S(2)}) collective-permute-start(bf16[32,4096]{1,0:T(8,128)(2,1)} %param.3), channel_id=1, source_target_pairs={{0,12},{1,30},{2,14},{3,28},{4,0},{5,18},{6,2},{7,16},{8,4},{9,22}... | collective-permute-start | bytes 786440 | tf_op jit(solution)/shard_map/ppermute | solution.py:39
  9.1 14.9 %collective-permute-start.5 = (bf16[32,4096]{1,0:T(8,128)(2,1)}, bf16[32,4096]{1,0:T(8,128)(2,1)S(1)}, u32[]{:S(2)}, u32[]{:S(2)}) collective-permute-start(bf16[32,4096]{1,0:T(8,128)(2,1)} %param.3), channel_id=1, source_target_pairs={{0,4},{1,22},{2,6},{3,20},{4,8},{5,26},{6,10},{7,24},{8,12},{9,30}... | collective-permute-start | bytes 786440 | tf_op jit(solution)/shard_map/ppermute | solution.py:39
  14.2 9.7 %collective-permute-start.4 = (bf16[32,4096]{1,0:T(8,128)(2,1)}, bf16[32,4096]{1,0:T(8,128)(2,1)S(1)}, u32[]{:S(2)}, u32[]{:S(2)}) collective-permute-start(bf16[32,4096]{1,0:T(8,128)(2,1)} %param.3), channel_id=1, source_target_pairs={{0,8},{1,26},{2,10},{3,24},{4,12},{5,30},{6,14},{7,28},{8,0},{9,18... | collective-permute-start | bytes 786440 | tf_op jit(solution)/shard_map/ppermute | solution.py:39
  15.8 15.4 %collective-permute-start.1 = (bf16[512,4096]{1,0:T(8,128)(2,1)}, bf16[512,4096]{1,0:T(8,128)(2,1)}, u32[]{:S(2)}, u32[]{:S(2)}) collective-permute-start(bf16[512,4096]{1,0:T(8,128)(2,1)} %refs_2_.3), channel_id=1, source_target_pairs={{0,1},{1,0},{2,3},{3,2},{4,5},{5,4},{6,7},{7,6},{8,9},{9,8},{10,11... | collective-permute-start | bytes 12582920 | tf_op jit(solution)/shard_map/ppermute | solution.py:39
  24.0 4.9 %copy-start.3 = (f32[512]{0:T(512)S(1)}, f32[512]{0:T(512)}, u32[]{:S(2)}) copy-start(f32[512]{0:T(512)} %param.5) | copy-start | bytes 6148
  24.3 17.4 %collective-permute-start.8 = (bf16[128,4096]{1,0:T(8,128)(2,1)S(1)}, bf16[128,4096]{1,0:T(8,128)(2,1)S(1)}, u32[]{:S(2)}, u32[]{:S(2)}) collective-permute-start(bf16[128,4096]{1,0:T(8,128)(2,1)S(1)} %bitcast.27), channel_id=1, source_target_pairs={{0,32},{1,5},{2,34},{3,7},{4,36},{5,9},{6,38},{7,11},{8,40},{9,13}... | collective-permute-start | bytes 3145736 | tf_op jit(solution)/shard_map/ppermute | solution.py:39
  25.6 25.0 %collective-permute-start.7 = (bf16[128,4096]{1,0:T(8,128)(2,1)S(1)}, bf16[128,4096]{1,0:T(8,128)(2,1)S(1)}, u32[]{:S(2)}, u32[]{:S(2)}) collective-permute-start(bf16[128,4096]{1,0:T(8,128)(2,1)S(1)} %bitcast.28), channel_id=1, source_target_pairs={{0,64},{1,9},{2,66},{3,11},{4,68},{5,13},{6,70},{7,15},{8,72},{9,1... | collective-permute-start | bytes 3145736 | tf_op jit(solution)/shard_map/ppermute | solution.py:39
  27.2 24.0 %collective-permute-start.6 = (bf16[128,4096]{1,0:T(8,128)(2,1)S(1)}, bf16[128,4096]{1,0:T(8,128)(2,1)}, u32[]{:S(2)}, u32[]{:S(2)}) collective-permute-start(bf16[128,4096]{1,0:T(8,128)(2,1)S(1)} %bitcast.29), channel_id=1, source_target_pairs={{0,96},{1,13},{2,98},{3,15},{4,100},{5,1},{6,102},{7,3},{8,104},{9... | collective-permute-start | bytes 3145736 | tf_op jit(solution)/shard_map/ppermute | solution.py:39
  28.9 1.2 collective-permute-start
  31.0 48.4 %collective-permute-start.11 = (bf16[128,4096]{1,0:T(8,128)(2,1)S(1)}, bf16[128,4096]{1,0:T(8,128)(2,1)S(1)}, u32[]{:S(2)}, u32[]{:S(2)}) collective-permute-start(bf16[128,4096]{1,0:T(8,128)(2,1)S(1)} %bitcast.30), channel_id=1, source_target_pairs={{0,1},{1,0},{2,3},{3,2},{4,5},{5,4},{6,7},{7,6},{8,9},{9,8},{10,11... | collective-permute-start | bytes 3145736 | tf_op jit(solution)/shard_map/ppermute | solution.py:39
  31.1 2.2 %copy-start = (bf16[512,4096]{1,0:T(8,128)(2,1)S(1)}, bf16[512,4096]{1,0:T(8,128)(2,1)}, u32[]{:S(2)}) copy-start(bf16[512,4096]{1,0:T(8,128)(2,1)} %refs_2_.3) | copy-start | bytes 12582916
  33.3 0.9 copy-start.1
  41.3 16.5 %collective-permute-start.9 = (f32[1,512,128]{2,1,0:T(8,128)S(1)}, f32[1,512,128]{2,1,0:T(8,128)S(1)}, u32[]{:S(2)}, u32[]{:S(2)}) collective-permute-start(f32[1,512,128]{2,1,0:T(8,128)S(1)} %get-tuple-element.31), channel_id=1, source_target_pairs={{0,1},{1,0},{2,3},{3,2},{4,5},{5,4},{6,7},{7,6},{8,9},{9,8},{10,11... | collective-permute-start | bytes 786440 | tf_op jit(solution)/shard_map/ppermute | solution.py:39
  51.2 28.1 %collective-permute-start.12 = (bf16[128,4096]{1,0:T(8,128)(2,1)S(1)}, bf16[128,4096]{1,0:T(8,128)(2,1)S(1)}, u32[]{:S(2)}, u32[]{:S(2)}) collective-permute-start(bf16[128,4096]{1,0:T(8,128)(2,1)S(1)} %collective-permute-done.8.refs_4_.refs_1_), channel_id=1, source_target_pairs={{0,1},{1,0},{2,3},{3,2},{4,5},{5,4},{6,7},{7,6},{8,9},{9,8},{10,11... | collective-permute-start | bytes 3145736 | tf_op jit(solution)/shard_map/ppermute | solution.py:39
  51.2 28.1 %collective-permute-start.13 = (bf16[128,4096]{1,0:T(8,128)(2,1)S(1)}, bf16[128,4096]{1,0:T(8,128)(2,1)S(1)}, u32[]{:S(2)}, u32[]{:S(2)}) collective-permute-start(bf16[128,4096]{1,0:T(8,128)(2,1)S(1)} %collective-permute-done.7.refs_5_.refs_2_), channel_id=1, source_target_pairs={{0,1},{1,0},{2,3},{3,2},{4,5},{5,4},{6,7},{7,6},{8,9},{9,8},{10,11... | collective-permute-start | bytes 3145736 | tf_op jit(solution)/shard_map/ppermute | solution.py:39
  51.7 27.6 %collective-permute-start.14 = (bf16[128,4096]{1,0:T(8,128)(2,1)}, bf16[128,4096]{1,0:T(8,128)(2,1)S(1)}, u32[]{:S(2)}, u32[]{:S(2)}) collective-permute-start(bf16[128,4096]{1,0:T(8,128)(2,1)} %collective-permute-done.6.refs_6_.refs_3_), channel_id=1, source_target_pairs={{0,1},{1,0},{2,3},{3,2},{4,5},{5,4},{6,7},{7,6},{8,9},{9,8},{10,11... | collective-permute-start | bytes 3145736 | tf_op jit(solution)/shard_map/ppermute | solution.py:39
  57.8 19.8 %collective-permute-start.10 = (f32[3,512,128]{2,1,0:T(8,128)S(1)}, f32[3,512,128]{2,1,0:T(8,128)S(1)}, u32[]{:S(2)}, u32[]{:S(2)}) collective-permute-start(f32[3,512,128]{2,1,0:T(8,128)S(1)} %get-tuple-element.38), channel_id=1, source_target_pairs={{0,1},{1,0},{2,3},{3,2},{4,5},{5,4},{6,7},{7,6},{8,9},{9,8},{10,11... | collective-permute-start | bytes 2359304 | tf_op jit(solution)/shard_map/ppermute | solution.py:39

commit v7 on v5

--- a/solution.py
+++ b/solution.py
@@ -15,7 +15,8 @@
 CHUNKS = 8
 OWN = (0, 3, 2, 1)
 LANES = 128
-WIDTH = 1024
+WIDTH = 2048
+PARTS = 16
 
 
 def coords(device):
@@ -57,17 +58,42 @@
     return lax.dynamic_slice_in_dim(jnp.concatenate([rows, rows], 0), 4 - places, 4, 0)
 
 
-def logits_kernel(factor, count, order_ref, *refs):
-    duals_refs, centroids_refs = refs[:2], refs[2:4]
-    chunk_refs, earlier = refs[4 : 4 + count], refs[4 + count : -4]
-    logits_refs, out_ref, rows_ref = refs[-4:-2], refs[-2], refs[-1]
-    chunks = jnp.concatenate([ref[...] for ref in chunk_refs], axis=0)
+def stage_kernel(*refs):
+    rows_refs, centroids_refs, columns_refs, held_refs, sem = refs[:2], refs[2:4], refs[4:6], refs[6:8], refs[8]
+    for source, target in zip(centroids_refs, held_refs):
+        size = target.shape[0] // PARTS
+        for part in range(PARTS):
+            rows = pl.ds(part * size, size)
+            pltpu.make_async_copy(source.at[rows], target.at[rows], sem).start()
+    square = (LANES, LANES)
+    diagonal = lax.broadcasted_iota(jnp.int32, square, 0) == lax.broadcasted_iota(
+        jnp.int32, square, 1
+    )
+    for source, target in zip(rows_refs, columns_refs):
+        for k in range(source.shape[0]):
+            row = jnp.broadcast_to(source[k : k + 1, :], square)
+            target[k * LANES : (k + 1) * LANES, :] = jnp.sum(
+                jnp.where(diagonal, row, 0.0), axis=1, keepdims=True
+            )
+    for target in held_refs:
+        pltpu.make_async_copy(target, target, sem).wait()
+
+
+def logits_kernel(factor, order_ref, *refs):
+    duals_refs, centroids_refs, piece_refs = refs[:2], refs[2:4], refs[4:11]
+    *logits_refs, out_ref, arrived_ref, rows_ref, sem = refs[11:]
+    start = 0
+    for ref in piece_refs[1:]:
+        size = ref.shape[0]
+        pltpu.make_async_copy(ref, arrived_ref.at[pl.ds(start, size)], sem).start()
+        start += size
+    chunks = jnp.concatenate([ref[...] for ref in piece_refs], axis=0)
     tops, totals = [], []
     for duals_ref, centroids_ref, logits_ref in zip(duals_refs, centroids_refs, logits_refs):
         product = factor * lax.dot_general(
             centroids_ref[...], chunks, (((1,), (1,)), ((), ())), preferred_element_type=jnp.float32
         )
-        for k in range(count):
+        for k in range(4):
             logits_ref[k] = product[:, k * LANES : (k + 1) * LANES]
         shifted = product + duals_ref[...]
         top = jnp.max(shifted, axis=0, keepdims=True)
@@ -75,40 +101,49 @@
         totals.append(jnp.sum(jnp.exp(shifted - top), axis=0, keepdims=True))
     top = jnp.maximum(*tops)
     logsum = top + jnp.log(sum(total * jnp.exp(own - top) for own, total in zip(tops, totals)))
-    logsums = [logsum[:, k * LANES : (k + 1) * LANES] for k in range(count)]
-    if not earlier:
-        for k in range(count):
-            out_ref[k : k + 1, :] = logsums[k]
-        return
-    logsums = [earlier[0][k : k + 1, :] for k in range(4 - count)] + logsums
-    for slot in range(4):
-        rows_ref[pl.ds(lax.rem(order_ref[slot], 4), 1), :] = logsums[slot]
+    for k in range(4):
+        rows_ref[pl.ds(lax.rem(order_ref[k], 4), 1), :] = logsum[:, k * LANES : (k + 1) * LANES]
     send_sums(rows_ref, out_ref)
+    pltpu.make_async_copy(arrived_ref, arrived_ref, sem).wait()
 
 
 def held(array):
     return pltpu.with_memory_space_constraint(array, pltpu.VMEM)
 
 
-def chunk_logits(factor, order, duals, centroids, chunks, earlier=()):
+def staged(duals, centroids):
     rows = centroids[0].shape[0]
+    column = jax.ShapeDtypeStruct((rows, 1), jnp.float32)
+    arrays = [jax.ShapeDtypeStruct(array.shape, array.dtype) for array in centroids]
+    return pl.pallas_call(
+        stage_kernel,
+        in_specs=[VMEM] * 2 + [ANY] * 2,
+        out_specs=[VMEM] * 4,
+        out_shape=[column, column] + arrays,
+        scratch_shapes=[pltpu.SemaphoreType.DMA],
+        compiler_params=LIMIT,
+    )(*[dual.reshape(rows // LANES, LANES) for dual in duals], *centroids)
+
+
+def chunk_logits(factor, order, columns, centroids, pieces):
+    rows, depth = centroids[0].shape
     devices = lax.axis_size(EVERY)
     f32 = jnp.float32
-    if earlier:
-        out_spec = pl.BlockSpec((devices, 4, LANES), lambda: (0, 0, 0))
-        out = jax.ShapeDtypeStruct((devices, 4, LANES), f32)
-    else:
-        out_spec, out = VMEM, jax.ShapeDtypeStruct((len(chunks), LANES), f32)
-    logits = jax.ShapeDtypeStruct((len(chunks), rows, LANES), f32)
+    logits = jax.ShapeDtypeStruct((4, rows, LANES), f32)
     block = pl.BlockSpec(logits.shape, lambda: (0, 0, 0))
     return pl.pallas_call(
-        functools.partial(logits_kernel, factor, len(chunks)),
-        in_specs=[SMEM] + [VMEM] * (4 + len(chunks) + len(earlier)),
-        out_specs=[block, block, out_spec],
-        out_shape=[logits, logits, out],
-        scratch_shapes=[pltpu.VMEM((4, LANES), f32)],
-        compiler_params=LIMIT,
-    )(order, *duals, *[held(array) for array in (*centroids, *chunks)], *earlier)
+        functools.partial(logits_kernel, factor),
+        in_specs=[SMEM] + [VMEM] * (4 + len(pieces)),
+        out_specs=[block, block, pl.BlockSpec((devices, 4, LANES), lambda: (0, 0, 0)), ANY],
+        out_shape=[
+            logits,
+            logits,
+            jax.ShapeDtypeStruct((devices, 4, LANES), f32),
+            jax.ShapeDtypeStruct((3 * LANES, depth), pieces[0].dtype),
+        ],
+        scratch_shapes=[pltpu.VMEM((4, LANES), f32), pltpu.SemaphoreType.DMA],
+        compiler_params=pltpu.CompilerParams(vmem_limit_bytes=24 * 2**20),
+    )(order, *columns, *centroids, *[held(array) for array in pieces])
 
 
 def send_sums(sums_ref, out_ref):
@@ -116,9 +151,9 @@
 
 
 def first_kernel(order_ref, parts_ref, *refs):
-    logits_refs = refs[:4]
-    kernel_ref, passage_ref, centroid_ref, out_ref, sums_ref, sems = refs[4:]
-    starts = (0, 1, 4, 5)
+    logits_refs = refs[:2]
+    kernel_ref, passage_ref, centroid_ref, out_ref, sums_ref, sems = refs[2:]
+    starts = (0, 4)
     copies = [
         pltpu.make_async_copy(ref, kernel_ref.at[pl.ds(start, ref.shape[0])], sems.at[number])
         for number, (ref, start) in enumerate(zip(logits_refs, starts))
@@ -179,17 +214,19 @@
 
 
 def last_kernel(order_ref, parts_ref, kernel_ref, passage_ref, centroid_ref, *refs):
-    chunk_refs = refs[:CHUNKS]
-    new_ref, own_ref, duals_ref, weight_ref, held_ref, tile_ref, scale_ref, sems, out_sems = refs[CHUNKS:]
-    span = chunk_refs[0].shape[0]
-    tiles = held_ref.shape[0]
+    *piece_refs, new_ref, own_ref, duals_ref = refs[:-6]
+    weight_ref, held_ref, tile_ref, scale_ref, sems, out_sems = refs[-6:]
+    span, tiles = LANES, held_ref.shape[0]
     for tile in range(tiles):
-        for k in range(CHUNKS):
+        start = 0
+        for ref in piece_refs:
+            size = ref.shape[0]
             pltpu.make_async_copy(
-                chunk_refs[k].at[:, pl.ds(tile * WIDTH, WIDTH)],
-                held_ref.at[tile, pl.ds(k * span, span), :],
+                ref.at[:, pl.ds(tile * WIDTH, WIDTH)],
+                held_ref.at[tile, pl.ds(start, size), :],
                 sems.at[tile],
             ).start()
+            start += size
 
     scale_ref[...] = row_scale_of(parts_ref)
     total = column_sums(order_ref, kernel_ref, scale_ref)
@@ -259,28 +296,31 @@
 
     ring = [jnp.where(h == c, passages, fetch(0)), fetch(1), fetch(2), fetch(3)]
     ring = turned(jnp.stack(ring), first).reshape(4 * local_rows, depth)
-    own = [ring, along_second(ring, -1), along_second(ring, 2), along_second(ring, 1)]
+    near_duals = to_sibling(dual_init)
+    ring, near_duals = lax.optimization_barrier((ring, near_duals))
+
+    half = ring.shape[0] // 2
+    top, bottom = ring[:half], ring[half:]
+    top_before, bottom_after = along_second(top, 1), along_second(bottom, -1)
+    bottom_before, top_after = along_second(bottom, 1), along_second(top, -1)
+    top_across, bottom_across = along_second(top_before, 1), along_second(bottom_after, -1)
+    arrived = [top_before, bottom_before, top_across, bottom_across, top_after, bottom_after]
     order = [c * 4 + (second + k) % 4 for k in OWN]
     order += [(1 - c) * 4 + (first + k) % 4 for k in OWN]
     row, lane = jnp.where(h == 0, z, 4 + x), jnp.where(h == 0, x, z) * local_rows
     order = jnp.stack(order + [row, lane]).astype(jnp.int32)
 
-    column = lambda duals: duals.reshape(count, 1)
-    logits_of = functools.partial(
-        chunk_logits,
-        factor,
-        order,
-        (column(dual_init), column(to_sibling(dual_init))),
-        (centroids, to_sibling(centroids)),
+    pairs, _ = lax.optimization_barrier(
+        ((dual_init, near_duals, centroids, to_sibling(centroids)), (top_before, bottom_after))
     )
-    groups = [logits_of((own[0],))]
-    own[1], own[2], own[3], _ = lax.optimization_barrier((*own[1:], groups[0]))
-    groups.append(logits_of([own[k] for k in OWN[1:]], earlier=[groups[0][2]]))
-    own = [own[k] for k in OWN]
-    logits = [group[0] for group in groups] + [to_sibling(group[1]) for group in groups]
+    *columns, near, sibling = staged(pairs[:2], pairs[2:])
+    arrived, near, sibling = lax.optimization_barrier((arrived, near, sibling))
+    *logits, parts, arrived = chunk_logits(factor, order, columns, (near, sibling), [ring] + arrived)
+    logits = [logits[0], to_sibling(logits[1])]
     span = LANES
     f32 = jnp.float32
-    parts = to_every(groups[-1][2])
+    parts = to_every(parts)
+    own = [ring, arrived]
     pieces = own + [to_sibling(chunk) for chunk in own]
 
     sent = jax.ShapeDtypeStruct((devices, CHUNKS, span), jnp.bfloat16)
@@ -310,7 +350,7 @@
     )(order, to_every(partial), kernel)
     new_centroids, own_duals, centroid_duals = pl.pallas_call(
         last_kernel,
-        in_specs=[SMEM] + [VMEM] * 4 + [ANY] * CHUNKS,
+        in_specs=[SMEM] + [VMEM] * 4 + [ANY] * len(pieces),
         out_specs=[ANY, VMEM, VMEM],
         out_shape=[
             jax.ShapeDtypeStruct((count, depth), jnp.bfloat16),

time: 121 us -> 115 us (0.950)
  Pallas kernels: 23.1 us -> 19.9 us
    pallas_call x3, Pallas kernels: 20.4 us -> 17.3 us  [the longest x1 8.52 us: body(): pl.pallas_call(last_kernel, in_specs=[SMEM] + [VMEM] * 4 + [ANY] * len(pi...]
    unnamed x13 -> x11, local copies, waits for them, and re-layouts: 3.24 us -> 2.29 us
  transfers between devices with their start and end apart: 15 -> 15, of which waited for: 5 -> 6; matrix products, arithmetic and copies ran while one was open for 1% -> 1% of each run, Pallas kernels for 11% -> 4%
where the time goes in v7:
time: 115 us
  blocking collectives  48.6 us (42%)
  starting transfers between devices  21.9 us (19%)
  waiting for transfers between devices  20 us (17%)
  Pallas kernels  19.9 us (17%)
  local copies, waits for them, and re-layouts  3.54 us (3%)
    all_to_all x3, blocking collectives, to_every(): return lax.all_to_all(copies, EVERY, 0, 0)  48.6 us
    ppermute x15, starting transfers between devices, move(): return lax.ppermute(value, EVERY, pairs)  21.9 us
    ppermute x15, waiting for transfers between devices, move(): return lax.ppermute(value, EVERY, pairs)  20 us
    pallas_call x1, Pallas kernels, body(): pl.pallas_call(last_kernel, in_specs=[SMEM] + [VMEM] * 4 + [ANY] * len(pi...  8.52 us
    pallas_call x1, Pallas kernels, chunk_logits(): pl.pallas_call(functools.partial(logits_kernel, factor), in_specs=[SMEM]...  6.28 us
    pallas_call x1, Pallas kernels, staged(): pl.pallas_call(stage_kernel, in_specs=[VMEM] * 2 + [ANY] * 2, out_specs=[...  2.46 us
  transfers between devices with their start and end apart: 15, of which 6 were waited for; matrix products, arithmetic and copies ran while one was open for 1% of the time, Pallas kernels for 4%

profile of v7, /device:TPU:1, one launch (start us, length us, event | category | flops | bytes accessed | tf_op | source)
XLA Modules:
  0.0 115.1 jit_solution(15410004087855721182)
XLA Ops:
  0.6 6.2 %collective-permute-start = (bf16[32,4096]{1,0:T(8,128)(2,1)}, bf16[32,4096]{1,0:T(8,128)(2,1)S(1)}, u32[]{:S(2)}, u32[]{:S(2)}) collective-permute-start(bf16[32,4096]{1,0:T(8,128)(2,1)} %param.3), channel_id=1, source_target_pairs={{1,18},{3,16},{5,22},{7,20},{9,26},{11,24},{13,30},{15,28},{16,3},... | collective-permute-start | bytes 786440 | tf_op jit(solution)/shard_map/ppermute | solution.py:39
  6.8 2.3 %collective-permute-start.1 = (bf16[32,4096]{1,0:T(8,128)(2,1)}, bf16[32,4096]{1,0:T(8,128)(2,1)S(1)}, u32[]{:S(2)}, u32[]{:S(2)}) collective-permute-start(bf16[32,4096]{1,0:T(8,128)(2,1)} %param.3), channel_id=1, source_target_pairs={{0,12},{1,30},{2,14},{3,28},{4,0},{5,18},{6,2},{7,16},{8,4},{9,22}... | collective-permute-start | bytes 786440 | tf_op jit(solution)/shard_map/ppermute | solution.py:39
  9.1 6.7 %collective-permute-start.2 = (bf16[32,4096]{1,0:T(8,128)(2,1)}, bf16[32,4096]{1,0:T(8,128)(2,1)S(1)}, u32[]{:S(2)}, u32[]{:S(2)}) collective-permute-start(bf16[32,4096]{1,0:T(8,128)(2,1)} %param.3), channel_id=1, source_target_pairs={{0,8},{1,26},{2,10},{3,24},{4,12},{5,30},{6,14},{7,28},{8,0},{9,18... | collective-permute-start | bytes 786440 | tf_op jit(solution)/shard_map/ppermute | solution.py:39
  15.8 0.5 collective-permute-start.5
  16.4 3.6 %collective-permute-done.2 = bf16[32,4096]{1,0:T(8,128)(2,1)S(1)} collective-permute-done((bf16[32,4096]{1,0:T(8,128)(2,1)}, bf16[32,4096]{1,0:T(8,128)(2,1)S(1)}, u32[]{:S(2)}, u32[]{:S(2)}) %collective-permute-start.2) | collective-permute-done | bytes 262176 | tf_op jit(solution)/shard_map/ppermute | solution.py:39
  20.0 5.1 %collective-permute-done.3 = bf16[32,4096]{1,0:T(8,128)(2,1)S(1)} collective-permute-done((bf16[32,4096]{1,0:T(8,128)(2,1)}, bf16[32,4096]{1,0:T(8,128)(2,1)S(1)}, u32[]{:S(2)}, u32[]{:S(2)}) %collective-permute-start.3) | collective-permute-done | bytes 262176 | tf_op jit(solution)/shard_map/ppermute | solution.py:39
  25.4 1.1 fusion
  26.5 0.9 collective-permute-start.7
  27.3 0.6 collective-permute-start.6
  27.9 2.1 %collective-permute-start.11 = (bf16[64,4096]{1,0:T(8,128)(2,1)}, bf16[64,4096]{1,0:T(8,128)(2,1)S(1)}, u32[]{:S(2)}, u32[]{:S(2)}) collective-permute-start(bf16[64,4096]{1,0:T(8,128)(2,1)} %get-tuple-element.72), channel_id=1, source_target_pairs={{0,96},{1,13},{2,98},{3,15},{4,100},{5,1},{6,102},{7,3},{8,104},{9... | collective-permute-start | bytes 1572872 | tf_op jit(solution)/shard_map/ppermute | solution.py:39
  30.0 5.0 %collective-permute-done.7.refs_10_ = bf16[64,4096]{1,0:T(8,128)(2,1)S(1)} collective-permute-done((bf16[64,4096]{1,0:T(8,128)(2,1)}, bf16[64,4096]{1,0:T(8,128)(2,1)S(1)}, u32[]{:S(2)}, u32[]{:S(2)}) %collective-permute-start.7) | collective-permute-done | bytes 524320 | tf_op jit(solution)/shard_map/ppermute | solution.py:39
  35.0 2.1 %collective-permute-start.10 = (bf16[64,4096]{1,0:T(8,128)(2,1)S(1)}, bf16[64,4096]{1,0:T(8,128)(2,1)}, u32[]{:S(2)}, u32[]{:S(2)}) collective-permute-start(bf16[64,4096]{1,0:T(8,128)(2,1)S(1)} %collective-permute-done.7.refs_10_), channel_id=1, source_target_pairs={{0,96},{1,13},{2,98},{3,15},{4,100},{5,1},{6,102},{7,3},{8,104},{9... | collective-permute-start | bytes 1572872 | tf_op jit(solution)/shard_map/ppermute | solution.py:39
  37.2 2.2 %copy-done = bf16[512,4096]{1,0:T(8,128)(2,1)S(1)} copy-done((bf16[512,4096]{1,0:T(8,128)(2,1)S(1)}, bf16[512,4096]{1,0:T(8,128)(2,1)}, u32[]{:S(2)}) %copy-start) | copy-done | bytes 4194328
  39.4 2.5 %shard_map.58 = (f32[512,1]{1,0:T(8,128)S(1)}, f32[512,1]{1,0:T(8,128)S(1)}, bf16[512,4096]{1,0:T(8,128)(2,1)S(1)}, bf16[512,4096]{1,0:T(8,128)(2,1)S(1)}) custom-call(f32[4,128]{1,0:T(4,128)S(1)} %bitcast.31, f32[4,128]{1,0:T(4,128)S(1)} %bitcast.32, bf16[512,4096]{1,0:T(8,128)(2,1)S(1)} %copy-done, bf16[512,4096]{1,0:T(8,128)(2,1)} %collective-permute-done.5.refs_3_), custom_call_target="tpu_custom_call" | custom-call | tf_op jit(solution)/shard_map/pallas_call | solution.py:118
  41.9 0.9 collective-permute-done.8.refs_6_
  42.8 3.5 %collective-permute-done.10.refs_8_ = bf16[64,4096]{1,0:T(8,128)(2,1)} collective-permute-done((bf16[64,4096]{1,0:T(8,128)(2,1)S(1)}, bf16[64,4096]{1,0:T(8,128)(2,1)}, u32[]{:S(2)}, u32[]{:S(2)}) %collective-permute-start.10) | collective-permute-done | bytes 524320 | tf_op jit(solution)/shard_map/ppermute | solution.py:39
  46.3 1.8 %collective-permute-done.9.refs_7_ = bf16[64,4096]{1,0:T(8,128)(2,1)} collective-permute-done((bf16[64,4096]{1,0:T(8,128)(2,1)S(1)}, bf16[64,4096]{1,0:T(8,128)(2,1)}, u32[]{:S(2)}, u32[]{:S(2)}) %collective-permute-start.9) | collective-permute-done | bytes 524320 | tf_op jit(solution)/shard_map/ppermute | solution.py:39
  48.1 6.3 %shard_map.59 = (f32[4,512,128]{2,1,0:T(8,128)S(1)}, f32[4,512,128]{2,1,0:T(8,128)S(1)}, f32[128,4,128]{2,1,0:T(4,128)S(1)}, bf16[384,4096]{1,0:T(8,128)(2,1)S(1)}) custom-call(s32[10]{0:T(128)S(1)} %stack.56.order_ref, f32[512,1]{1,0:T(8,128)S(1)} %get-tuple-element.43.refs_0_, f32[512,1]{1,0:T(8,128)S(1)} %get-tuple-element.44.refs_1_, ...), custom_call_target="tpu_custom_call" | custom-call | tf_op jit(solution)/shard_map/pallas_call | solution.py:134
  55.1 18.3 %all_to_all.15.parts_ref = f32[128,4,128]{2,1,0:T(4,128)S(1)} all-to-all(f32[128,4,128]{2,1,0:T(4,128)S(1)} %get-tuple-element.55), channel_id=1, replica_groups=mesh['psg'=32,'cen'=4] {'psg','cen'}, dimensions={0} | all-to-all | bytes 524288 | tf_op jit(solution)/shard_map/all_to_all | solution.py:54
  73.4 1.7 %shard_map.60 = (f32[8,512,128]{2,1,0:T(8,128)S(1)}, f32[8,128]{1,0:T(8,128)S(1)}, f32[512,1]{1,0:T(8,128)S(1)}, bf16[128,8,128]{2,1,0:T(8,128)(2,1)S(1)}) custom-call(s32[10]{0:T(128)S(1)} %stack.56.order_ref, f32[128,4,128]{2,1,0:T(4,128)S(1)} %all_to_all.15.parts_ref, f32[4,512,128]{2,1,0:T(8,128)S(1)} %get-tuple-element.56.refs_0_, ...), custom_call_target="tpu_custom_call" | custom-call | tf_op jit(solution)/shard_map/pallas_call | solution.py:329
  75.0 15.2 %all_to_all.16.parts_ref = bf16[128,8,128]{2,1,0:T(8,128)(2,1)S(1)} all-to-all(bf16[128,8,128]{2,1,0:T(8,128)(2,1)S(1)} %get-tuple-element.60), channel_id=1, replica_groups=mesh['psg'=32,'cen'=4] {'psg','cen'}, dimensions={0} | all-to-all | bytes 524288 | tf_op jit(solution)/shard_map/all_to_all | solution.py:54
  90.2 1.0 shard_map.61
  91.2 15.2 %all_to_all.17.parts_ref = bf16[128,8,128]{2,1,0:T(8,128)(2,1)S(1)} all-to-all(bf16[128,8,128]{2,1,0:T(8,128)(2,1)S(1)} %shard_map.61), channel_id=1, replica_groups=mesh['psg'=32,'cen'=4] {'psg','cen'}, dimensions={0} | all-to-all | bytes 524288 | tf_op jit(solution)/shard_map/all_to_all | solution.py:54
  106.4 8.5 %shard_map.62 = (bf16[512,4096]{1,0:T(8,128)(2,1)}, f32[1,32]{1,0:T(1,128)}, f32[4,128]{1,0:T(4,128)}) custom-call(s32[10]{0:T(128)S(1)} %stack.56.order_ref, bf16[128,8,128]{2,1,0:T(8,128)(2,1)S(1)} %all_to_all.17.parts_ref, f32[8,512,128]{2,1,0:T(8,128)S(1)} %get-tuple-element.61.kernel_ref, f32[8,128]{1,0:T(8,128)S(1)} %get-tuple-element.62.passage_ref, ...), custom_call_target="tpu_custom_call" | custom-call | tf_op jit(solution)/shard_map/pallas_call | solution.py:351
  (31 shorter events, 1.1 us)
Async XLA Ops:
  0.6 24.5 %copy-start.2 = (bf16[32,4096]{1,0:T(8,128)(2,1)S(1)}, bf16[32,4096]{1,0:T(8,128)(2,1)}, u32[]{:S(2)}) copy-start(bf16[32,4096]{1,0:T(8,128)(2,1)} %param.3) | copy-start | bytes 786436
  0.6 15.1 %collective-permute-start = (bf16[32,4096]{1,0:T(8,128)(2,1)}, bf16[32,4096]{1,0:T(8,128)(2,1)S(1)}, u32[]{:S(2)}, u32[]{:S(2)}) collective-permute-start(bf16[32,4096]{1,0:T(8,128)(2,1)} %param.3), channel_id=1, source_target_pairs={{1,18},{3,16},{5,22},{7,20},{9,26},{11,24},{13,30},{15,28},{16,3},... | collective-permute-start | bytes 786440 | tf_op jit(solution)/shard_map/ppermute | solution.py:39
  6.8 9.6 %collective-permute-start.1 = (bf16[32,4096]{1,0:T(8,128)(2,1)}, bf16[32,4096]{1,0:T(8,128)(2,1)S(1)}, u32[]{:S(2)}, u32[]{:S(2)}) collective-permute-start(bf16[32,4096]{1,0:T(8,128)(2,1)} %param.3), channel_id=1, source_target_pairs={{0,12},{1,30},{2,14},{3,28},{4,0},{5,18},{6,2},{7,16},{8,4},{9,22}... | collective-permute-start | bytes 786440 | tf_op jit(solution)/shard_map/ppermute | solution.py:39
  9.1 10.9 %collective-permute-start.2 = (bf16[32,4096]{1,0:T(8,128)(2,1)}, bf16[32,4096]{1,0:T(8,128)(2,1)S(1)}, u32[]{:S(2)}, u32[]{:S(2)}) collective-permute-start(bf16[32,4096]{1,0:T(8,128)(2,1)} %param.3), channel_id=1, source_target_pairs={{0,8},{1,26},{2,10},{3,24},{4,12},{5,30},{6,14},{7,28},{8,0},{9,18... | collective-permute-start | bytes 786440 | tf_op jit(solution)/shard_map/ppermute | solution.py:39
  15.8 9.3 %collective-permute-start.3 = (bf16[32,4096]{1,0:T(8,128)(2,1)}, bf16[32,4096]{1,0:T(8,128)(2,1)S(1)}, u32[]{:S(2)}, u32[]{:S(2)}) collective-permute-start(bf16[32,4096]{1,0:T(8,128)(2,1)} %param.3), channel_id=1, source_target_pairs={{0,4},{1,22},{2,6},{3,20},{4,8},{5,26},{6,10},{7,24},{8,12},{9,30}... | collective-permute-start | bytes 786440 | tf_op jit(solution)/shard_map/ppermute | solution.py:39
  15.8 9.6 %collective-permute-start.4 = (f32[512]{0:T(512)}, f32[512]{0:T(512)S(1)}, u32[]{:S(2)}, u32[]{:S(2)}) collective-permute-start(f32[512]{0:T(512)} %param.5), channel_id=1, source_target_pairs={{0,1},{1,0},{2,3},{3,2},{4,5},{5,4},{6,7},{7,6},{8,9},{9,8},{10,11... | collective-permute-start | bytes 6152 | tf_op jit(solution)/shard_map/ppermute | solution.py:39
  15.8 21.4 %collective-permute-start.5 = (bf16[512,4096]{1,0:T(8,128)(2,1)}, bf16[512,4096]{1,0:T(8,128)(2,1)}, u32[]{:S(2)}, u32[]{:S(2)}) collective-permute-start(bf16[512,4096]{1,0:T(8,128)(2,1)} %refs_2_), channel_id=1, source_target_pairs={{0,1},{1,0},{2,3},{3,2},{4,5},{5,4},{6,7},{7,6},{8,9},{9,8},{10,11... | collective-permute-start | bytes 12582920 | tf_op jit(solution)/shard_map/ppermute | solution.py:39
  25.3 11.9 %copy-start.1 = (f32[512]{0:T(512)S(1)}, f32[512]{0:T(512)}, u32[]{:S(2)}) copy-start(f32[512]{0:T(512)} %param.5) | copy-start | bytes 6148
  26.5 8.5 %collective-permute-start.7 = (bf16[64,4096]{1,0:T(8,128)(2,1)}, bf16[64,4096]{1,0:T(8,128)(2,1)S(1)}, u32[]{:S(2)}, u32[]{:S(2)}) collective-permute-start(bf16[64,4096]{1,0:T(8,128)(2,1)} %get-tuple-element.71), channel_id=1, source_target_pairs={{0,96},{1,13},{2,98},{3,15},{4,100},{5,1},{6,102},{7,3},{8,104},{9... | collective-permute-start | bytes 1572872 | tf_op jit(solution)/shard_map/ppermute | solution.py:39
  27.3 9.8 %collective-permute-start.6 = (bf16[64,4096]{1,0:T(8,128)(2,1)}, bf16[64,4096]{1,0:T(8,128)(2,1)S(1)}, u32[]{:S(2)}, u32[]{:S(2)}) collective-permute-start(bf16[64,4096]{1,0:T(8,128)(2,1)} %get-tuple-element.72), channel_id=1, source_target_pairs={{0,32},{1,5},{2,34},{3,7},{4,36},{5,9},{6,38},{7,11},{8,40},{9,13}... | collective-permute-start | bytes 1572872 | tf_op jit(solution)/shard_map/ppermute | solution.py:39
  27.9 13.9 %collective-permute-start.11 = (bf16[64,4096]{1,0:T(8,128)(2,1)}, bf16[64,4096]{1,0:T(8,128)(2,1)S(1)}, u32[]{:S(2)}, u32[]{:S(2)}) collective-permute-start(bf16[64,4096]{1,0:T(8,128)(2,1)} %get-tuple-element.72), channel_id=1, source_target_pairs={{0,96},{1,13},{2,98},{3,15},{4,100},{5,1},{6,102},{7,3},{8,104},{9... | collective-permute-start | bytes 1572872 | tf_op jit(solution)/shard_map/ppermute | solution.py:39
  30.0 12.8 %collective-permute-start.8 = (bf16[64,4096]{1,0:T(8,128)(2,1)}, bf16[64,4096]{1,0:T(8,128)(2,1)S(1)}, u32[]{:S(2)}, u32[]{:S(2)}) collective-permute-start(bf16[64,4096]{1,0:T(8,128)(2,1)} %get-tuple-element.71), channel_id=1, source_target_pairs={{0,32},{1,5},{2,34},{3,7},{4,36},{5,9},{6,38},{7,11},{8,40},{9,13}... | collective-permute-start | bytes 1572872 | tf_op jit(solution)/shard_map/ppermute | solution.py:39
  35.0 11.3 %collective-permute-start.10 = (bf16[64,4096]{1,0:T(8,128)(2,1)S(1)}, bf16[64,4096]{1,0:T(8,128)(2,1)}, u32[]{:S(2)}, u32[]{:S(2)}) collective-permute-start(bf16[64,4096]{1,0:T(8,128)(2,1)S(1)} %collective-permute-done.7.refs_10_), channel_id=1, source_target_pairs={{0,96},{1,13},{2,98},{3,15},{4,100},{5,1},{6,102},{7,3},{8,104},{9... | collective-permute-start | bytes 1572872 | tf_op jit(solution)/shard_map/ppermute | solution.py:39
  37.1 11.0 %collective-permute-start.9 = (bf16[64,4096]{1,0:T(8,128)(2,1)S(1)}, bf16[64,4096]{1,0:T(8,128)(2,1)}, u32[]{:S(2)}, u32[]{:S(2)}) collective-permute-start(bf16[64,4096]{1,0:T(8,128)(2,1)S(1)} %collective-permute-done.6.refs_5_), channel_id=1, source_target_pairs={{0,32},{1,5},{2,34},{3,7},{4,36},{5,9},{6,38},{7,11},{8,40},{9,13}... | collective-permute-start | bytes 1572872 | tf_op jit(solution)/shard_map/ppermute | solution.py:39
  37.2 2.2 %copy-start = (bf16[512,4096]{1,0:T(8,128)(2,1)S(1)}, bf16[512,4096]{1,0:T(8,128)(2,1)}, u32[]{:S(2)}) copy-start(bf16[512,4096]{1,0:T(8,128)(2,1)} %refs_2_) | copy-start | bytes 12582916
  54.4 20.6 %collective-permute-start.14 = (bf16[384,4096]{1,0:T(8,128)(2,1)S(1)}, bf16[384,4096]{1,0:T(8,128)(2,1)S(1)}, u32[]{:S(2)}, u32[]{:S(2)}) collective-permute-start(bf16[384,4096]{1,0:T(8,128)(2,1)S(1)} %get-tuple-element.65.refs_1_), channel_id=1, source_target_pairs={{0,1},{1,0},{2,3},{3,2},{4,5},{5,4},{6,7},{7,6},{8,9},{9,8},{10,11... | collective-permute-start | bytes 9437192 | tf_op jit(solution)/shard_map/ppermute | solution.py:39
  54.5 18.8 %collective-permute-start.12 = (f32[4,512,128]{2,1,0:T(8,128)S(1)}, f32[4,512,128]{2,1,0:T(8,128)S(1)}, u32[]{:S(2)}, u32[]{:S(2)}) collective-permute-start(f32[4,512,128]{2,1,0:T(8,128)S(1)} %get-tuple-element.57), channel_id=1, source_target_pairs={{0,1},{1,0},{2,3},{3,2},{4,5},{5,4},{6,7},{7,6},{8,9},{9,8},{10,11... | collective-permute-start | bytes 3145736 | tf_op jit(solution)/shard_map/ppermute | solution.py:39
  55.0 20.0 %collective-permute-start.13 = (bf16[128,4096]{1,0:T(8,128)(2,1)S(1)}, bf16[128,4096]{1,0:T(8,128)(2,1)S(1)}, u32[]{:S(2)}, u32[]{:S(2)}) collective-permute-start(bf16[128,4096]{1,0:T(8,128)(2,1)S(1)} %bitcast.29), channel_id=1, source_target_pairs={{0,1},{1,0},{2,3},{3,2},{4,5},{5,4},{6,7},{7,6},{8,9},{9,8},{10,11... | collective-permute-start | bytes 3145736 | tf_op jit(solution)/shard_map/ppermute | solution.py:39

commit v8 on v7

--- a/solution.py
+++ b/solution.py
@@ -54,8 +54,19 @@
     return lax.all_to_all(copies, EVERY, 0, 0)
 
 
-def turned(rows, places):
-    return lax.dynamic_slice_in_dim(jnp.concatenate([rows, rows], 0), 4 - places, 4, 0)
+def rolled(order_ref, first, rows):
+    low = lax.broadcasted_iota(jnp.int32, rows.shape, 0) < 4
+    return jnp.where(
+        low, pltpu.roll(rows, order_ref[first], 1), pltpu.roll(rows, order_ref[first + 1], 1)
+    )
+
+
+def to_common(order_ref, rows):
+    return rolled(order_ref, CHUNKS + 2, rows)
+
+
+def to_local(order_ref, rows):
+    return rolled(order_ref, CHUNKS + 4, rows)
 
 
 def stage_kernel(*refs):
@@ -80,10 +91,10 @@
 
 
 def logits_kernel(factor, order_ref, *refs):
-    duals_refs, centroids_refs, piece_refs = refs[:2], refs[2:4], refs[4:11]
-    *logits_refs, out_ref, arrived_ref, rows_ref, sem = refs[11:]
+    duals_refs, centroids_refs, piece_refs = refs[:2], refs[2:4], refs[4:12]
+    *logits_refs, out_ref, arrived_ref, rows_ref, sem = refs[12:]
     start = 0
-    for ref in piece_refs[1:]:
+    for ref in piece_refs:
         size = ref.shape[0]
         pltpu.make_async_copy(ref, arrived_ref.at[pl.ds(start, size)], sem).start()
         start += size
@@ -103,7 +114,8 @@
     logsum = top + jnp.log(sum(total * jnp.exp(own - top) for own, total in zip(tops, totals)))
     for k in range(4):
         rows_ref[pl.ds(lax.rem(order_ref[k], 4), 1), :] = logsum[:, k * LANES : (k + 1) * LANES]
-    send_sums(rows_ref, out_ref)
+    core = lax.div(order_ref[0], 4)
+    send_rows(pltpu.roll(rows_ref[...], order_ref[CHUNKS + 2 + core], 1), out_ref)
     pltpu.make_async_copy(arrived_ref, arrived_ref, sem).wait()
 
 
@@ -139,15 +151,15 @@
             logits,
             logits,
             jax.ShapeDtypeStruct((devices, 4, LANES), f32),
-            jax.ShapeDtypeStruct((3 * LANES, depth), pieces[0].dtype),
+            jax.ShapeDtypeStruct((4 * LANES, depth), pieces[0].dtype),
         ],
         scratch_shapes=[pltpu.VMEM((4, LANES), f32), pltpu.SemaphoreType.DMA],
         compiler_params=pltpu.CompilerParams(vmem_limit_bytes=24 * 2**20),
     )(order, *columns, *centroids, *[held(array) for array in pieces])
 
 
-def send_sums(sums_ref, out_ref):
-    out_ref[...] = jnp.broadcast_to(sums_ref[...].astype(out_ref.dtype)[None], out_ref.shape)
+def send_rows(rows, out_ref):
+    out_ref[...] = jnp.broadcast_to(rows.astype(out_ref.dtype)[None], out_ref.shape)
 
 
 def first_kernel(order_ref, parts_ref, *refs):
@@ -167,11 +179,12 @@
         passage_ref[core * 4 : core * 4 + 4, :] = -math.log(PASSAGES) - (
             top + jnp.log(jnp.sum(jnp.exp(part - top[None]), axis=0))
         )
+    sums_ref[...] = to_local(order_ref, passage_ref[...])
     peak = None
     for k in range(CHUNKS):
         if k in starts:
             copies[starts.index(k)].wait()
-        terms = kernel_ref[k] + passage_ref[pl.ds(order_ref[k], 1), :]
+        terms = kernel_ref[k] + sums_ref[pl.ds(order_ref[k], 1), :]
         kernel_ref[k] = terms
         peak = terms if peak is None else jnp.maximum(peak, terms)
     peak = jnp.max(peak, axis=1, keepdims=True)
@@ -187,7 +200,7 @@
         terms = kernel_ref[k] * inverse
         kernel_ref[k] = terms
         sums_ref[pl.ds(order_ref[k], 1), :] = jnp.sum(terms, axis=0, keepdims=True)
-    send_sums(sums_ref, out_ref)
+    send_rows(to_common(order_ref, sums_ref[...]), out_ref)
 
 
 def row_scale_of(parts_ref):
@@ -204,13 +217,13 @@
 
 
 def middle_kernel(order_ref, parts_ref, kernel_ref, out_ref, sums_ref):
-    sums_ref[...] = row_scale_of(parts_ref)
+    sums_ref[...] = to_local(order_ref, row_scale_of(parts_ref))
     scale = 1.0 / column_sums(order_ref, kernel_ref, sums_ref)
     for k in range(CHUNKS):
         sums_ref[pl.ds(order_ref[k], 1), :] = jnp.sum(
             kernel_ref[k] * scale, axis=0, keepdims=True
         )
-    send_sums(sums_ref, out_ref)
+    send_rows(to_common(order_ref, sums_ref[...]), out_ref)
 
 
 def last_kernel(order_ref, parts_ref, kernel_ref, passage_ref, centroid_ref, *refs):
@@ -228,7 +241,8 @@
             ).start()
             start += size
 
-    scale_ref[...] = row_scale_of(parts_ref)
+    scale = row_scale_of(parts_ref)
+    scale_ref[...] = to_local(order_ref, scale)
     total = column_sums(order_ref, kernel_ref, scale_ref)
     inverse = 1.0 / total
     for k in range(CHUNKS):
@@ -257,7 +271,7 @@
                 duals_ref[pl.ds(k, 1), :] = jnp.sum(
                     jnp.where(diagonal, column, 0.0), axis=0, keepdims=True
                 )
-            scale_ref[...] = passage_ref[...] + jnp.log(scale_ref[...])
+            scale_ref[...] = passage_ref[...] + jnp.log(scale)
             own = pltpu.roll(scale_ref[pl.ds(order_ref[CHUNKS], 1), :], LANES - order_ref[CHUNKS + 1], 1)
             own_ref[...] = own[:, : own_ref.shape[1]]
         if tile >= 2:
@@ -294,34 +308,32 @@
 
         return move(passages, target)
 
-    ring = [jnp.where(h == c, passages, fetch(0)), fetch(1), fetch(2), fetch(3)]
-    ring = turned(jnp.stack(ring), first).reshape(4 * local_rows, depth)
-    near_duals = to_sibling(dual_init)
-    ring, near_duals = lax.optimization_barrier((ring, near_duals))
-
-    half = ring.shape[0] // 2
-    top, bottom = ring[:half], ring[half:]
+    mine = jnp.where(h == c, passages, fetch(0))
+    top = jnp.concatenate([mine, fetch(1)], axis=0)
+    bottom = jnp.concatenate([fetch(2), fetch(3)], axis=0)
+    bottom, near_duals = lax.optimization_barrier((bottom, to_sibling(dual_init)))
     top_before, bottom_after = along_second(top, 1), along_second(bottom, -1)
     bottom_before, top_after = along_second(bottom, 1), along_second(top, -1)
     top_across, bottom_across = along_second(top_before, 1), along_second(bottom_after, -1)
-    arrived = [top_before, bottom_before, top_across, bottom_across, top_after, bottom_after]
+    arrived = [top, bottom, top_before, bottom_before, top_across, bottom_across, top_after, bottom_after]
     order = [c * 4 + (second + k) % 4 for k in OWN]
     order += [(1 - c) * 4 + (first + k) % 4 for k in OWN]
     row, lane = jnp.where(h == 0, z, 4 + x), jnp.where(h == 0, x, z) * local_rows
-    order = jnp.stack(order + [row, lane]).astype(jnp.int32)
+    order += [row, lane] + [x * local_rows, z * local_rows]
+    order += [(4 - x) % 4 * local_rows, (4 - z) % 4 * local_rows]
+    order = jnp.stack(order).astype(jnp.int32)
 
     pairs, _ = lax.optimization_barrier(
         ((dual_init, near_duals, centroids, to_sibling(centroids)), (top_before, bottom_after))
     )
     *columns, near, sibling = staged(pairs[:2], pairs[2:])
     arrived, near, sibling = lax.optimization_barrier((arrived, near, sibling))
-    *logits, parts, arrived = chunk_logits(factor, order, columns, (near, sibling), [ring] + arrived)
+    *logits, parts, arrived = chunk_logits(factor, order, columns, (near, sibling), arrived)
     logits = [logits[0], to_sibling(logits[1])]
     span = LANES
     f32 = jnp.float32
     parts = to_every(parts)
-    own = [ring, arrived]
-    pieces = own + [to_sibling(chunk) for chunk in own]
+    pieces = [arrived, to_sibling(arrived)]
 
     sent = jax.ShapeDtypeStruct((devices, CHUNKS, span), jnp.bfloat16)
     block = pl.BlockSpec((devices, CHUNKS, span), lambda: (0, 0, 0))

time: 115 us -> 114 us (level)
  waiting for transfers between devices: 20 us -> 15 us
  blocking collectives: 48.6 us -> 50.8 us
    ppermute x15 -> x14, waiting for transfers between devices: 20 us -> 15 us  [move(): return lax.ppermute(value, EVERY, pairs)]
    all_to_all x3, blocking collectives: 48.6 us -> 50.8 us  [to_every(): return lax.all_to_all(copies, EVERY, 0, 0)]
    ppermute x15 -> x14, starting transfers between devices: 21.9 us -> 22.7 us  [move(): return lax.ppermute(value, EVERY, pairs)]
    unnamed x11 -> x4, local copies, waits for them, and re-layouts: 2.29 us -> 2.86 us
  transfers between devices with their start and end apart: 15 -> 14, of which waited for: 6 -> 5; matrix products, arithmetic and copies ran while one was open for 1% -> 0% of each run, Pallas kernels for 4% -> 4%
where the time goes in v8:
time: 114 us; the launch traced here: 113 us
  blocking collectives  50.8 us (45%)
  starting transfers between devices  22.7 us (20%)
  Pallas kernels  20.9 us (18%)
  waiting for transfers between devices  15 us (13%)
  local copies, waits for them, and re-layouts  2.95 us (3%)
    all_to_all x3, blocking collectives, to_every(): return lax.all_to_all(copies, EVERY, 0, 0)  50.8 us
    ppermute x14, starting transfers between devices, move(): return lax.ppermute(value, EVERY, pairs)  22.7 us
    ppermute x14, waiting for transfers between devices, move(): return lax.ppermute(value, EVERY, pairs)  15 us
    pallas_call x1, Pallas kernels, body(): pl.pallas_call(last_kernel, in_specs=[SMEM] + [VMEM] * 4 + [ANY] * len(pi...  8.86 us
    pallas_call x1, Pallas kernels, chunk_logits(): pl.pallas_call(functools.partial(logits_kernel, factor), in_specs=[SMEM]...  6.53 us
    unnamed x4, local copies, waits for them, and re-layouts  2.86 us
    pallas_call x1, Pallas kernels, staged(): pl.pallas_call(stage_kernel, in_specs=[VMEM] * 2 + [ANY] * 2, out_specs=[...  2.46 us
  transfers between devices with their start and end apart: 14, of which 5 were waited for; matrix products, arithmetic and copies ran while one was open for 0% of the time, Pallas kernels for 4%

profile of v8, /device:TPU:1, one launch (start us, length us, event | category | flops | bytes accessed | tf_op | source)
XLA Modules:
  0.0 113.3 jit_solution(12183945494861105764)
XLA Ops:
  0.6 1.5 %collective-permute-start.3 = (bf16[512,4096]{1,0:T(8,128)(2,1)}, bf16[512,4096]{1,0:T(8,128)(2,1)}, u32[]{:S(2)}, u32[]{:S(2)}) collective-permute-start(bf16[512,4096]{1,0:T(8,128)(2,1)} %refs_2_), channel_id=1, source_target_pairs={{0,1},{1,0},{2,3},{3,2},{4,5},{5,4},{6,7},{7,6},{8,9},{9,8},{10,11... | collective-permute-start | bytes 12582920 | tf_op jit(solution)/shard_map/ppermute | solution.py:39
  2.1 4.6 %collective-permute-start.4 = (bf16[32,4096]{1,0:T(8,128)(2,1)}, bf16[32,4096]{1,0:T(8,128)(2,1)S(1)}, u32[]{:S(2)}, u32[]{:S(2)}) collective-permute-start(bf16[32,4096]{1,0:T(8,128)(2,1)} %param.3), channel_id=1, source_target_pairs={{1,18},{3,16},{5,22},{7,20},{9,26},{11,24},{13,30},{15,28},{16,3},... | collective-permute-start | bytes 786440 | tf_op jit(solution)/shard_map/ppermute | solution.py:39
  6.8 1.3 %collective-permute-start.1 = (bf16[32,4096]{1,0:T(8,128)(2,1)}, bf16[32,4096]{1,0:T(8,128)(2,1)S(1)}, u32[]{:S(2)}, u32[]{:S(2)}) collective-permute-start(bf16[32,4096]{1,0:T(8,128)(2,1)} %param.3), channel_id=1, source_target_pairs={{0,4},{1,22},{2,6},{3,20},{4,8},{5,26},{6,10},{7,24},{8,12},{9,30}... | collective-permute-start | bytes 786440 | tf_op jit(solution)/shard_map/ppermute | solution.py:39
  8.1 5.5 %collective-permute-start = (bf16[32,4096]{1,0:T(8,128)(2,1)}, bf16[32,4096]{1,0:T(8,128)(2,1)S(1)}, u32[]{:S(2)}, u32[]{:S(2)}) collective-permute-start(bf16[32,4096]{1,0:T(8,128)(2,1)} %param.3), channel_id=1, source_target_pairs={{0,8},{1,26},{2,10},{3,24},{4,12},{5,30},{6,14},{7,28},{8,0},{9,18... | collective-permute-start | bytes 786440 | tf_op jit(solution)/shard_map/ppermute | solution.py:39
  13.6 1.9 %collective-permute-start.5 = (bf16[32,4096]{1,0:T(8,128)(2,1)}, bf16[32,4096]{1,0:T(8,128)(2,1)S(1)}, u32[]{:S(2)}, u32[]{:S(2)}) collective-permute-start(bf16[32,4096]{1,0:T(8,128)(2,1)} %param.3), channel_id=1, source_target_pairs={{0,12},{1,30},{2,14},{3,28},{4,0},{5,18},{6,2},{7,16},{8,4},{9,22}... | collective-permute-start | bytes 786440 | tf_op jit(solution)/shard_map/ppermute | solution.py:39
  15.6 2.0 %collective-permute-done.1 = bf16[32,4096]{1,0:T(8,128)(2,1)S(1)} collective-permute-done((bf16[32,4096]{1,0:T(8,128)(2,1)}, bf16[32,4096]{1,0:T(8,128)(2,1)S(1)}, u32[]{:S(2)}, u32[]{:S(2)}) %collective-permute-start.1) | collective-permute-done | bytes 262176 | tf_op jit(solution)/shard_map/ppermute | solution.py:39
  17.6 3.6 %collective-permute-done = bf16[32,4096]{1,0:T(8,128)(2,1)S(1)} collective-permute-done((bf16[32,4096]{1,0:T(8,128)(2,1)}, bf16[32,4096]{1,0:T(8,128)(2,1)S(1)}, u32[]{:S(2)}, u32[]{:S(2)}) %collective-permute-start) | collective-permute-done | bytes 262176 | tf_op jit(solution)/shard_map/ppermute | solution.py:39
  21.3 1.2 %collective-permute-done.5 = bf16[32,4096]{1,0:T(8,128)(2,1)S(1)} collective-permute-done((bf16[32,4096]{1,0:T(8,128)(2,1)}, bf16[32,4096]{1,0:T(8,128)(2,1)S(1)}, u32[]{:S(2)}, u32[]{:S(2)}) %collective-permute-start.5) | collective-permute-done | bytes 262176 | tf_op jit(solution)/shard_map/ppermute | solution.py:39
  22.5 1.2 %collective-permute-start.6 = (bf16[64,4096]{1,0:T(8,128)(2,1)S(1)}, bf16[64,4096]{1,0:T(8,128)(2,1)S(1)}, u32[]{:S(2)}, u32[]{:S(2)}) collective-permute-start(bf16[64,4096]{1,0:T(8,128)(2,1)S(1)} %pad_maximum_fusion.1.refs_4_), channel_id=1, source_target_pairs={{0,32},{1,5},{2,34},{3,7},{4,36},{5,9},{6,38},{7,11},{8,40},{9,13}... | collective-permute-start | bytes 1572872 | tf_op jit(solution)/shard_map/ppermute | solution.py:39
  23.7 1.8 %collective-permute-start.7 = (bf16[64,4096]{1,0:T(8,128)(2,1)S(1)}, bf16[64,4096]{1,0:T(8,128)(2,1)S(1)}, u32[]{:S(2)}, u32[]{:S(2)}) collective-permute-start(bf16[64,4096]{1,0:T(8,128)(2,1)S(1)} %pad_maximum_fusion.refs_5_), channel_id=1, source_target_pairs={{0,96},{1,13},{2,98},{3,15},{4,100},{5,1},{6,102},{7,3},{8,104},{9... | collective-permute-start | bytes 1572872 | tf_op jit(solution)/shard_map/ppermute | solution.py:39
  25.5 1.4 %collective-permute-start.11 = (bf16[64,4096]{1,0:T(8,128)(2,1)S(1)}, bf16[64,4096]{1,0:T(8,128)(2,1)S(1)}, u32[]{:S(2)}, u32[]{:S(2)}) collective-permute-start(bf16[64,4096]{1,0:T(8,128)(2,1)S(1)} %pad_maximum_fusion.1.refs_4_), channel_id=1, source_target_pairs={{0,96},{1,13},{2,98},{3,15},{4,100},{5,1},{6,102},{7,3},{8,104},{9... | collective-permute-start | bytes 1572872 | tf_op jit(solution)/shard_map/ppermute | solution.py:39
  27.0 5.3 %collective-permute-done.6.refs_6_ = bf16[64,4096]{1,0:T(8,128)(2,1)S(1)} collective-permute-done((bf16[64,4096]{1,0:T(8,128)(2,1)S(1)}, bf16[64,4096]{1,0:T(8,128)(2,1)S(1)}, u32[]{:S(2)}, u32[]{:S(2)}) %collective-permute-start.6) | collective-permute-done | bytes 524320 | tf_op jit(solution)/shard_map/ppermute | solution.py:39
  32.3 2.7 %collective-permute-start.10 = (bf16[64,4096]{1,0:T(8,128)(2,1)S(1)}, bf16[64,4096]{1,0:T(8,128)(2,1)}, u32[]{:S(2)}, u32[]{:S(2)}) collective-permute-start(bf16[64,4096]{1,0:T(8,128)(2,1)S(1)} %collective-permute-done.7.refs_11_), channel_id=1, source_target_pairs={{0,96},{1,13},{2,98},{3,15},{4,100},{5,1},{6,102},{7,3},{8,104},{9... | collective-permute-start | bytes 1572872 | tf_op jit(solution)/shard_map/ppermute | solution.py:39
  35.1 2.2 %copy-done = bf16[512,4096]{1,0:T(8,128)(2,1)S(1)} copy-done((bf16[512,4096]{1,0:T(8,128)(2,1)S(1)}, bf16[512,4096]{1,0:T(8,128)(2,1)}, u32[]{:S(2)}) %copy-start) | copy-done | bytes 4194328
  37.3 0.7 copy-done.1
  38.0 2.5 %shard_map.58 = (f32[512,1]{1,0:T(8,128)S(1)}, f32[512,1]{1,0:T(8,128)S(1)}, bf16[512,4096]{1,0:T(8,128)(2,1)S(1)}, bf16[512,4096]{1,0:T(8,128)(2,1)S(1)}) custom-call(f32[4,128]{1,0:T(4,128)S(1)} %bitcast.18, f32[4,128]{1,0:T(4,128)S(1)} %bitcast.19, bf16[512,4096]{1,0:T(8,128)(2,1)S(1)} %copy-done, bf16[512,4096]{1,0:T(8,128)(2,1)} %collective-permute-done.3.refs_3_), custom_call_target="tpu_custom_call" | custom-call | tf_op jit(solution)/shard_map/pallas_call | solution.py:130
  40.5 2.8 %collective-permute-done.9.refs_8_ = bf16[64,4096]{1,0:T(8,128)(2,1)} collective-permute-done((bf16[64,4096]{1,0:T(8,128)(2,1)S(1)}, bf16[64,4096]{1,0:T(8,128)(2,1)}, u32[]{:S(2)}, u32[]{:S(2)}) %collective-permute-start.9) | collective-permute-done | bytes 524320 | tf_op jit(solution)/shard_map/ppermute | solution.py:39
  43.3 6.5 %shard_map.59 = (f32[4,512,128]{2,1,0:T(8,128)S(1)}, f32[4,512,128]{2,1,0:T(8,128)S(1)}, f32[128,4,128]{2,1,0:T(4,128)S(1)}, bf16[512,4096]{1,0:T(8,128)(2,1)S(1)}) custom-call(s32[14]{0:T(128)S(1)} %stack.59.order_ref, f32[512,1]{1,0:T(8,128)S(1)} %get-tuple-element.43.refs_0_, f32[512,1]{1,0:T(8,128)S(1)} %get-tuple-element.44.refs_1_, ...), custom_call_target="tpu_custom_call" | custom-call | tf_op jit(solution)/shard_map/pallas_call | solution.py:146
  50.5 20.4 %all_to_all.15.parts_ref = f32[128,4,128]{2,1,0:T(4,128)S(1)} all-to-all(f32[128,4,128]{2,1,0:T(4,128)S(1)} %get-tuple-element.57), channel_id=1, replica_groups=mesh['psg'=32,'cen'=4] {'psg','cen'}, dimensions={0} | all-to-all | bytes 524288 | tf_op jit(solution)/shard_map/all_to_all | solution.py:54
  70.9 1.8 %shard_map.60 = (f32[8,512,128]{2,1,0:T(8,128)S(1)}, f32[8,128]{1,0:T(8,128)S(1)}, f32[512,1]{1,0:T(8,128)S(1)}, bf16[128,8,128]{2,1,0:T(8,128)(2,1)S(1)}) custom-call(s32[14]{0:T(128)S(1)} %stack.59.order_ref, f32[128,4,128]{2,1,0:T(4,128)S(1)} %all_to_all.15.parts_ref, f32[4,512,128]{2,1,0:T(8,128)S(1)} %get-tuple-element.58.refs_0_, ...), custom_call_target="tpu_custom_call" | custom-call | tf_op jit(solution)/shard_map/pallas_call | solution.py:341
  72.8 15.2 %all_to_all.16.parts_ref = bf16[128,8,128]{2,1,0:T(8,128)(2,1)S(1)} all-to-all(bf16[128,8,128]{2,1,0:T(8,128)(2,1)S(1)} %get-tuple-element.62), channel_id=1, replica_groups=mesh['psg'=32,'cen'=4] {'psg','cen'}, dimensions={0} | all-to-all | bytes 524288 | tf_op jit(solution)/shard_map/all_to_all | solution.py:54
  87.9 1.2 %shard_map.61 = bf16[128,8,128]{2,1,0:T(8,128)(2,1)S(1)} custom-call(s32[14]{0:T(128)S(1)} %stack.59.order_ref, bf16[128,8,128]{2,1,0:T(8,128)(2,1)S(1)} %all_to_all.16.parts_ref, f32[8,512,128]{2,1,0:T(8,128)S(1)} %get-tuple-element.63.kernel_ref), custom_call_target="tpu_custom_call" | custom-call | tf_op jit(solution)/shard_map/pallas_call | solution.py:355
  89.1 15.2 %all_to_all.17.parts_ref = bf16[128,8,128]{2,1,0:T(8,128)(2,1)S(1)} all-to-all(bf16[128,8,128]{2,1,0:T(8,128)(2,1)S(1)} %shard_map.61), channel_id=1, replica_groups=mesh['psg'=32,'cen'=4] {'psg','cen'}, dimensions={0} | all-to-all | bytes 524288 | tf_op jit(solution)/shard_map/all_to_all | solution.py:54
  104.2 8.9 %shard_map.62 = (bf16[512,4096]{1,0:T(8,128)(2,1)}, f32[1,32]{1,0:T(1,128)}, f32[4,128]{1,0:T(4,128)}) custom-call(s32[14]{0:T(128)S(1)} %stack.59.order_ref, bf16[128,8,128]{2,1,0:T(8,128)(2,1)S(1)} %all_to_all.17.parts_ref, f32[8,512,128]{2,1,0:T(8,128)S(1)} %get-tuple-element.63.kernel_ref, f32[8,128]{1,0:T(8,128)S(1)} %get-tuple-element.64.passage_ref, ...), custom_call_target="tpu_custom_call" | custom-call | tf_op jit(solution)/shard_map/pallas_call | solution.py:363
  (20 shorter events, 0.9 us)
Async XLA Ops:
  0.6 34.5 %collective-permute-start.3 = (bf16[512,4096]{1,0:T(8,128)(2,1)}, bf16[512,4096]{1,0:T(8,128)(2,1)}, u32[]{:S(2)}, u32[]{:S(2)}) collective-permute-start(bf16[512,4096]{1,0:T(8,128)(2,1)} %refs_2_), channel_id=1, source_target_pairs={{0,1},{1,0},{2,3},{3,2},{4,5},{5,4},{6,7},{7,6},{8,9},{9,8},{10,11... | collective-permute-start | bytes 12582920 | tf_op jit(solution)/shard_map/ppermute | solution.py:39
  2.1 13.4 %collective-permute-start.4 = (bf16[32,4096]{1,0:T(8,128)(2,1)}, bf16[32,4096]{1,0:T(8,128)(2,1)S(1)}, u32[]{:S(2)}, u32[]{:S(2)}) collective-permute-start(bf16[32,4096]{1,0:T(8,128)(2,1)} %param.3), channel_id=1, source_target_pairs={{1,18},{3,16},{5,22},{7,20},{9,26},{11,24},{13,30},{15,28},{16,3},... | collective-permute-start | bytes 786440 | tf_op jit(solution)/shard_map/ppermute | solution.py:39
  6.8 10.8 %collective-permute-start.1 = (bf16[32,4096]{1,0:T(8,128)(2,1)}, bf16[32,4096]{1,0:T(8,128)(2,1)S(1)}, u32[]{:S(2)}, u32[]{:S(2)}) collective-permute-start(bf16[32,4096]{1,0:T(8,128)(2,1)} %param.3), channel_id=1, source_target_pairs={{0,4},{1,22},{2,6},{3,20},{4,8},{5,26},{6,10},{7,24},{8,12},{9,30}... | collective-permute-start | bytes 786440 | tf_op jit(solution)/shard_map/ppermute | solution.py:39
  8.1 13.2 %collective-permute-start = (bf16[32,4096]{1,0:T(8,128)(2,1)}, bf16[32,4096]{1,0:T(8,128)(2,1)S(1)}, u32[]{:S(2)}, u32[]{:S(2)}) collective-permute-start(bf16[32,4096]{1,0:T(8,128)(2,1)} %param.3), channel_id=1, source_target_pairs={{0,8},{1,26},{2,10},{3,24},{4,12},{5,30},{6,14},{7,28},{8,0},{9,18... | collective-permute-start | bytes 786440 | tf_op jit(solution)/shard_map/ppermute | solution.py:39
  13.6 8.9 %collective-permute-start.5 = (bf16[32,4096]{1,0:T(8,128)(2,1)}, bf16[32,4096]{1,0:T(8,128)(2,1)S(1)}, u32[]{:S(2)}, u32[]{:S(2)}) collective-permute-start(bf16[32,4096]{1,0:T(8,128)(2,1)} %param.3), channel_id=1, source_target_pairs={{0,12},{1,30},{2,14},{3,28},{4,0},{5,18},{6,2},{7,16},{8,4},{9,22}... | collective-permute-start | bytes 786440 | tf_op jit(solution)/shard_map/ppermute | solution.py:39
  15.5 5.7 %collective-permute-start.2 = (f32[512]{0:T(512)}, f32[512]{0:T(512)S(1)}, u32[]{:S(2)}, u32[]{:S(2)}) collective-permute-start(f32[512]{0:T(512)} %param.5), channel_id=1, source_target_pairs={{0,1},{1,0},{2,3},{3,2},{4,5},{5,4},{6,7},{7,6},{8,9},{9,8},{10,11... | collective-permute-start | bytes 6152 | tf_op jit(solution)/shard_map/ppermute | solution.py:39
  22.5 9.8 %collective-permute-start.6 = (bf16[64,4096]{1,0:T(8,128)(2,1)S(1)}, bf16[64,4096]{1,0:T(8,128)(2,1)S(1)}, u32[]{:S(2)}, u32[]{:S(2)}) collective-permute-start(bf16[64,4096]{1,0:T(8,128)(2,1)S(1)} %pad_maximum_fusion.1.refs_4_), channel_id=1, source_target_pairs={{0,32},{1,5},{2,34},{3,7},{4,36},{5,9},{6,38},{7,11},{8,40},{9,13}... | collective-permute-start | bytes 1572872 | tf_op jit(solution)/shard_map/ppermute | solution.py:39
  23.7 8.6 %collective-permute-start.7 = (bf16[64,4096]{1,0:T(8,128)(2,1)S(1)}, bf16[64,4096]{1,0:T(8,128)(2,1)S(1)}, u32[]{:S(2)}, u32[]{:S(2)}) collective-permute-start(bf16[64,4096]{1,0:T(8,128)(2,1)S(1)} %pad_maximum_fusion.refs_5_), channel_id=1, source_target_pairs={{0,96},{1,13},{2,98},{3,15},{4,100},{5,1},{6,102},{7,3},{8,104},{9... | collective-permute-start | bytes 1572872 | tf_op jit(solution)/shard_map/ppermute | solution.py:39
  25.5 15.0 %collective-permute-start.11 = (bf16[64,4096]{1,0:T(8,128)(2,1)S(1)}, bf16[64,4096]{1,0:T(8,128)(2,1)S(1)}, u32[]{:S(2)}, u32[]{:S(2)}) collective-permute-start(bf16[64,4096]{1,0:T(8,128)(2,1)S(1)} %pad_maximum_fusion.1.refs_4_), channel_id=1, source_target_pairs={{0,96},{1,13},{2,98},{3,15},{4,100},{5,1},{6,102},{7,3},{8,104},{9... | collective-permute-start | bytes 1572872 | tf_op jit(solution)/shard_map/ppermute | solution.py:39
  26.9 13.6 %collective-permute-start.8 = (bf16[64,4096]{1,0:T(8,128)(2,1)S(1)}, bf16[64,4096]{1,0:T(8,128)(2,1)S(1)}, u32[]{:S(2)}, u32[]{:S(2)}) collective-permute-start(bf16[64,4096]{1,0:T(8,128)(2,1)S(1)} %pad_maximum_fusion.refs_5_), channel_id=1, source_target_pairs={{0,32},{1,5},{2,34},{3,7},{4,36},{5,9},{6,38},{7,11},{8,40},{9,13}... | collective-permute-start | bytes 1572872 | tf_op jit(solution)/shard_map/ppermute | solution.py:39
  32.3 11.0 %collective-permute-start.9 = (bf16[64,4096]{1,0:T(8,128)(2,1)S(1)}, bf16[64,4096]{1,0:T(8,128)(2,1)}, u32[]{:S(2)}, u32[]{:S(2)}) collective-permute-start(bf16[64,4096]{1,0:T(8,128)(2,1)S(1)} %collective-permute-done.6.refs_6_), channel_id=1, source_target_pairs={{0,32},{1,5},{2,34},{3,7},{4,36},{5,9},{6,38},{7,11},{8,40},{9,13}... | collective-permute-start | bytes 1572872 | tf_op jit(solution)/shard_map/ppermute | solution.py:39
  32.3 11.0 %collective-permute-start.10 = (bf16[64,4096]{1,0:T(8,128)(2,1)S(1)}, bf16[64,4096]{1,0:T(8,128)(2,1)}, u32[]{:S(2)}, u32[]{:S(2)}) collective-permute-start(bf16[64,4096]{1,0:T(8,128)(2,1)S(1)} %collective-permute-done.7.refs_11_), channel_id=1, source_target_pairs={{0,96},{1,13},{2,98},{3,15},{4,100},{5,1},{6,102},{7,3},{8,104},{9... | collective-permute-start | bytes 1572872 | tf_op jit(solution)/shard_map/ppermute | solution.py:39
  35.1 2.2 %copy-start = (bf16[512,4096]{1,0:T(8,128)(2,1)S(1)}, bf16[512,4096]{1,0:T(8,128)(2,1)}, u32[]{:S(2)}) copy-start(bf16[512,4096]{1,0:T(8,128)(2,1)} %refs_2_) | copy-start | bytes 12582916
  37.3 0.7 copy-start.1
  49.9 22.9 %collective-permute-start.13 = (bf16[512,4096]{1,0:T(8,128)(2,1)S(1)}, bf16[512,4096]{1,0:T(8,128)(2,1)S(1)}, u32[]{:S(2)}, u32[]{:S(2)}) collective-permute-start(bf16[512,4096]{1,0:T(8,128)(2,1)S(1)} %get-tuple-element.66.refs_0_), channel_id=1, source_target_pairs={{0,1},{1,0},{2,3},{3,2},{4,5},{5,4},{6,7},{7,6},{8,9},{9,8},{10,11... | collective-permute-start | bytes 12582920 | tf_op jit(solution)/shard_map/ppermute | solution.py:39
  50.0 20.9 %collective-permute-start.12 = (f32[4,512,128]{2,1,0:T(8,128)S(1)}, f32[4,512,128]{2,1,0:T(8,128)S(1)}, u32[]{:S(2)}, u32[]{:S(2)}) collective-permute-start(f32[4,512,128]{2,1,0:T(8,128)S(1)} %get-tuple-element.59), channel_id=1, source_target_pairs={{0,1},{1,0},{2,3},{3,2},{4,5},{5,4},{6,7},{7,6},{8,9},{9,8},{10,11... | collective-permute-start | bytes 3145736 | tf_op jit(solution)/shard_map/ppermute | solution.py:39

commit v9 on v8

--- a/solution.py
+++ b/solution.py
@@ -13,7 +13,7 @@
 EVERY = ("psg", "cen")
 X, Z, HALVES = 4, 4, 2
 CHUNKS = 8
-OWN = (0, 3, 2, 1)
+OWN = (0, 3, 1, 2)
 LANES = 128
 WIDTH = 2048
 PARTS = 16
@@ -69,13 +69,60 @@
     return rolled(order_ref, CHUNKS + 4, rows)
 
 
-def stage_kernel(*refs):
-    rows_refs, centroids_refs, columns_refs, held_refs, sem = refs[:2], refs[2:4], refs[4:6], refs[6:8], refs[8]
-    for source, target in zip(centroids_refs, held_refs):
-        size = target.shape[0] // PARTS
+def mixed(rows_ref, one, two):
+    low = lax.broadcasted_iota(jnp.int32, (1, LANES), 1) < LANES // 2
+    a, b = rows_ref[pl.ds(one, 1), :], rows_ref[pl.ds(two, 1), :]
+    rows_ref[pl.ds(one, 1), :] = jnp.where(low, a, b)
+    rows_ref[pl.ds(two, 1), :] = jnp.where(low, b, a)
+
+
+def both_mixed(order_ref, rows_ref):
+    for slot in (0, 4):
+        mixed(rows_ref, order_ref[slot + 1], order_ref[slot + 2])
+
+
+def two_chunks(factor, columns_refs, centroids_refs, piece_refs, logits_refs, ready):
+    chunks = jnp.concatenate([ref[...] for ref in piece_refs], axis=0)
+    tops, totals = [], []
+    for number in range(2):
+        ready(number)
+        product = factor * lax.dot_general(
+            centroids_refs[number][...],
+            chunks,
+            (((1,), (1,)), ((), ())),
+            preferred_element_type=jnp.float32,
+        )
+        for k in range(2):
+            logits_refs[number][k] = product[:, k * LANES : (k + 1) * LANES]
+        shifted = product + columns_refs[number][...]
+        top = jnp.max(shifted, axis=0, keepdims=True)
+        tops.append(top)
+        totals.append(jnp.sum(jnp.exp(shifted - top), axis=0, keepdims=True))
+    top = jnp.maximum(*tops)
+    logsum = top + jnp.log(sum(total * jnp.exp(own - top) for own, total in zip(tops, totals)))
+    return [logsum[:, k * LANES : (k + 1) * LANES] for k in range(2)]
+
+
+def gathered(piece_refs, arrived_ref, sem):
+    start = 0
+    for ref in piece_refs:
+        size = ref.shape[0]
+        pltpu.make_async_copy(ref, arrived_ref.at[pl.ds(start, size)], sem).start()
+        start += size
+
+
+def early_kernel(factor, *refs):
+    rows_refs, centroids_refs, piece_refs = refs[:2], refs[2:4], refs[4:8]
+    columns_refs, held_refs, logits_refs, logsum_ref, arrived_ref = refs[8:10], refs[10:12], refs[12:14], refs[14], refs[15]
+    sems, sem = refs[16:]
+    for number in range(2):
+        size = held_refs[number].shape[0] // PARTS
         for part in range(PARTS):
             rows = pl.ds(part * size, size)
-            pltpu.make_async_copy(source.at[rows], target.at[rows], sem).start()
+            pltpu.make_async_copy(
+                centroids_refs[number].at[rows], held_refs[number].at[rows], sems.at[number]
+            ).start()
+    gathered(piece_refs, arrived_ref, sem)
     square = (LANES, LANES)
     diagonal = lax.broadcasted_iota(jnp.int32, square, 0) == lax.broadcasted_iota(
         jnp.int32, square, 1
@@ -86,34 +133,27 @@
             target[k * LANES : (k + 1) * LANES, :] = jnp.sum(
                 jnp.where(diagonal, row, 0.0), axis=1, keepdims=True
             )
-    for target in held_refs:
-        pltpu.make_async_copy(target, target, sem).wait()
-
-
-def logits_kernel(factor, order_ref, *refs):
-    duals_refs, centroids_refs, piece_refs = refs[:2], refs[2:4], refs[4:12]
-    *logits_refs, out_ref, arrived_ref, rows_ref, sem = refs[12:]
-    start = 0
-    for ref in piece_refs:
-        size = ref.shape[0]
-        pltpu.make_async_copy(ref, arrived_ref.at[pl.ds(start, size)], sem).start()
-        start += size
-    chunks = jnp.concatenate([ref[...] for ref in piece_refs], axis=0)
-    tops, totals = [], []
-    for duals_ref, centroids_ref, logits_ref in zip(duals_refs, centroids_refs, logits_refs):
-        product = factor * lax.dot_general(
-            centroids_ref[...], chunks, (((1,), (1,)), ((), ())), preferred_element_type=jnp.float32
-        )
-        for k in range(4):
-            logits_ref[k] = product[:, k * LANES : (k + 1) * LANES]
-        shifted = product + duals_ref[...]
-        top = jnp.max(shifted, axis=0, keepdims=True)
-        tops.append(top)
-        totals.append(jnp.sum(jnp.exp(shifted - top), axis=0, keepdims=True))
-    top = jnp.maximum(*tops)
-    logsum = top + jnp.log(sum(total * jnp.exp(own - top) for own, total in zip(tops, totals)))
+
+    def ready(number):
+        pltpu.make_async_copy(held_refs[number], held_refs[number], sems.at[number]).wait()
+
+    logsums = two_chunks(factor, columns_refs, held_refs, piece_refs, logits_refs, ready)
+    for k in range(2):
+        logsum_ref[k : k + 1, :] = logsums[k]
+    pltpu.make_async_copy(arrived_ref, arrived_ref, sem).wait()
+
+
+def late_kernel(factor, order_ref, *refs):
+    columns_refs, centroids_refs, piece_refs, earlier_ref = refs[:2], refs[2:4], refs[4:8], refs[8]
+    logits_refs, out_ref, arrived_ref, rows_ref, sem = refs[9:11], refs[11], refs[12], refs[13], refs[14]
+    gathered(piece_refs, arrived_ref, sem)
+    logsums = [earlier_ref[k : k + 1, :] for k in range(2)]
+    logsums += two_chunks(
+        factor, columns_refs, centroids_refs, piece_refs, logits_refs, lambda number: None
+    )
     for k in range(4):
-        rows_ref[pl.ds(lax.rem(order_ref[k], 4), 1), :] = logsum[:, k * LANES : (k + 1) * LANES]
+        rows_ref[pl.ds(lax.rem(order_ref[k], 4), 1), :] = logsums[k]
+    mixed(rows_ref, lax.rem(order_ref[1], 4), lax.rem(order_ref[2], 4))
     core = lax.div(order_ref[0], 4)
     send_rows(pltpu.roll(rows_ref[...], order_ref[CHUNKS + 2 + core], 1), out_ref)
     pltpu.make_async_copy(arrived_ref, arrived_ref, sem).wait()
@@ -123,39 +163,47 @@
     return pltpu.with_memory_space_constraint(array, pltpu.VMEM)
 
 
-def staged(duals, centroids):
-    rows = centroids[0].shape[0]
-    column = jax.ShapeDtypeStruct((rows, 1), jnp.float32)
-    arrays = [jax.ShapeDtypeStruct(array.shape, array.dtype) for array in centroids]
+def early_logits(factor, duals, centroids, pieces):
+    rows, depth = centroids[0].shape
+    f32 = jnp.float32
+    column = jax.ShapeDtypeStruct((rows, 1), f32)
+    logits = jax.ShapeDtypeStruct((2, rows, LANES), f32)
+    block = pl.BlockSpec(logits.shape, lambda: (0, 0, 0))
     return pl.pallas_call(
-        stage_kernel,
-        in_specs=[VMEM] * 2 + [ANY] * 2,
-        out_specs=[VMEM] * 4,
-        out_shape=[column, column] + arrays,
-        scratch_shapes=[pltpu.SemaphoreType.DMA],
-        compiler_params=LIMIT,
-    )(*[dual.reshape(rows // LANES, LANES) for dual in duals], *centroids)
-
-
-def chunk_logits(factor, order, columns, centroids, pieces):
+        functools.partial(early_kernel, factor),
+        in_specs=[VMEM] * 2 + [ANY] * 2 + [VMEM] * len(pieces),
+        out_specs=[VMEM] * 4 + [block, block, VMEM, ANY],
+        out_shape=[column, column]
+        + [jax.ShapeDtypeStruct(array.shape, array.dtype) for array in centroids]
+        + [logits, logits]
+        + [
+            jax.ShapeDtypeStruct((2, LANES), f32),
+            jax.ShapeDtypeStruct((2 * LANES, depth), pieces[0].dtype),
+        ],
+        scratch_shapes=[pltpu.SemaphoreType.DMA((2,)), pltpu.SemaphoreType.DMA],
+        compiler_params=pltpu.CompilerParams(vmem_limit_bytes=24 * 2**20),
+    )(*[dual.reshape(rows // LANES, LANES) for dual in duals], *centroids, *map(held, pieces))
+
+
+def late_logits(factor, order, columns, centroids, pieces, earlier):
     rows, depth = centroids[0].shape
     devices = lax.axis_size(EVERY)
     f32 = jnp.float32
-    logits = jax.ShapeDtypeStruct((4, rows, LANES), f32)
+    logits = jax.ShapeDtypeStruct((2, rows, LANES), f32)
     block = pl.BlockSpec(logits.shape, lambda: (0, 0, 0))
     return pl.pallas_call(
-        functools.partial(logits_kernel, factor),
-        in_specs=[SMEM] + [VMEM] * (4 + len(pieces)),
+        functools.partial(late_kernel, factor),
+        in_specs=[SMEM] + [VMEM] * (5 + len(pieces)),
         out_specs=[block, block, pl.BlockSpec((devices, 4, LANES), lambda: (0, 0, 0)), ANY],
         out_shape=[
             logits,
             logits,
             jax.ShapeDtypeStruct((devices, 4, LANES), f32),
-            jax.ShapeDtypeStruct((4 * LANES, depth), pieces[0].dtype),
+            jax.ShapeDtypeStruct((2 * LANES, depth), pieces[0].dtype),
         ],
         scratch_shapes=[pltpu.VMEM((4, LANES), f32), pltpu.SemaphoreType.DMA],
         compiler_params=pltpu.CompilerParams(vmem_limit_bytes=24 * 2**20),
-    )(order, *columns, *centroids, *[held(array) for array in pieces])
+    )(order, *columns, *centroids, *map(held, pieces), earlier)
 
 
 def send_rows(rows, out_ref):
@@ -163,9 +211,9 @@
 
 
 def first_kernel(order_ref, parts_ref, *refs):
-    logits_refs = refs[:2]
-    kernel_ref, passage_ref, centroid_ref, out_ref, sums_ref, sems = refs[2:]
-    starts = (0, 4)
+    logits_refs = refs[:4]
+    kernel_ref, passage_ref, centroid_ref, out_ref, sums_ref, sems = refs[4:]
+    starts = (0, 2, 4, 6)
     copies = [
         pltpu.make_async_copy(ref, kernel_ref.at[pl.ds(start, ref.shape[0])], sems.at[number])
         for number, (ref, start) in enumerate(zip(logits_refs, starts))
@@ -180,6 +228,7 @@
             top + jnp.log(jnp.sum(jnp.exp(part - top[None]), axis=0))
         )
     sums_ref[...] = to_local(order_ref, passage_ref[...])
+    both_mixed(order_ref, sums_ref)
     peak = None
     for k in range(CHUNKS):
         if k in starts:
@@ -200,6 +249,7 @@
         terms = kernel_ref[k] * inverse
         kernel_ref[k] = terms
         sums_ref[pl.ds(order_ref[k], 1), :] = jnp.sum(terms, axis=0, keepdims=True)
+    both_mixed(order_ref, sums_ref)
     send_rows(to_common(order_ref, sums_ref[...]), out_ref)
 
 
@@ -218,11 +268,13 @@
 
 def middle_kernel(order_ref, parts_ref, kernel_ref, out_ref, sums_ref):
     sums_ref[...] = to_local(order_ref, row_scale_of(parts_ref))
+    both_mixed(order_ref, sums_ref)
     scale = 1.0 / column_sums(order_ref, kernel_ref, sums_ref)
     for k in range(CHUNKS):
         sums_ref[pl.ds(order_ref[k], 1), :] = jnp.sum(
             kernel_ref[k] * scale, axis=0, keepdims=True
         )
+    both_mixed(order_ref, sums_ref)
     send_rows(to_common(order_ref, sums_ref[...]), out_ref)
 
 
@@ -243,6 +295,7 @@
 
     scale = row_scale_of(parts_ref)
     scale_ref[...] = to_local(order_ref, scale)
+    both_mixed(order_ref, scale_ref)
     total = column_sums(order_ref, kernel_ref, scale_ref)
     inverse = 1.0 / total
     for k in range(CHUNKS):
@@ -315,7 +368,8 @@
     top_before, bottom_after = along_second(top, 1), along_second(bottom, -1)
     bottom_before, top_after = along_second(bottom, 1), along_second(top, -1)
     top_across, bottom_across = along_second(top_before, 1), along_second(bottom_after, -1)
-    arrived = [top, bottom, top_before, bottom_before, top_across, bottom_across, top_after, bottom_after]
+    first_pieces = [top, bottom, top_before, bottom_after]
+    last_pieces = [top_after, bottom_before, top_across, bottom_across]
     order = [c * 4 + (second + k) % 4 for k in OWN]
     order += [(1 - c) * 4 + (first + k) % 4 for k in OWN]
     row, lane = jnp.where(h == 0, z, 4 + x), jnp.where(h == 0, x, z) * local_rows
@@ -323,17 +377,18 @@
     order += [(4 - x) % 4 * local_rows, (4 - z) % 4 * local_rows]
     order = jnp.stack(order).astype(jnp.int32)
 
-    pairs, _ = lax.optimization_barrier(
-        ((dual_init, near_duals, centroids, to_sibling(centroids)), (top_before, bottom_after))
-    )
-    *columns, near, sibling = staged(pairs[:2], pairs[2:])
-    arrived, near, sibling = lax.optimization_barrier((arrived, near, sibling))
-    *logits, parts, arrived = chunk_logits(factor, order, columns, (near, sibling), arrived)
-    logits = [logits[0], to_sibling(logits[1])]
+    pairs, first_pieces = lax.optimization_barrier(
+        ((dual_init, near_duals, centroids, to_sibling(centroids)), first_pieces)
+    )
+    early = early_logits(factor, pairs[:2], pairs[2:], first_pieces)
+    last_pieces, early = lax.optimization_barrier((last_pieces, early))
+    late = late_logits(factor, order, early[:2], early[2:4], last_pieces, early[6])
+    logits = [early[4], late[0], to_sibling(early[5]), to_sibling(late[1])]
+    parts, arrived = late[2], [early[7], late[3]]
     span = LANES
     f32 = jnp.float32
     parts = to_every(parts)
-    pieces = [arrived, to_sibling(arrived)]
+    pieces = arrived + [to_sibling(array) for array in arrived]
 
     sent = jax.ShapeDtypeStruct((devices, CHUNKS, span), jnp.bfloat16)
     block = pl.BlockSpec((devices, CHUNKS, span), lambda: (0, 0, 0))

time: 114 us -> 112 us (0.982)
  waiting for transfers between devices: 15 us -> 13.3 us
    ppermute x14 -> x16, waiting for transfers between devices: 15 us -> 13.3 us  [move(): return lax.ppermute(value, EVERY, pairs)]
    ppermute x14 -> x16, starting transfers between devices: 22.7 us -> 22.9 us  [move(): return lax.ppermute(value, EVERY, pairs)]
  transfers between devices with their start and end apart: 14 -> 16, of which waited for: 5 -> 5; matrix products, arithmetic and copies ran while one was open for 0% -> 0% of each run, Pallas kernels for 4% -> 7%
where the time goes in v9:
time: 112 us
  blocking collectives  50 us (45%)
  starting transfers between devices  22.9 us (20%)
  Pallas kernels  21.5 us (19%)
  waiting for transfers between devices  13.3 us (12%)
  local copies, waits for them, and re-layouts  2.95 us (3%)
    all_to_all x3, blocking collectives, to_every(): return lax.all_to_all(copies, EVERY, 0, 0)  50 us
    ppermute x16, starting transfers between devices, move(): return lax.ppermute(value, EVERY, pairs)  22.9 us
    ppermute x16, waiting for transfers between devices, move(): return lax.ppermute(value, EVERY, pairs)  13.3 us
    pallas_call x1, Pallas kernels, body(): pl.pallas_call(last_kernel, in_specs=[SMEM] + [VMEM] * 4 + [ANY] * len(pi...  8.59 us
    pallas_call x1, Pallas kernels, early_logits(): pl.pallas_call(functools.partial(early_kernel, factor), in_specs=[VMEM] *...  5.73 us
    pallas_call x1, Pallas kernels, late_logits(): pl.pallas_call(functools.partial(late_kernel, factor), in_specs=[SMEM] +...  4.09 us
    unnamed x4, local copies, waits for them, and re-layouts  2.86 us
  transfers between devices with their start and end apart: 16, of which 5 were waited for; matrix products, arithmetic and copies ran while one was open for 0% of the time, Pallas kernels for 7%

profile of v9, /device:TPU:1, one launch (start us, length us, event | category | flops | bytes accessed | tf_op | source)
XLA Modules:
  0.0 111.7 jit_solution(16442602226895658463)
XLA Ops:
  0.6 1.5 %collective-permute-start.11 = (bf16[512,4096]{1,0:T(8,128)(2,1)}, bf16[512,4096]{1,0:T(8,128)(2,1)}, u32[]{:S(2)}, u32[]{:S(2)}) collective-permute-start(bf16[512,4096]{1,0:T(8,128)(2,1)} %refs_2_), channel_id=1, source_target_pairs={{0,1},{1,0},{2,3},{3,2},{4,5},{5,4},{6,7},{7,6},{8,9},{9,8},{10,11... | collective-permute-start | bytes 12582920 | tf_op jit(solution)/shard_map/ppermute | solution.py:39
  2.1 4.6 %collective-permute-start = (bf16[32,4096]{1,0:T(8,128)(2,1)}, bf16[32,4096]{1,0:T(8,128)(2,1)S(1)}, u32[]{:S(2)}, u32[]{:S(2)}) collective-permute-start(bf16[32,4096]{1,0:T(8,128)(2,1)} %param.3), channel_id=1, source_target_pairs={{1,18},{3,16},{5,22},{7,20},{9,26},{11,24},{13,30},{15,28},{16,3},... | collective-permute-start | bytes 786440 | tf_op jit(solution)/shard_map/ppermute | solution.py:39
  6.8 2.6 %collective-permute-start.1 = (bf16[32,4096]{1,0:T(8,128)(2,1)}, bf16[32,4096]{1,0:T(8,128)(2,1)S(1)}, u32[]{:S(2)}, u32[]{:S(2)}) collective-permute-start(bf16[32,4096]{1,0:T(8,128)(2,1)} %param.3), channel_id=1, source_target_pairs={{0,12},{1,30},{2,14},{3,28},{4,0},{5,18},{6,2},{7,16},{8,4},{9,22}... | collective-permute-start | bytes 786440 | tf_op jit(solution)/shard_map/ppermute | solution.py:39
  9.3 6.4 %collective-permute-start.3 = (bf16[32,4096]{1,0:T(8,128)(2,1)}, bf16[32,4096]{1,0:T(8,128)(2,1)S(1)}, u32[]{:S(2)}, u32[]{:S(2)}) collective-permute-start(bf16[32,4096]{1,0:T(8,128)(2,1)} %param.3), channel_id=1, source_target_pairs={{0,8},{1,26},{2,10},{3,24},{4,12},{5,30},{6,14},{7,28},{8,0},{9,18... | collective-permute-start | bytes 786440 | tf_op jit(solution)/shard_map/ppermute | solution.py:39
  15.8 1.0 collective-permute-start.7
  16.8 3.5 %collective-permute-done.3 = bf16[32,4096]{1,0:T(8,128)(2,1)S(1)} collective-permute-done((bf16[32,4096]{1,0:T(8,128)(2,1)}, bf16[32,4096]{1,0:T(8,128)(2,1)S(1)}, u32[]{:S(2)}, u32[]{:S(2)}) %collective-permute-start.3) | collective-permute-done | bytes 262176 | tf_op jit(solution)/shard_map/ppermute | solution.py:39
  20.3 4.9 %collective-permute-done.4 = bf16[32,4096]{1,0:T(8,128)(2,1)S(1)} collective-permute-done((bf16[32,4096]{1,0:T(8,128)(2,1)}, bf16[32,4096]{1,0:T(8,128)(2,1)S(1)}, u32[]{:S(2)}, u32[]{:S(2)}) %collective-permute-start.4) | collective-permute-done | bytes 262176 | tf_op jit(solution)/shard_map/ppermute | solution.py:39
  25.2 0.9 collective-permute-start.9
  26.4 1.2 %collective-permute-start.6 = (bf16[64,4096]{1,0:T(8,128)(2,1)S(1)}, bf16[64,4096]{1,0:T(8,128)(2,1)S(1)}, u32[]{:S(2)}, u32[]{:S(2)}) collective-permute-start(bf16[64,4096]{1,0:T(8,128)(2,1)S(1)} %pad_maximum_fusion.1.refs_5_), channel_id=1, source_target_pairs={{0,32},{1,5},{2,34},{3,7},{4,36},{5,9},{6,38},{7,11},{8,40},{9,13}... | collective-permute-start | bytes 1572872 | tf_op jit(solution)/shard_map/ppermute | solution.py:39
  27.6 1.0 collective-permute-done.7.refs_6_
  28.6 1.3 %collective-permute-start.8 = (bf16[64,4096]{1,0:T(8,128)(2,1)S(1)}, bf16[64,4096]{1,0:T(8,128)(2,1)}, u32[]{:S(2)}, u32[]{:S(2)}) collective-permute-start(bf16[64,4096]{1,0:T(8,128)(2,1)S(1)} %collective-permute-done.7.refs_6_), channel_id=1, source_target_pairs={{0,32},{1,5},{2,34},{3,7},{4,36},{5,9},{6,38},{7,11},{8,40},{9,13}... | collective-permute-start | bytes 1572872 | tf_op jit(solution)/shard_map/ppermute | solution.py:39
  29.9 3.7 %collective-permute-done.9.refs_7_ = bf16[64,4096]{1,0:T(8,128)(2,1)S(1)} collective-permute-done((bf16[64,4096]{1,0:T(8,128)(2,1)S(1)}, bf16[64,4096]{1,0:T(8,128)(2,1)S(1)}, u32[]{:S(2)}, u32[]{:S(2)}) %collective-permute-start.9) | collective-permute-done | bytes 524320 | tf_op jit(solution)/shard_map/ppermute | solution.py:39
  33.6 2.1 %collective-permute-start.10 = (bf16[64,4096]{1,0:T(8,128)(2,1)S(1)}, bf16[64,4096]{1,0:T(8,128)(2,1)}, u32[]{:S(2)}, u32[]{:S(2)}) collective-permute-start(bf16[64,4096]{1,0:T(8,128)(2,1)S(1)} %collective-permute-done.9.refs_7_), channel_id=1, source_target_pairs={{0,96},{1,13},{2,98},{3,15},{4,100},{5,1},{6,102},{7,3},{8,104},{9... | collective-permute-start | bytes 1572872 | tf_op jit(solution)/shard_map/ppermute | solution.py:39
  35.8 2.2 %copy-done = bf16[512,4096]{1,0:T(8,128)(2,1)S(1)} copy-done((bf16[512,4096]{1,0:T(8,128)(2,1)S(1)}, bf16[512,4096]{1,0:T(8,128)(2,1)}, u32[]{:S(2)}) %copy-start) | copy-done | bytes 4194328
  38.0 0.7 copy-done.1
  38.6 5.7 %shard_map.58 = (f32[512,1]{1,0:T(8,128)S(1)}, f32[512,1]{1,0:T(8,128)S(1)}, bf16[512,4096]{1,0:T(8,128)(2,1)S(1)}, bf16[512,4096]{1,0:T(8,128)(2,1)S(1)}, f32[2...) custom-call(f32[4,128]{1,0:T(4,128)S(1)} %bitcast.18, ...), custom_call_target="tpu_custom_call" | custom-call | tf_op jit(solution)/shard_map/pallas_call | solution.py:172
  44.7 4.1 %shard_map.59 = (f32[2,512,128]{2,1,0:T(8,128)S(1)}, f32[2,512,128]{2,1,0:T(8,128)S(1)}, f32[128,4,128]{2,1,0:T(4,128)S(1)}, bf16[256,4096]{1,0:T(8,128)(2,1)S(1)}) custom-call(s32[14]{0:T(128)S(1)} %stack.59.order_ref, f32[512,1]{1,0:T(8,128)S(1)} %get-tuple-element.67.refs_0_, f32[512,1]{1,0:T(8,128)S(1)} %get-tuple-element.68.refs_1_, ...), custom_call_target="tpu_custom_call" | custom-call | tf_op jit(solution)/shard_map/pallas_call | solution.py:194
  48.8 0.5 collective-permute-start.14
  49.8 19.6 %all_to_all.15.parts_ref = f32[128,4,128]{2,1,0:T(4,128)S(1)} all-to-all(f32[128,4,128]{2,1,0:T(4,128)S(1)} %get-tuple-element.76), channel_id=1, replica_groups=mesh['psg'=32,'cen'=4] {'psg','cen'}, dimensions={0} | all-to-all | bytes 524288 | tf_op jit(solution)/shard_map/all_to_all | solution.py:54
  69.5 2.0 %shard_map.60 = (f32[8,512,128]{2,1,0:T(8,128)S(1)}, f32[8,128]{1,0:T(8,128)S(1)}, f32[512,1]{1,0:T(8,128)S(1)}, bf16[128,8,128]{2,1,0:T(8,128)(2,1)S(1)}) custom-call(s32[14]{0:T(128)S(1)} %stack.59.order_ref, f32[128,4,128]{2,1,0:T(4,128)S(1)} %all_to_all.15.parts_ref, f32[2,512,128]{2,1,0:T(8,128)S(1)} %get-tuple-element.77.refs_0_, ...), custom_call_target="tpu_custom_call" | custom-call | tf_op jit(solution)/shard_map/pallas_call | solution.py:396
  71.5 15.2 %all_to_all.16.parts_ref = bf16[128,8,128]{2,1,0:T(8,128)(2,1)S(1)} all-to-all(bf16[128,8,128]{2,1,0:T(8,128)(2,1)S(1)} %get-tuple-element.84), channel_id=1, replica_groups=mesh['psg'=32,'cen'=4] {'psg','cen'}, dimensions={0} | all-to-all | bytes 524288 | tf_op jit(solution)/shard_map/all_to_all | solution.py:54
  86.7 1.2 %shard_map.61 = bf16[128,8,128]{2,1,0:T(8,128)(2,1)S(1)} custom-call(s32[14]{0:T(128)S(1)} %stack.59.order_ref, bf16[128,8,128]{2,1,0:T(8,128)(2,1)S(1)} %all_to_all.16.parts_ref, f32[8,512,128]{2,1,0:T(8,128)S(1)} %get-tuple-element.85.kernel_ref), custom_call_target="tpu_custom_call" | custom-call | tf_op jit(solution)/shard_map/pallas_call | solution.py:410
  87.8 15.2 %all_to_all.17.parts_ref = bf16[128,8,128]{2,1,0:T(8,128)(2,1)S(1)} all-to-all(bf16[128,8,128]{2,1,0:T(8,128)(2,1)S(1)} %shard_map.61), channel_id=1, replica_groups=mesh['psg'=32,'cen'=4] {'psg','cen'}, dimensions={0} | all-to-all | bytes 524288 | tf_op jit(solution)/shard_map/all_to_all | solution.py:54
  103.0 8.6 %shard_map.62 = (bf16[512,4096]{1,0:T(8,128)(2,1)}, f32[1,32]{1,0:T(1,128)}, f32[4,128]{1,0:T(4,128)}) custom-call(s32[14]{0:T(128)S(1)} %stack.59.order_ref, bf16[128,8,128]{2,1,0:T(8,128)(2,1)S(1)} %all_to_all.17.parts_ref, f32[8,512,128]{2,1,0:T(8,128)S(1)} %get-tuple-element.85.kernel_ref, f32[8,128]{1,0:T(8,128)S(1)} %get-tuple-element.86.passage_ref, ...), custom_call_target="tpu_custom_call" | custom-call | tf_op jit(solution)/shard_map/pallas_call | solution.py:418
  (24 shorter events, 1.3 us)
Async XLA Ops:
  0.6 35.1 %collective-permute-start.11 = (bf16[512,4096]{1,0:T(8,128)(2,1)}, bf16[512,4096]{1,0:T(8,128)(2,1)}, u32[]{:S(2)}, u32[]{:S(2)}) collective-permute-start(bf16[512,4096]{1,0:T(8,128)(2,1)} %refs_2_), channel_id=1, source_target_pairs={{0,1},{1,0},{2,3},{3,2},{4,5},{5,4},{6,7},{7,6},{8,9},{9,8},{10,11... | collective-permute-start | bytes 12582920 | tf_op jit(solution)/shard_map/ppermute | solution.py:39
  2.1 13.6 %collective-permute-start = (bf16[32,4096]{1,0:T(8,128)(2,1)}, bf16[32,4096]{1,0:T(8,128)(2,1)S(1)}, u32[]{:S(2)}, u32[]{:S(2)}) collective-permute-start(bf16[32,4096]{1,0:T(8,128)(2,1)} %param.3), channel_id=1, source_target_pairs={{1,18},{3,16},{5,22},{7,20},{9,26},{11,24},{13,30},{15,28},{16,3},... | collective-permute-start | bytes 786440 | tf_op jit(solution)/shard_map/ppermute | solution.py:39
  6.8 9.0 %collective-permute-start.1 = (bf16[32,4096]{1,0:T(8,128)(2,1)}, bf16[32,4096]{1,0:T(8,128)(2,1)S(1)}, u32[]{:S(2)}, u32[]{:S(2)}) collective-permute-start(bf16[32,4096]{1,0:T(8,128)(2,1)} %param.3), channel_id=1, source_target_pairs={{0,12},{1,30},{2,14},{3,28},{4,0},{5,18},{6,2},{7,16},{8,4},{9,22}... | collective-permute-start | bytes 786440 | tf_op jit(solution)/shard_map/ppermute | solution.py:39
  9.3 10.9 %collective-permute-start.3 = (bf16[32,4096]{1,0:T(8,128)(2,1)}, bf16[32,4096]{1,0:T(8,128)(2,1)S(1)}, u32[]{:S(2)}, u32[]{:S(2)}) collective-permute-start(bf16[32,4096]{1,0:T(8,128)(2,1)} %param.3), channel_id=1, source_target_pairs={{0,8},{1,26},{2,10},{3,24},{4,12},{5,30},{6,14},{7,28},{8,0},{9,18... | collective-permute-start | bytes 786440 | tf_op jit(solution)/shard_map/ppermute | solution.py:39
  15.7 9.4 %collective-permute-start.4 = (bf16[32,4096]{1,0:T(8,128)(2,1)}, bf16[32,4096]{1,0:T(8,128)(2,1)S(1)}, u32[]{:S(2)}, u32[]{:S(2)}) collective-permute-start(bf16[32,4096]{1,0:T(8,128)(2,1)} %param.3), channel_id=1, source_target_pairs={{0,4},{1,22},{2,6},{3,20},{4,8},{5,26},{6,10},{7,24},{8,12},{9,30}... | collective-permute-start | bytes 786440 | tf_op jit(solution)/shard_map/ppermute | solution.py:39
  15.7 9.5 %collective-permute-start.5 = (f32[512]{0:T(512)}, f32[512]{0:T(512)S(1)}, u32[]{:S(2)}, u32[]{:S(2)}) collective-permute-start(f32[512]{0:T(512)} %param.5), channel_id=1, source_target_pairs={{0,1},{1,0},{2,3},{3,2},{4,5},{5,4},{6,7},{7,6},{8,9},{9,8},{10,11... | collective-permute-start | bytes 6152 | tf_op jit(solution)/shard_map/ppermute | solution.py:39
  15.8 12.8 %collective-permute-start.7 = (bf16[64,4096]{1,0:T(8,128)(2,1)S(1)}, bf16[64,4096]{1,0:T(8,128)(2,1)S(1)}, u32[]{:S(2)}, u32[]{:S(2)}) collective-permute-start(bf16[64,4096]{1,0:T(8,128)(2,1)S(1)} %pad_maximum_fusion.refs_4_), channel_id=1, source_target_pairs={{0,32},{1,5},{2,34},{3,7},{4,36},{5,9},{6,38},{7,11},{8,40},{9,13}... | collective-permute-start | bytes 1572872 | tf_op jit(solution)/shard_map/ppermute | solution.py:39
  25.2 8.4 %collective-permute-start.9 = (bf16[64,4096]{1,0:T(8,128)(2,1)S(1)}, bf16[64,4096]{1,0:T(8,128)(2,1)S(1)}, u32[]{:S(2)}, u32[]{:S(2)}) collective-permute-start(bf16[64,4096]{1,0:T(8,128)(2,1)S(1)} %pad_maximum_fusion.1.refs_5_), channel_id=1, source_target_pairs={{0,96},{1,13},{2,98},{3,15},{4,100},{5,1},{6,102},{7,3},{8,104},{9... | collective-permute-start | bytes 1572872 | tf_op jit(solution)/shard_map/ppermute | solution.py:39
  26.1 18.3 %collective-permute-start.2 = (bf16[64,4096]{1,0:T(8,128)(2,1)S(1)}, bf16[64,4096]{1,0:T(8,128)(2,1)S(1)}, u32[]{:S(2)}, u32[]{:S(2)}) collective-permute-start(bf16[64,4096]{1,0:T(8,128)(2,1)S(1)} %pad_maximum_fusion.refs_4_), channel_id=1, source_target_pairs={{0,96},{1,13},{2,98},{3,15},{4,100},{5,1},{6,102},{7,3},{8,104},{9... | collective-permute-start | bytes 1572872 | tf_op jit(solution)/shard_map/ppermute | solution.py:39
  26.4 18.0 %collective-permute-start.6 = (bf16[64,4096]{1,0:T(8,128)(2,1)S(1)}, bf16[64,4096]{1,0:T(8,128)(2,1)S(1)}, u32[]{:S(2)}, u32[]{:S(2)}) collective-permute-start(bf16[64,4096]{1,0:T(8,128)(2,1)S(1)} %pad_maximum_fusion.1.refs_5_), channel_id=1, source_target_pairs={{0,32},{1,5},{2,34},{3,7},{4,36},{5,9},{6,38},{7,11},{8,40},{9,13}... | collective-permute-start | bytes 1572872 | tf_op jit(solution)/shard_map/ppermute | solution.py:39
  28.6 15.8 %collective-permute-start.8 = (bf16[64,4096]{1,0:T(8,128)(2,1)S(1)}, bf16[64,4096]{1,0:T(8,128)(2,1)}, u32[]{:S(2)}, u32[]{:S(2)}) collective-permute-start(bf16[64,4096]{1,0:T(8,128)(2,1)S(1)} %collective-permute-done.7.refs_6_), channel_id=1, source_target_pairs={{0,32},{1,5},{2,34},{3,7},{4,36},{5,9},{6,38},{7,11},{8,40},{9,13}... | collective-permute-start | bytes 1572872 | tf_op jit(solution)/shard_map/ppermute | solution.py:39
  33.6 11.0 %collective-permute-start.10 = (bf16[64,4096]{1,0:T(8,128)(2,1)S(1)}, bf16[64,4096]{1,0:T(8,128)(2,1)}, u32[]{:S(2)}, u32[]{:S(2)}) collective-permute-start(bf16[64,4096]{1,0:T(8,128)(2,1)S(1)} %collective-permute-done.9.refs_7_), channel_id=1, source_target_pairs={{0,96},{1,13},{2,98},{3,15},{4,100},{5,1},{6,102},{7,3},{8,104},{9... | collective-permute-start | bytes 1572872 | tf_op jit(solution)/shard_map/ppermute | solution.py:39
  35.8 2.2 %copy-start = (bf16[512,4096]{1,0:T(8,128)(2,1)S(1)}, bf16[512,4096]{1,0:T(8,128)(2,1)}, u32[]{:S(2)}) copy-start(bf16[512,4096]{1,0:T(8,128)(2,1)} %refs_2_) | copy-start | bytes 12582916
  38.0 0.7 copy-start.1
  48.7 22.7 %collective-permute-start.15 = (bf16[256,4096]{1,0:T(8,128)(2,1)S(1)}, bf16[256,4096]{1,0:T(8,128)(2,1)S(1)}, u32[]{:S(2)}, u32[]{:S(2)}) collective-permute-start(bf16[256,4096]{1,0:T(8,128)(2,1)S(1)} %get-tuple-element.89.refs_1_), channel_id=1, source_target_pairs={{0,1},{1,0},{2,3},{3,2},{4,5},{5,4},{6,7},{7,6},{8,9},{9,8},{10,11... | collective-permute-start | bytes 6291464 | tf_op jit(solution)/shard_map/ppermute | solution.py:39
  48.8 22.6 %collective-permute-start.14 = (bf16[256,4096]{1,0:T(8,128)(2,1)S(1)}, bf16[256,4096]{1,0:T(8,128)(2,1)S(1)}, u32[]{:S(2)}, u32[]{:S(2)}) collective-permute-start(bf16[256,4096]{1,0:T(8,128)(2,1)S(1)} %get-tuple-element.88.refs_0_), channel_id=1, source_target_pairs={{0,1},{1,0},{2,3},{3,2},{4,5},{5,4},{6,7},{7,6},{8,9},{9,8},{10,11... | collective-permute-start | bytes 6291464 | tf_op jit(solution)/shard_map/ppermute | solution.py:39
  49.3 20.2 %collective-permute-start.13 = (f32[2,512,128]{2,1,0:T(8,128)S(1)}, f32[2,512,128]{2,1,0:T(8,128)S(1)}, u32[]{:S(2)}, u32[]{:S(2)}) collective-permute-start(f32[2,512,128]{2,1,0:T(8,128)S(1)} %get-tuple-element.80), channel_id=1, source_target_pairs={{0,1},{1,0},{2,3},{3,2},{4,5},{5,4},{6,7},{7,6},{8,9},{9,8},{10,11... | collective-permute-start | bytes 1572872 | tf_op jit(solution)/shard_map/ppermute | solution.py:39
  49.4 20.1 %collective-permute-start.12 = (f32[2,512,128]{2,1,0:T(8,128)S(1)}, f32[2,512,128]{2,1,0:T(8,128)S(1)}, u32[]{:S(2)}, u32[]{:S(2)}) collective-permute-start(f32[2,512,128]{2,1,0:T(8,128)S(1)} %get-tuple-element.79), channel_id=1, source_target_pairs={{0,1},{1,0},{2,3},{3,2},{4,5},{5,4},{6,7},{7,6},{8,9},{9,8},{10,11... | collective-permute-start | bytes 1572872 | tf_op jit(solution)/shard_map/ppermute | solution.py:39

commit v10 on v9

--- a/solution.py
+++ b/solution.py
@@ -113,7 +113,8 @@
 
 def early_kernel(factor, *refs):
     rows_refs, centroids_refs, piece_refs = refs[:2], refs[2:4], refs[4:8]
-    columns_refs, held_refs, logits_refs, logsum_ref, arrived_ref = refs[8:10], refs[10:12], refs[12:14], refs[14], refs[15]
+    columns_refs, held_refs, logits_refs, logsum_ref = refs[8:10], refs[10:12], refs[12:14], refs[14]
+    arrived_ref = refs[15].at[pl.ds(0, 2 * LANES)]
     sems, sem = refs[16:]
     for number in range(2):
         size = held_refs[number].shape[0] // PARTS
@@ -145,7 +146,8 @@
 
 def late_kernel(factor, order_ref, *refs):
     columns_refs, centroids_refs, piece_refs, earlier_ref = refs[:2], refs[2:4], refs[4:8], refs[8]
-    logits_refs, out_ref, arrived_ref, rows_ref, sem = refs[9:11], refs[11], refs[12], refs[13], refs[14]
+    logits_refs, out_ref, all_ref, rows_ref, sem = refs[10:12], refs[12], refs[13], refs[14], refs[15]
+    arrived_ref = all_ref.at[pl.ds(2 * LANES, 2 * LANES)]
     gathered(piece_refs, arrived_ref, sem)
     logsums = [earlier_ref[k : k + 1, :] for k in range(2)]
     logsums += two_chunks(
@@ -178,14 +180,14 @@
         + [logits, logits]
         + [
             jax.ShapeDtypeStruct((2, LANES), f32),
-            jax.ShapeDtypeStruct((2 * LANES, depth), pieces[0].dtype),
+            jax.ShapeDtypeStruct((4 * LANES, depth), pieces[0].dtype),
         ],
         scratch_shapes=[pltpu.SemaphoreType.DMA((2,)), pltpu.SemaphoreType.DMA],
         compiler_params=pltpu.CompilerParams(vmem_limit_bytes=24 * 2**20),
     )(*[dual.reshape(rows // LANES, LANES) for dual in duals], *centroids, *map(held, pieces))
 
 
-def late_logits(factor, order, columns, centroids, pieces, earlier):
+def late_logits(factor, order, columns, centroids, pieces, earlier, arrived):
     rows, depth = centroids[0].shape
     devices = lax.axis_size(EVERY)
     f32 = jnp.float32
@@ -193,17 +195,18 @@
     block = pl.BlockSpec(logits.shape, lambda: (0, 0, 0))
     return pl.pallas_call(
         functools.partial(late_kernel, factor),
-        in_specs=[SMEM] + [VMEM] * (5 + len(pieces)),
+        in_specs=[SMEM] + [VMEM] * (5 + len(pieces)) + [ANY],
         out_specs=[block, block, pl.BlockSpec((devices, 4, LANES), lambda: (0, 0, 0)), ANY],
         out_shape=[
             logits,
             logits,
             jax.ShapeDtypeStruct((devices, 4, LANES), f32),
-            jax.ShapeDtypeStruct((2 * LANES, depth), pieces[0].dtype),
+            jax.ShapeDtypeStruct((4 * LANES, depth), pieces[0].dtype),
         ],
         scratch_shapes=[pltpu.VMEM((4, LANES), f32), pltpu.SemaphoreType.DMA],
         compiler_params=pltpu.CompilerParams(vmem_limit_bytes=24 * 2**20),
-    )(order, *columns, *centroids, *map(held, pieces), earlier)
+        input_output_aliases={10: 3},
+    )(order, *columns, *centroids, *map(held, pieces), earlier, arrived)
 
 
 def send_rows(rows, out_ref):
@@ -382,9 +385,9 @@
     )
     early = early_logits(factor, pairs[:2], pairs[2:], first_pieces)
     last_pieces, early = lax.optimization_barrier((last_pieces, early))
-    late = late_logits(factor, order, early[:2], early[2:4], last_pieces, early[6])
+    late = late_logits(factor, order, early[:2], early[2:4], last_pieces, early[6], early[7])
     logits = [early[4], late[0], to_sibling(early[5]), to_sibling(late[1])]
-    parts, arrived = late[2], [early[7], late[3]]
+    parts, arrived = late[2], [late[3]]
     span = LANES
     f32 = jnp.float32
     parts = to_every(parts)

time: 112 us -> 112 us (level)
    ppermute x16 -> x15, starting transfers between devices: 22.9 us -> 22.5 us  [move(): return lax.ppermute(value, EVERY, pairs)]
    ppermute x16 -> x15, waiting for transfers between devices: 13.3 us -> 13.3 us  [move(): return lax.ppermute(value, EVERY, pairs)]
  transfers between devices with their start and end apart: 16 -> 15, of which waited for: 5 -> 5; matrix products, arithmetic and copies ran while one was open for 0% -> 0% of each run, Pallas kernels for 7% -> 7%
where the time goes in v10:
time: 112 us
  blocking collectives  50 us (45%)
  starting transfers between devices  22.5 us (20%)
  Pallas kernels  21.7 us (19%)
  waiting for transfers between devices  13.3 us (12%)
  local copies, waits for them, and re-layouts  2.95 us (3%)
    all_to_all x3, blocking collectives, to_every(): return lax.all_to_all(copies, EVERY, 0, 0)  50 us
    ppermute x15, starting transfers between devices, move(): return lax.ppermute(value, EVERY, pairs)  22.5 us
    ppermute x15, waiting for transfers between devices, move(): return lax.ppermute(value, EVERY, pairs)  13.3 us
    pallas_call x1, Pallas kernels, body(): pl.pallas_call(last_kernel, in_specs=[SMEM] + [VMEM] * 4 + [ANY] * len(pi...  8.84 us
    pallas_call x1, Pallas kernels, early_logits(): pl.pallas_call(functools.partial(early_kernel, factor), in_specs=[VMEM] *...  5.73 us
    pallas_call x1, Pallas kernels, late_logits(): pl.pallas_call(functools.partial(late_kernel, factor), in_specs=[SMEM] +...  4.07 us
    unnamed x4, local copies, waits for them, and re-layouts  2.86 us
  transfers between devices with their start and end apart: 15, of which 5 were waited for; matrix products, arithmetic and copies ran while one was open for 0% of the time, Pallas kernels for 7%

profile of v10, /device:TPU:1, one launch (start us, length us, event | category | flops | bytes accessed | tf_op | source)
XLA Modules:
  0.0 111.5 jit_solution(11613694630798913355)
XLA Ops:
  0.6 1.5 %collective-permute-start.11 = (bf16[512,4096]{1,0:T(8,128)(2,1)}, bf16[512,4096]{1,0:T(8,128)(2,1)}, u32[]{:S(2)}, u32[]{:S(2)}) collective-permute-start(bf16[512,4096]{1,0:T(8,128)(2,1)} %refs_2_), channel_id=1, source_target_pairs={{0,1},{1,0},{2,3},{3,2},{4,5},{5,4},{6,7},{7,6},{8,9},{9,8},{10,11... | collective-permute-start | bytes 12582920 | tf_op jit(solution)/shard_map/ppermute | solution.py:39
  2.1 4.6 %collective-permute-start = (bf16[32,4096]{1,0:T(8,128)(2,1)}, bf16[32,4096]{1,0:T(8,128)(2,1)S(1)}, u32[]{:S(2)}, u32[]{:S(2)}) collective-permute-start(bf16[32,4096]{1,0:T(8,128)(2,1)} %param.3), channel_id=1, source_target_pairs={{1,18},{3,16},{5,22},{7,20},{9,26},{11,24},{13,30},{15,28},{16,3},... | collective-permute-start | bytes 786440 | tf_op jit(solution)/shard_map/ppermute | solution.py:39
  6.8 2.6 %collective-permute-start.1 = (bf16[32,4096]{1,0:T(8,128)(2,1)}, bf16[32,4096]{1,0:T(8,128)(2,1)S(1)}, u32[]{:S(2)}, u32[]{:S(2)}) collective-permute-start(bf16[32,4096]{1,0:T(8,128)(2,1)} %param.3), channel_id=1, source_target_pairs={{0,12},{1,30},{2,14},{3,28},{4,0},{5,18},{6,2},{7,16},{8,4},{9,22}... | collective-permute-start | bytes 786440 | tf_op jit(solution)/shard_map/ppermute | solution.py:39
  9.3 6.4 %collective-permute-start.3 = (bf16[32,4096]{1,0:T(8,128)(2,1)}, bf16[32,4096]{1,0:T(8,128)(2,1)S(1)}, u32[]{:S(2)}, u32[]{:S(2)}) collective-permute-start(bf16[32,4096]{1,0:T(8,128)(2,1)} %param.3), channel_id=1, source_target_pairs={{0,8},{1,26},{2,10},{3,24},{4,12},{5,30},{6,14},{7,28},{8,0},{9,18... | collective-permute-start | bytes 786440 | tf_op jit(solution)/shard_map/ppermute | solution.py:39
  15.8 1.0 collective-permute-start.7
  16.8 3.5 %collective-permute-done.3 = bf16[32,4096]{1,0:T(8,128)(2,1)S(1)} collective-permute-done((bf16[32,4096]{1,0:T(8,128)(2,1)}, bf16[32,4096]{1,0:T(8,128)(2,1)S(1)}, u32[]{:S(2)}, u32[]{:S(2)}) %collective-permute-start.3) | collective-permute-done | bytes 262176 | tf_op jit(solution)/shard_map/ppermute | solution.py:39
  20.3 4.9 %collective-permute-done.4 = bf16[32,4096]{1,0:T(8,128)(2,1)S(1)} collective-permute-done((bf16[32,4096]{1,0:T(8,128)(2,1)}, bf16[32,4096]{1,0:T(8,128)(2,1)S(1)}, u32[]{:S(2)}, u32[]{:S(2)}) %collective-permute-start.4) | collective-permute-done | bytes 262176 | tf_op jit(solution)/shard_map/ppermute | solution.py:39
  25.2 0.9 collective-permute-start.9
  26.4 1.2 %collective-permute-start.6 = (bf16[64,4096]{1,0:T(8,128)(2,1)S(1)}, bf16[64,4096]{1,0:T(8,128)(2,1)S(1)}, u32[]{:S(2)}, u32[]{:S(2)}) collective-permute-start(bf16[64,4096]{1,0:T(8,128)(2,1)S(1)} %pad_maximum_fusion.1.refs_5_), channel_id=1, source_target_pairs={{0,32},{1,5},{2,34},{3,7},{4,36},{5,9},{6,38},{7,11},{8,40},{9,13}... | collective-permute-start | bytes 1572872 | tf_op jit(solution)/shard_map/ppermute | solution.py:39
  27.6 1.0 collective-permute-done.7.refs_6_
  28.6 1.3 %collective-permute-start.8 = (bf16[64,4096]{1,0:T(8,128)(2,1)S(1)}, bf16[64,4096]{1,0:T(8,128)(2,1)}, u32[]{:S(2)}, u32[]{:S(2)}) collective-permute-start(bf16[64,4096]{1,0:T(8,128)(2,1)S(1)} %collective-permute-done.7.refs_6_), channel_id=1, source_target_pairs={{0,32},{1,5},{2,34},{3,7},{4,36},{5,9},{6,38},{7,11},{8,40},{9,13}... | collective-permute-start | bytes 1572872 | tf_op jit(solution)/shard_map/ppermute | solution.py:39
  29.9 3.7 %collective-permute-done.9.refs_7_ = bf16[64,4096]{1,0:T(8,128)(2,1)S(1)} collective-permute-done((bf16[64,4096]{1,0:T(8,128)(2,1)S(1)}, bf16[64,4096]{1,0:T(8,128)(2,1)S(1)}, u32[]{:S(2)}, u32[]{:S(2)}) %collective-permute-start.9) | collective-permute-done | bytes 524320 | tf_op jit(solution)/shard_map/ppermute | solution.py:39
  33.6 2.1 %collective-permute-start.10 = (bf16[64,4096]{1,0:T(8,128)(2,1)S(1)}, bf16[64,4096]{1,0:T(8,128)(2,1)}, u32[]{:S(2)}, u32[]{:S(2)}) collective-permute-start(bf16[64,4096]{1,0:T(8,128)(2,1)S(1)} %collective-permute-done.9.refs_7_), channel_id=1, source_target_pairs={{0,96},{1,13},{2,98},{3,15},{4,100},{5,1},{6,102},{7,3},{8,104},{9... | collective-permute-start | bytes 1572872 | tf_op jit(solution)/shard_map/ppermute | solution.py:39
  35.8 2.2 %copy-done = bf16[512,4096]{1,0:T(8,128)(2,1)S(1)} copy-done((bf16[512,4096]{1,0:T(8,128)(2,1)S(1)}, bf16[512,4096]{1,0:T(8,128)(2,1)}, u32[]{:S(2)}) %copy-start) | copy-done | bytes 4194328
  38.0 0.7 copy-done.1
  38.6 5.7 %shard_map.58 = (f32[512,1]{1,0:T(8,128)S(1)}, f32[512,1]{1,0:T(8,128)S(1)}, bf16[512,4096]{1,0:T(8,128)(2,1)S(1)}, bf16[512,4096]{1,0:T(8,128)(2,1)S(1)}, f32[2...) custom-call(f32[4,128]{1,0:T(4,128)S(1)} %bitcast.18, ...), custom_call_target="tpu_custom_call" | custom-call | tf_op jit(solution)/shard_map/pallas_call | solution.py:174
  44.7 4.1 %shard_map.59 = (f32[2,512,128]{2,1,0:T(8,128)S(1)}, f32[2,512,128]{2,1,0:T(8,128)S(1)}, f32[128,4,128]{2,1,0:T(4,128)S(1)}, bf16[512,4096]{1,0:T(8,128)(2,1)S(1)}) custom-call(s32[14]{0:T(128)S(1)} %stack.59.order_ref, f32[512,1]{1,0:T(8,128)S(1)} %get-tuple-element.65.refs_0_, ...), custom_call_target="tpu_custom_call", output_to_operand_aliasing={{3}: (10, {})} | custom-call | tf_op jit(solution)/shard_map/pallas_call | solution.py:196
  48.8 0.5 collective-permute-start.13
  49.4 19.7 %all_to_all.15.parts_ref = f32[128,4,128]{2,1,0:T(4,128)S(1)} all-to-all(f32[128,4,128]{2,1,0:T(4,128)S(1)} %get-tuple-element.75), channel_id=1, replica_groups=mesh['psg'=32,'cen'=4] {'psg','cen'}, dimensions={0} | all-to-all | bytes 524288 | tf_op jit(solution)/shard_map/all_to_all | solution.py:54
  69.1 1.9 %shard_map.60 = (f32[8,512,128]{2,1,0:T(8,128)S(1)}, f32[8,128]{1,0:T(8,128)S(1)}, f32[512,1]{1,0:T(8,128)S(1)}, bf16[128,8,128]{2,1,0:T(8,128)(2,1)S(1)}) custom-call(s32[14]{0:T(128)S(1)} %stack.59.order_ref, f32[128,4,128]{2,1,0:T(4,128)S(1)} %all_to_all.15.parts_ref, f32[2,512,128]{2,1,0:T(8,128)S(1)} %get-tuple-element.76.refs_0_, ...), custom_call_target="tpu_custom_call" | custom-call | tf_op jit(solution)/shard_map/pallas_call | solution.py:399
  71.0 15.2 %all_to_all.16.parts_ref = bf16[128,8,128]{2,1,0:T(8,128)(2,1)S(1)} all-to-all(bf16[128,8,128]{2,1,0:T(8,128)(2,1)S(1)} %get-tuple-element.82), channel_id=1, replica_groups=mesh['psg'=32,'cen'=4] {'psg','cen'}, dimensions={0} | all-to-all | bytes 524288 | tf_op jit(solution)/shard_map/all_to_all | solution.py:54
  86.2 1.1 %shard_map.61 = bf16[128,8,128]{2,1,0:T(8,128)(2,1)S(1)} custom-call(s32[14]{0:T(128)S(1)} %stack.59.order_ref, bf16[128,8,128]{2,1,0:T(8,128)(2,1)S(1)} %all_to_all.16.parts_ref, f32[8,512,128]{2,1,0:T(8,128)S(1)} %get-tuple-element.83.kernel_ref), custom_call_target="tpu_custom_call" | custom-call | tf_op jit(solution)/shard_map/pallas_call | solution.py:413
  87.4 15.2 %all_to_all.17.parts_ref = bf16[128,8,128]{2,1,0:T(8,128)(2,1)S(1)} all-to-all(bf16[128,8,128]{2,1,0:T(8,128)(2,1)S(1)} %shard_map.61), channel_id=1, replica_groups=mesh['psg'=32,'cen'=4] {'psg','cen'}, dimensions={0} | all-to-all | bytes 524288 | tf_op jit(solution)/shard_map/all_to_all | solution.py:54
  102.5 8.8 %shard_map.62 = (bf16[512,4096]{1,0:T(8,128)(2,1)}, f32[1,32]{1,0:T(1,128)}, f32[4,128]{1,0:T(4,128)}) custom-call(s32[14]{0:T(128)S(1)} %stack.59.order_ref, bf16[128,8,128]{2,1,0:T(8,128)(2,1)S(1)} %all_to_all.17.parts_ref, f32[8,512,128]{2,1,0:T(8,128)S(1)} %get-tuple-element.83.kernel_ref, f32[8,128]{1,0:T(8,128)S(1)} %get-tuple-element.84.passage_ref, ...), custom_call_target="tpu_custom_call" | custom-call | tf_op jit(solution)/shard_map/pallas_call | solution.py:421
  (22 shorter events, 0.9 us)
Async XLA Ops:
  0.6 35.1 %collective-permute-start.11 = (bf16[512,4096]{1,0:T(8,128)(2,1)}, bf16[512,4096]{1,0:T(8,128)(2,1)}, u32[]{:S(2)}, u32[]{:S(2)}) collective-permute-start(bf16[512,4096]{1,0:T(8,128)(2,1)} %refs_2_), channel_id=1, source_target_pairs={{0,1},{1,0},{2,3},{3,2},{4,5},{5,4},{6,7},{7,6},{8,9},{9,8},{10,11... | collective-permute-start | bytes 12582920 | tf_op jit(solution)/shard_map/ppermute | solution.py:39
  2.1 13.6 %collective-permute-start = (bf16[32,4096]{1,0:T(8,128)(2,1)}, bf16[32,4096]{1,0:T(8,128)(2,1)S(1)}, u32[]{:S(2)}, u32[]{:S(2)}) collective-permute-start(bf16[32,4096]{1,0:T(8,128)(2,1)} %param.3), channel_id=1, source_target_pairs={{1,18},{3,16},{5,22},{7,20},{9,26},{11,24},{13,30},{15,28},{16,3},... | collective-permute-start | bytes 786440 | tf_op jit(solution)/shard_map/ppermute | solution.py:39
  6.8 9.0 %collective-permute-start.1 = (bf16[32,4096]{1,0:T(8,128)(2,1)}, bf16[32,4096]{1,0:T(8,128)(2,1)S(1)}, u32[]{:S(2)}, u32[]{:S(2)}) collective-permute-start(bf16[32,4096]{1,0:T(8,128)(2,1)} %param.3), channel_id=1, source_target_pairs={{0,12},{1,30},{2,14},{3,28},{4,0},{5,18},{6,2},{7,16},{8,4},{9,22}... | collective-permute-start | bytes 786440 | tf_op jit(solution)/shard_map/ppermute | solution.py:39
  9.3 10.9 %collective-permute-start.3 = (bf16[32,4096]{1,0:T(8,128)(2,1)}, bf16[32,4096]{1,0:T(8,128)(2,1)S(1)}, u32[]{:S(2)}, u32[]{:S(2)}) collective-permute-start(bf16[32,4096]{1,0:T(8,128)(2,1)} %param.3), channel_id=1, source_target_pairs={{0,8},{1,26},{2,10},{3,24},{4,12},{5,30},{6,14},{7,28},{8,0},{9,18... | collective-permute-start | bytes 786440 | tf_op jit(solution)/shard_map/ppermute | solution.py:39
  15.7 9.4 %collective-permute-start.4 = (bf16[32,4096]{1,0:T(8,128)(2,1)}, bf16[32,4096]{1,0:T(8,128)(2,1)S(1)}, u32[]{:S(2)}, u32[]{:S(2)}) collective-permute-start(bf16[32,4096]{1,0:T(8,128)(2,1)} %param.3), channel_id=1, source_target_pairs={{0,4},{1,22},{2,6},{3,20},{4,8},{5,26},{6,10},{7,24},{8,12},{9,30}... | collective-permute-start | bytes 786440 | tf_op jit(solution)/shard_map/ppermute | solution.py:39
  15.7 9.5 %collective-permute-start.5 = (f32[512]{0:T(512)}, f32[512]{0:T(512)S(1)}, u32[]{:S(2)}, u32[]{:S(2)}) collective-permute-start(f32[512]{0:T(512)} %param.5), channel_id=1, source_target_pairs={{0,1},{1,0},{2,3},{3,2},{4,5},{5,4},{6,7},{7,6},{8,9},{9,8},{10,11... | collective-permute-start | bytes 6152 | tf_op jit(solution)/shard_map/ppermute | solution.py:39
  15.8 12.8 %collective-permute-start.7 = (bf16[64,4096]{1,0:T(8,128)(2,1)S(1)}, bf16[64,4096]{1,0:T(8,128)(2,1)S(1)}, u32[]{:S(2)}, u32[]{:S(2)}) collective-permute-start(bf16[64,4096]{1,0:T(8,128)(2,1)S(1)} %pad_maximum_fusion.refs_4_), channel_id=1, source_target_pairs={{0,32},{1,5},{2,34},{3,7},{4,36},{5,9},{6,38},{7,11},{8,40},{9,13}... | collective-permute-start | bytes 1572872 | tf_op jit(solution)/shard_map/ppermute | solution.py:39
  25.2 8.4 %collective-permute-start.9 = (bf16[64,4096]{1,0:T(8,128)(2,1)S(1)}, bf16[64,4096]{1,0:T(8,128)(2,1)S(1)}, u32[]{:S(2)}, u32[]{:S(2)}) collective-permute-start(bf16[64,4096]{1,0:T(8,128)(2,1)S(1)} %pad_maximum_fusion.1.refs_5_), channel_id=1, source_target_pairs={{0,96},{1,13},{2,98},{3,15},{4,100},{5,1},{6,102},{7,3},{8,104},{9... | collective-permute-start | bytes 1572872 | tf_op jit(solution)/shard_map/ppermute | solution.py:39
  26.1 18.3 %collective-permute-start.2 = (bf16[64,4096]{1,0:T(8,128)(2,1)S(1)}, bf16[64,4096]{1,0:T(8,128)(2,1)S(1)}, u32[]{:S(2)}, u32[]{:S(2)}) collective-permute-start(bf16[64,4096]{1,0:T(8,128)(2,1)S(1)} %pad_maximum_fusion.refs_4_), channel_id=1, source_target_pairs={{0,96},{1,13},{2,98},{3,15},{4,100},{5,1},{6,102},{7,3},{8,104},{9... | collective-permute-start | bytes 1572872 | tf_op jit(solution)/shard_map/ppermute | solution.py:39
  26.4 18.0 %collective-permute-start.6 = (bf16[64,4096]{1,0:T(8,128)(2,1)S(1)}, bf16[64,4096]{1,0:T(8,128)(2,1)S(1)}, u32[]{:S(2)}, u32[]{:S(2)}) collective-permute-start(bf16[64,4096]{1,0:T(8,128)(2,1)S(1)} %pad_maximum_fusion.1.refs_5_), channel_id=1, source_target_pairs={{0,32},{1,5},{2,34},{3,7},{4,36},{5,9},{6,38},{7,11},{8,40},{9,13}... | collective-permute-start | bytes 1572872 | tf_op jit(solution)/shard_map/ppermute | solution.py:39
  28.6 15.8 %collective-permute-start.8 = (bf16[64,4096]{1,0:T(8,128)(2,1)S(1)}, bf16[64,4096]{1,0:T(8,128)(2,1)}, u32[]{:S(2)}, u32[]{:S(2)}) collective-permute-start(bf16[64,4096]{1,0:T(8,128)(2,1)S(1)} %collective-permute-done.7.refs_6_), channel_id=1, source_target_pairs={{0,32},{1,5},{2,34},{3,7},{4,36},{5,9},{6,38},{7,11},{8,40},{9,13}... | collective-permute-start | bytes 1572872 | tf_op jit(solution)/shard_map/ppermute | solution.py:39
  33.6 11.0 %collective-permute-start.10 = (bf16[64,4096]{1,0:T(8,128)(2,1)S(1)}, bf16[64,4096]{1,0:T(8,128)(2,1)}, u32[]{:S(2)}, u32[]{:S(2)}) collective-permute-start(bf16[64,4096]{1,0:T(8,128)(2,1)S(1)} %collective-permute-done.9.refs_7_), channel_id=1, source_target_pairs={{0,96},{1,13},{2,98},{3,15},{4,100},{5,1},{6,102},{7,3},{8,104},{9... | collective-permute-start | bytes 1572872 | tf_op jit(solution)/shard_map/ppermute | solution.py:39
  35.8 2.2 %copy-start = (bf16[512,4096]{1,0:T(8,128)(2,1)S(1)}, bf16[512,4096]{1,0:T(8,128)(2,1)}, u32[]{:S(2)}) copy-start(bf16[512,4096]{1,0:T(8,128)(2,1)} %refs_2_) | copy-start | bytes 12582916
  38.0 0.7 copy-start.1
  48.7 22.3 %collective-permute-start.14 = (bf16[512,4096]{1,0:T(8,128)(2,1)S(1)}, bf16[512,4096]{1,0:T(8,128)(2,1)S(1)}, u32[]{:S(2)}, u32[]{:S(2)}) collective-permute-start(bf16[512,4096]{1,0:T(8,128)(2,1)S(1)} %get-tuple-element.86.refs_0_), channel_id=1, source_target_pairs={{0,1},{1,0},{2,3},{3,2},{4,5},{5,4},{6,7},{7,6},{8,9},{9,8},{10,11... | collective-permute-start | bytes 12582920 | tf_op jit(solution)/shard_map/ppermute | solution.py:39
  48.8 20.3 %collective-permute-start.13 = (f32[2,512,128]{2,1,0:T(8,128)S(1)}, f32[2,512,128]{2,1,0:T(8,128)S(1)}, u32[]{:S(2)}, u32[]{:S(2)}) collective-permute-start(f32[2,512,128]{2,1,0:T(8,128)S(1)} %get-tuple-element.79), channel_id=1, source_target_pairs={{0,1},{1,0},{2,3},{3,2},{4,5},{5,4},{6,7},{7,6},{8,9},{9,8},{10,11... | collective-permute-start | bytes 1572872 | tf_op jit(solution)/shard_map/ppermute | solution.py:39
  49.3 19.8 %collective-permute-start.12 = (f32[2,512,128]{2,1,0:T(8,128)S(1)}, f32[2,512,128]{2,1,0:T(8,128)S(1)}, u32[]{:S(2)}, u32[]{:S(2)}) collective-permute-start(f32[2,512,128]{2,1,0:T(8,128)S(1)} %get-tuple-element.78), channel_id=1, source_target_pairs={{0,1},{1,0},{2,3},{3,2},{4,5},{5,4},{6,7},{7,6},{8,9},{9,8},{10,11... | collective-permute-start | bytes 1572872 | tf_op jit(solution)/shard_map/ppermute | solution.py:39
